TPU v7x, 32 devices: a whole 2x2x4 slice. The times are simulated.
32 devices in a mesh: row: 4 (over x, core), col: 8 (over z, y).
Axes of the slice: x: 2, y: 2, z: 4, core: 2. Of those that a mesh axis runs over, the one named last changes fastest.
Arguments:
- sample_heights: float32 [32, 512, 1024], P(None, 'row', 'col'), may hold values from -6 to 6
- depth: int32 [512, 1024], P('row', 'col'), may hold values from 5 to 200
- land_sea: int32 [512, 1024], P('row', 'col'), may hold values 0 or 1
- batch_order: int32 [4], replicated, may hold values from 0 to 3, each once
- obs_value: float32 [4, 2048], P(None, ('row', 'col')), may hold values from -8 to 8
- obs_error: float32 [4, 2048], P(None, ('row', 'col')), may hold values from 50 to 900
- obs_tile: int32 [4, 2048, 1], P(None, ('row', 'col')), may hold values from 0 to 7; in each aligned block of 64 rows (0 to 63, 64 to 127, ..., all dimensions but the last counted through in order) at most 16 rows name the same one
- obs_cell: int32 [4, 2048], P(None, ('row', 'col')), may hold values from 0 to 16383
- loc_level: int32 [4, 512, 8, 32], P(None, 'row', 'col'), may hold values from 1 to 8
Outputs:
- analysis: float32 [32, 512, 1024], P(None, 'row', 'col')
Inputs may be any that keep to these rules, and one draw needn't show every extreme that they name: `obs_tile`: for each batch, of the 64 observations of one owner at most 16 lie in one column tile, and in every draw some owner has exactly 16 in some tile.
All inputs are finite; a program needn't handle non-finite values. No bound on the sum of `land_sea` on one device may be relied on, other than what follows from the above.
Results may differ from a plain program's by a relative error of at most 0.0001.
Values sent between devices are 32-bit elements; how exact they have to be, the bound alone decides.
No kernel may reach another device: no remote copies, remote signals or barrier semaphores. Data moves between devices by JAX's collectives and lax.ppermute only.
A program may use at most 128 MiB of HBM per device.

v0:
```python
import functools

import jax
import jax.numpy as jnp
from jax import lax
from jax.experimental import pallas as pl
from jax.experimental.pallas import tpu as pltpu
from jax.sharding import PartitionSpec as P

BATCH_COUNT = 4
STEPS = 2
SWEEPS = 2
HALO = 8
SEG = 2 * HALO
LANES = 128
FIELDS = 4
HIGH = lax.Precision.HIGHEST
F32 = jnp.float32
BF16 = jnp.bfloat16
SMEM = pl.BlockSpec(memory_space=pltpu.SMEM)
VMEM = pl.BlockSpec(memory_space=pltpu.VMEM)
PARAMS = pltpu.CompilerParams(vmem_limit_bytes=48 * 1024 * 1024)


def iota(shape, dim):
    return lax.broadcasted_iota(jnp.int32, shape, dim)


def strides_of(n):
    out = []
    while n > 1:
        n //= 2
        out.append(n)
    return out


def offset_at(position, strides):
    out = position * 0
    for bit, stride in enumerate(strides):
        out = out + ((position >> bit) & 1) * stride
    return out


def position_of(offset, strides):
    out = offset * 0
    for bit, stride in enumerate(strides):
        out = out + ((offset // stride) & 1) * (1 << bit)
    return out


def gather_over(block, axis, beside=None):
    n = lax.axis_size(axis)
    held = block[None]
    strides = strides_of(n)
    for stride in strides:
        if stride == strides[-1] and beside is not None:
            held, beside = lax.optimization_barrier((held, beside))
        other = lax.ppermute(held, axis, [(i, i ^ stride) for i in range(n)])
        if stride != strides[-1]:
            held = jnp.concatenate([held, other], axis=0)
    return (held, other) if beside is None else ((held, other), beside)


def shift_pair(low_send, high_send, axis):
    n = lax.axis_size(axis)
    forward = [(i, i + 1) for i in range(n - 1)]
    backward = [(b, a) for a, b in forward]
    return lax.ppermute(high_send, axis, forward), lax.ppermute(low_send, axis, backward)


def nt(a, b, precision=HIGH):
    return lax.dot_general(
        a, b, (((1,), (1,)), ((), ())), precision=precision, preferred_element_type=F32
    )


def split3(x):
    hi = x.astype(BF16).astype(F32)
    rest = x - hi
    mid = rest.astype(BF16).astype(F32)
    return hi, mid, rest - mid


def prep_kernel(h_ref, coef_ref, loc_ref, obs_ref, to_right_ref, to_left_ref, record_ref):
    members, rows, lanes = h_ref.shape
    groups = members // 8
    half = groups // 2
    seg = iota((rows, lanes), 1) // SEG
    first = iota((rows, lanes), 1) % SEG < HALO
    kappa, sea = coef_ref[0], coef_ref[1]

    devices = loc_ref.shape[2]
    base = BATCH_COUNT * devices
    fields = FIELDS * BATCH_COUNT
    width = obs_ref.shape[1]
    record_ref[base:, :] = jnp.zeros((fields, lanes), F32)

    def chosen(k, values):
        order = obs_ref[fields : fields + 1, k : k + 1]
        out = values[0]
        for b in range(1, BATCH_COUNT):
            out = jnp.where(order == b, values[b], out)
        return out

    for k in range(BATCH_COUNT):
        level = chosen(k, [loc_ref[b].astype(F32) for b in range(BATCH_COUNT)])
        record_ref[k * devices : (k + 1) * devices, :] = level.T
        for f in range(FIELDS):
            row = f * BATCH_COUNT
            record_ref[base + row + k : base + row + k + 1, 0:width] = chosen(
                k, [obs_ref[row + b : row + b + 1, :] for b in range(BATCH_COUNT)]
            )

    def pack(pick):
        out = None
        for q in range(8):
            rolled = pltpu.roll(pick(q), q * SEG + HALO, axis=1)
            out = rolled if out is None else jnp.where(seg == q, rolled, out)
        return out

    def send(g, a, b):
        to_right_ref[g] = jnp.where(first, a, pltpu.roll(b, HALO, axis=1))
        to_left_ref[g] = jnp.where(first, pltpu.roll(b, lanes - HALO, axis=1), a)

    send(half, pack(lambda q: kappa), pack(lambda q: sea))
    for g in range(half):
        send(g, pack(lambda q: h_ref[8 * g + q]), pack(lambda q: h_ref[8 * (g + half) + q]))


def forecast_kernel(
    h_ref, coef_ref, left_ref, right_ref, up_ref, down_ref, out_ref,
    a_ref, b_ref, rhs_ref, sa_ref, sb_ref, srhs_ref, k_ref, sk_ref, w_ref, sw_ref, edge_ref,
):
    members, rows, lanes = h_ref.shape
    groups = members // 8
    half = groups // 2
    ext = rows + 2 * HALO
    pad = HALO
    inner = pad + HALO
    block = 16
    starts = list(range(0, ext, block))

    def fill(ref, index, upper, centre, lower):
        ref[index, pl.ds(pad, HALO), :] = upper
        ref[index, pl.ds(inner, rows), :] = centre
        ref[index, pl.ds(inner + rows, HALO), :] = lower

    for ref in (k_ref, sk_ref):
        for i in range(ref.shape[0]):
            ref[i, pl.ds(0, pad), :] = jnp.zeros((pad, lanes), F32)
            ref[i, pl.ds(pad + ext, pad), :] = jnp.zeros((pad, lanes), F32)
    for i in range(2):
        fill(k_ref, i, up_ref[members + i], coef_ref[i], down_ref[members + i])

    @pl.loop(0, members)
    def _(m):
        fill(a_ref, m, up_ref[m], h_ref[m], down_ref[m])

    def strips(start, pick, at, number):
        shape = (block, lanes)
        seg = iota(shape, 1) // SEG
        first = iota(shape, 1) % SEG < HALO

        def incoming(which, g):
            base = members + 2 + which * (half + 1) + g
            ref = (left_ref, right_ref)[which]
            parts = []
            for s in range(start, start + block, HALO):
                if s < HALO:
                    parts.append(up_ref[base])
                elif s >= rows + HALO:
                    parts.append(down_ref[base])
                else:
                    parts.append(ref[g, pl.ds(s - HALO, HALO), :])
            return jnp.concatenate(parts, axis=0)

        own = None
        for q in range(8):
            rolled = pltpu.roll(pick(q), q * SEG + HALO, axis=1)
            own = rolled if own is None else jnp.where(seg == q, rolled, own)
        source = at % half if number else half
        from_left = incoming(0, source)
        from_right = incoming(1, source)
        if at >= half if number else at:
            from_left = pltpu.roll(from_left, lanes - HALO, axis=1)
            from_right = pltpu.roll(from_right, HALO, axis=1)
        return jnp.where(first, from_left, own), jnp.where(first, own, from_right)

    for start in starts:
        rows_here = pl.ds(pad + start, block)
        for i in range(2):
            lo, hi = strips(start, lambda q: k_ref[i, rows_here, :], i, 0)
            sk_ref[2 * i, rows_here, :] = lo
            sk_ref[2 * i + 1, rows_here, :] = hi
        for g in range(groups):
            lo, hi = strips(start, lambda q: a_ref[8 * g + q, rows_here, :], g, groups)
            sa_ref[g, rows_here, :] = lo
            sa_ref[groups + g, rows_here, :] = hi

    lane = iota((block, lanes), 1)
    is_last = lane == lanes - 1
    is_first = lane == 0
    at_seven = lane % SEG == HALO - 1

    def sides(centre, edge):
        if edge is None:
            return pltpu.roll(centre, 1, axis=1), pltpu.roll(centre, lanes - 1, axis=1)
        return (
            jnp.where(is_first, edge, pltpu.roll(centre, 1, axis=1)),
            jnp.where(is_last, edge, pltpu.roll(centre, lanes - 1, axis=1)),
        )

    def edges_of(low, high):
        return jnp.where(
            at_seven, pltpu.roll(high, lanes - 1, axis=1), pltpu.roll(low, 1, axis=1)
        )

    def weights(ref, at, kap, sea, edges, start):
        here = pl.ds(pad + start, block)

        def four(src, i, edge):
            centre = src[i, here, :]
            return centre, [
                src[i, pl.ds(pad + start - 1, block), :],
                src[i, pl.ds(pad + start + 1, block), :],
                *sides(centre, edge),
            ]

        src = k_ref if edges is not None else sk_ref
        kc, kn = four(src, kap, None if edges is None else edges[0])
        sc, sn = four(src, sea, None if edges is None else edges[1])
        w = [0.5 * (kc + kn[i]) * sc * sn[i] for i in range(4)]
        wsum = w[0] + w[1] + w[2] + w[3]
        inverse = 1.0 / (1.0 + 0.5 * wsum)
        values = [1.0 - 0.5 * wsum] + [0.5 * v for v in w]
        values += [inverse] + [0.5 * v * inverse for v in w]
        for i, value in enumerate(values):
            if at is None:
                ref[i, pl.ds(start, block), :] = value
            else:
                ref[at, i, pl.ds(start, block), :] = value

    for start in starts:
        here = pl.ds(pad + start, block)
        edges = [
            pltpu.roll(
                edges_of(sk_ref[2 * i, here, :], sk_ref[2 * i + 1, here, :]), lanes - HALO, axis=1
            )
            for i in range(2)
        ]
        weights(w_ref, None, 0, 1, edges, start)
        weights(sw_ref, 0, 0, 2, None, start)
        weights(sw_ref, 1, 1, 3, None, start)

    def update(src, dst, rhs, m, start, coef, edge, explicit, store):
        centre = src[m, pl.ds(pad + start, block), :]
        upper = src[m, pl.ds(pad + start - 1, block), :]
        lower = src[m, pl.ds(pad + start + 1, block), :]
        west, east = sides(centre, edge)
        if explicit:
            c0, h0, h1, h2, h3, inverse = coef
            total = c0 * centre + (h0 * upper + h1 * lower) + (h2 * west + h3 * east)
            rhs[m, pl.ds(start, block), :] = total * inverse
        else:
            v0, v1, v2, v3 = coef
            total = rhs[m, pl.ds(start, block), :] + (v0 * upper + v1 * lower)
            total = total + (v2 * west + v3 * east)
        store(m, start, total)

    def sweep(src, dst, ssrc, sdst, explicit, last):
        chosen = range(6) if explicit else range(6, 10)

        def to(ref):
            def store(m, start, value):
                ref[m, pl.ds(pad + start, block), :] = value

            return store

        def to_out(m, start, value):
            out_ref[m, pl.ds(start - HALO, block), :] = value

        @pl.loop(0, groups)
        def _(g):
            for start in starts:
                here = pl.ds(pad + start, block)
                edge_ref[g, pl.ds(start, block), :] = edges_of(
                    ssrc[g, here, :], ssrc[groups + g, here, :]
                )
                for side in (0, 1) if not last else ():
                    coef = [sw_ref[side, i, pl.ds(start, block), :] for i in chosen]
                    update(
                        ssrc, sdst, srhs_ref, side * groups + g, start, coef, None, explicit,
                        to(sdst),
                    )

        @pl.loop(0, groups)
        def _(g):
            for start in range(HALO, HALO + rows, block) if last else starts:
                coef = [w_ref[i, pl.ds(start, block), :] for i in chosen]
                edge = edge_ref[g, pl.ds(start, block), :]
                for q in range(8):
                    rolled = pltpu.roll(edge, (lanes - HALO - SEG * q) % lanes, axis=1)
                    update(
                        src, dst, rhs_ref, 8 * g + q, start, coef, rolled, explicit,
                        to_out if last else to(dst),
                    )

    now, later = (a_ref, sa_ref), (b_ref, sb_ref)
    for step in range(STEPS):
        for stage in range(SWEEPS + 1):
            last = step == STEPS - 1 and stage == SWEEPS
            sweep(now[0], later[0], now[1], later[1], stage == 0, last)
            now, later = later, now


def extract_kernel(owner_share, me_ref, record_ref, state_ref, out_ref, meta_ref):
    members, rows, lanes = state_ref.shape
    ncol, height, _ = record_ref.shape
    fields = FIELDS * BATCH_COUNT
    base = height - fields
    capacity = lanes // ncol
    me = me_ref[1]
    stacked = jnp.concatenate([record_ref[p, base:, :] for p in range(ncol)], axis=0)
    pieces = [
        stacked[i * lanes : (i + 1) * lanes, :].T for i in range(ncol * fields // lanes)
    ]
    lane = iota((lanes, lanes), 1)
    triangle = (lane < iota((lanes, lanes), 0)).astype(BF16)
    valid = iota((lanes, lanes), 0) < owner_share
    slot = (lane % capacity).astype(F32)

    def spread(f, k):
        index = (lane // capacity) * fields + f * BATCH_COUNT + k
        out = None
        for i, piece in enumerate(pieces):
            got = jnp.take_along_axis(piece, jnp.clip(index - i * lanes, 0, lanes - 1), axis=1)
            out = got if out is None else jnp.where(index >= i * lanes, got, out)
        return out

    base = BATCH_COUNT * members
    out_ref[base + 3 * BATCH_COUNT :, :] = jnp.zeros((BATCH_COUNT, lanes), F32)
    for k in range(BATCH_COUNT):
        mine = valid & (spread(0, k) == me.astype(F32))
        rank = jnp.dot(triangle, mine.astype(BF16), preferred_element_type=F32)
        hot = mine & (rank == slot)

        def slotted(values):
            return jnp.sum(jnp.where(hot, values, 0.0), axis=0, keepdims=True)

        cell = spread(1, k).astype(jnp.int32)
        x = cell // lanes
        error = jnp.where(hot, spread(3, k), 1.0)
        for n, values in enumerate((1.0 / error, spread(2, k), (x + 1).astype(F32))):
            row = base + n * BATCH_COUNT + k
            out_ref[row : row + 1, :] = slotted(values) - (1.0 if n == 2 else 0.0)
        meta_ref[k : k + 1, :] = slotted((cell - x * lanes).astype(F32))

    level = iota((8, lanes), 0)
    place = base + 2 * BATCH_COUNT
    for k in range(BATCH_COUNT):
        xs = jnp.broadcast_to(out_ref[place + k : place + k + 1, :], (8, lanes)).astype(jnp.int32)
        ys = jnp.broadcast_to(meta_ref[k : k + 1, :], (8, lanes)).astype(jnp.int32)

        @pl.loop(0, members // 8)
        def _(g):
            totals = []
            for q in range(8):
                total = jnp.zeros((8, lanes), F32)
                for s in range(0, rows, 8):
                    block = state_ref[8 * g + q, pl.ds(s, 8), :]
                    got = jnp.take_along_axis(block, ys, axis=1)
                    total = total + jnp.where(xs == level + s, got, 0.0)
                totals.append(jnp.sum(total, axis=0, keepdims=True))
            row = pl.multiple_of(k * members + 8 * g, 8)
            out_ref[pl.ds(row, 8), :] = jnp.concatenate(totals, axis=0)


def band_sums(ncol, parts):
    lanes = LANES
    mask = (iota((ncol, lanes), 1) // (lanes // ncol) == iota((ncol, lanes), 0)).astype(F32)
    row = iota((8, lanes), 0)
    lefts, rights = [], []
    for z, w, value in parts:
        members = z.shape[0]
        mean = jnp.mean(z, axis=0, keepdims=True)
        anomaly = z - mean
        innov = value - mean
        scaled = anomaly * w

        def masked(values):
            return jnp.concatenate(
                [values[m : m + 1, :] * mask for m in range(members)], axis=0
            ).astype(BF16)

        hi, lo, _ = split3(scaled)
        hi, lo = masked(hi), masked(lo)
        lefts += [hi, lo, hi]
        right = jnp.concatenate([anomaly, jnp.where(row == 0, innov, 0.0)], axis=0)
        hi, lo, _ = split3(right)
        hi, lo = hi.astype(BF16), lo.astype(BF16)
        rights += [hi, hi, lo]
    return nt(jnp.concatenate(rights, axis=1), jnp.concatenate(lefts, axis=1), None)


def seen_rows(seen_refs, p):
    half = seen_refs[0].shape[0]
    return seen_refs[p // half].at[p % half]


def first_kernel(members, low_ref, high_ref, out_ref):
    seen = (low_ref, high_ref)
    ncol = 2 * low_ref.shape[0]
    parts = []
    for p in range(ncol):
        rows = seen_rows(seen, p)
        meta = BATCH_COUNT * members
        parts.append(
            (
                rows[0:members, :],
                rows[meta : meta + 1, :],
                rows[meta + BATCH_COUNT : meta + BATCH_COUNT + 1, :],
            )
        )
    out_ref[...] = band_sums(ncol, parts)


def bands_of(row_strides, me, low_ref, high_ref):
    half = low_ref.shape[0]
    out = []
    for r in range(2 * half):
        at = position_of(jnp.bitwise_xor(me, r), row_strides)
        out.append(
            jnp.where(at < half, low_ref[at % half], high_ref[at % half])
        )
    return out


def spread_sums(bands, spread_ref, ncol):
    height, width = bands[0].shape
    nrow = len(bands)
    members = width // ncol
    devices = nrow * ncol
    lanes = LANES
    lane = iota((height, lanes), 1)
    owner = lane % devices
    which = lane // devices
    per = max(1, lanes // devices)
    for first in range(0, members, per):
        tile, start = divmod(first * ncol, lanes)
        index = start + which * ncol + owner % ncol
        group = None
        for r in range(nrow):
            piece = bands[r][:, tile * lanes : (tile + 1) * lanes]
            got = jnp.take_along_axis(piece, index, axis=1)
            group = got if group is None else jnp.where(owner // ncol == r, got, group)
        for n in range(per):
            m = first + n
            if per > 1:
                value = jnp.take_along_axis(group, n * devices + owner, axis=1)
                hi, mid, lo = split3(value)
                value = jnp.where(which == 0, hi, jnp.where(which == 1, mid, lo))
            else:
                value = jnp.concatenate(split3(group), axis=1)
            spread_ref[pl.ds(m * height, height), :] = value.astype(BF16)


def copies_of(levels):
    devices = levels.shape[0]
    copies = max(3, LANES // devices)
    scaled = (levels * 0.125).astype(BF16)
    return jnp.concatenate([scaled] * 3 + [jnp.zeros_like(scaled)] * (copies - 3), axis=0)


def solve_sums(bands, ncol):
    height, width = bands[0].shape
    members = width // ncol
    lanes = LANES
    total = bands[0]
    for band in bands[1:]:
        total = total + band
    pick = (iota((width, lanes), 0) // ncol == iota((width, lanes), 1)).astype(BF16)
    a = sum(
        jnp.dot(part.astype(BF16), pick, preferred_element_type=F32)
        for part in reversed(split3(total))
    )
    row = iota((height, lanes), 0)
    lane = iota((height, lanes), 1)
    a = a + jnp.where((row == lane) & (row < members), members - 1.0, 0.0)
    lane1 = iota((1, lanes), 1)
    block = 8
    for start in range(0, members, block):
        columns = [
            jnp.broadcast_to(a[:, k : k + 1], (height, lanes))
            for k in range(start, start + block)
        ]
        for s in range(block):
            k, column = start + s, columns[s]
            inverse = 1.0 / column[k : k + 1, :]
            scaled = jnp.where(lane1 == k, inverse, a[k : k + 1, :] * inverse)
            a = jnp.where(row == k, scaled, jnp.where(lane == k, 0.0, a) - column * scaled)
            for t in range(s + 1, block):
                part = columns[t][k : k + 1, :] * inverse
                columns[t] = jnp.where(row == k, part, columns[t] - column * part)
    gain = a[members : members + 1, :] * (1.0 / (members - 1))
    out = jnp.where(lane1 < members, -0.5 * a[0:members, :] + gain, 0.0)
    return jnp.where(lane1 == members, 1.0 / (members - 1), out)


def apply_sums(spread, levels, z, height):
    at = jnp.dot(spread, levels, preferred_element_type=F32)
    total = None
    for m in range(z.shape[0]):
        term = at[m * height : (m + 1) * height, :] * z[m : m + 1, :]
        total = term if total is None else total + term
    return total


def levels_at(rows, batch, devices, place):
    lanes = LANES
    hot = (iota((lanes, lanes), 0) == place.astype(jnp.int32)).astype(BF16)
    table = rows[batch * devices : (batch + 1) * devices, :].astype(BF16)
    return jnp.dot(table, hot, preferred_element_type=F32)


def moved(strides, me, record_ref, seen, spread, solved, batch, target, devices, read):
    ncol = 2 * seen[0].shape[0]
    members = solved.shape[0]
    height = members + 8
    place = BATCH_COUNT * members + 2 * BATCH_COUNT + target
    out = []
    for p in range(0, ncol, 2):
        pair = (p, p + 1)
        levels = []
        for i in pair:
            offset = sum(((i >> bit) & 1) * stride for bit, stride in enumerate(strides))
            levels.append(
                copies_of(
                    levels_at(
                        record_ref.at[jnp.bitwise_xor(me, offset)], batch, devices,
                        seen_rows(seen, i)[place : place + 1, :],
                    )
                )
            )
        z = jnp.concatenate([read(i) for i in pair], axis=1)
        sums = apply_sums(spread, jnp.concatenate(levels, axis=1), z, height)
        z = z + jnp.dot(
            solved[:, 0:height], sums, precision=HIGH, preferred_element_type=F32
        )
        out += [z[:, 0:LANES], z[:, LANES:]]
    return out


def reader(seen, z_ref, members, target):
    if z_ref is not None:
        return lambda i: z_ref[i]
    return lambda i: seen_rows(seen, i)[target * members : (target + 1) * members, :]


def next_kernel(strides, row_strides, batch, *refs):
    me_ref, lows_ref, highs_ref, record_ref = refs[:4]
    seen = refs[4:6]
    z_ref = refs[6] if batch else None
    out_ref, spread_ref, solved_ref = refs[-3:]
    ncol = 2 * seen[0].shape[0]
    members = solved_ref.shape[0]
    devices = 2 * ncol * lows_ref.shape[0]
    bands = bands_of(row_strides, me_ref[0], lows_ref, highs_ref)
    spread_sums(bands, spread_ref, ncol)
    solved = solve_sums(bands, ncol)
    solved_ref[...] = solved
    target = batch + 1
    zs = moved(
        strides, me_ref[1], record_ref, seen, spread_ref[...], solved, batch, target, devices,
        reader(seen, z_ref, members, target),
    )
    parts = []
    meta = BATCH_COUNT * members + target
    for p in range(ncol):
        rows = seen_rows(seen, p)
        parts.append(
            (
                zs[p],
                rows[meta : meta + 1, :],
                rows[meta + BATCH_COUNT : meta + BATCH_COUNT + 1, :],
            )
        )
    out_ref[...] = band_sums(ncol, parts)


def moved_kernel(strides, batches, target, *refs):
    me_ref, record_ref = refs[:2]
    seen = refs[2:4]
    given = refs[4 : 4 + 2 * len(batches)]
    z_ref = refs[4 + 2 * len(batches)] if len(refs) == 6 + 2 * len(batches) else None
    out_ref = refs[-1]
    members = given[1].shape[0]
    devices = (record_ref.shape[1] - FIELDS * BATCH_COUNT) // BATCH_COUNT
    read = reader(seen, z_ref, members, target)
    for n, batch in enumerate(batches):
        zs = moved(
            strides, me_ref[1], record_ref, seen, given[2 * n][...], given[2 * n + 1][...],
            batch, target, devices, read,
        )
        read = zs.__getitem__
    for p, z in enumerate(zs):
        out_ref[p] = z


def compose(spread, solved, levels, batch, trans_ref, dst_ref, height):
    members = solved.shape[0]
    at = jnp.dot(spread, levels, preferred_element_type=F32)
    lanes = LANES
    gain = solved[:, 0:height]
    for j in range(0, members, 2):
        sums = []
        for i in (j, j + 1):
            if batch == 0:
                sums.append(at[i * height : (i + 1) * height, :])
            else:
                total = None
                for m in range(members):
                    term = at[m * height : (m + 1) * height, :] * trans_ref[i, m : m + 1, :]
                    total = term if total is None else total + term
                sums.append(total)
        change = jnp.dot(
            gain, jnp.concatenate(sums, axis=1), precision=HIGH, preferred_element_type=F32
        )
        for n, i in enumerate((j, j + 1)):
            part = change[:, n * lanes : (n + 1) * lanes]
            if batch == 0:
                dst_ref[i] = part + (iota((members, lanes), 0) == i).astype(F32)
            else:
                dst_ref[i] = part + trans_ref[i]


def compose_kernel(batches, me_ref, record_ref, *refs):
    given = refs[: 2 * len(batches)]
    trans_ref = refs[2 * len(batches)] if batches[0] else None
    out_ref = refs[-1]
    members = given[1].shape[0]
    devices = (record_ref.shape[1] - FIELDS * BATCH_COUNT) // BATCH_COUNT
    for n, batch in enumerate(batches):
        levels = copies_of(record_ref[me_ref[1], batch * devices : (batch + 1) * devices, :])
        source = trans_ref if n == 0 else out_ref
        compose(
            given[2 * n][...], given[2 * n + 1][...], levels, batch, source, out_ref, members + 8
        )


def final_kernel(
    row_strides, me_ref, lows_ref, highs_ref, record_ref, trans_ref, state_ref, out_ref,
    spread_ref, whole_ref, turned_ref,
):
    members, rows, lanes = state_ref.shape
    height, width = lows_ref.shape[1:]
    ncol = width // members
    devices = 2 * lows_ref.shape[0] * ncol
    batch = BATCH_COUNT - 1
    bands = bands_of(row_strides, me_ref[0], lows_ref, highs_ref)
    spread_sums(bands, spread_ref, ncol)
    solved = solve_sums(bands, ncol)
    levels = copies_of(record_ref[me_ref[1], batch * devices : (batch + 1) * devices, :])
    compose(spread_ref[...], solved, levels, batch, trans_ref, whole_ref, height)
    for i in range(members):
        hi, lo, _ = split3(whole_ref[:, i, :])
        turned_ref[:, i, :] = jnp.concatenate([hi, hi, lo, jnp.zeros_like(hi)], axis=0).T

    @pl.loop(0, rows // 8)
    def _(b):
        start = pl.multiple_of(b * 8, 8)
        turned = jnp.swapaxes(state_ref[:, pl.ds(start, 8), :], 0, 1)
        done = []
        for i in range(8):
            hi, lo, _ = split3(turned[i])
            right = jnp.concatenate([hi, lo, hi, jnp.zeros_like(hi)], axis=0).astype(BF16)
            done.append(
                jnp.dot(
                    turned_ref[start + i].astype(BF16), right, preferred_element_type=F32
                )
            )
        out_ref[:, pl.ds(start, 8), :] = jnp.swapaxes(jnp.stack(done), 0, 1)


def call(kernel, out_shape, in_specs, scratch=(), flops=10**6):
    return pl.pallas_call(
        kernel,
        out_shape=out_shape,
        in_specs=in_specs,
        out_specs=jax.tree.map(lambda _: VMEM, out_shape),
        scratch_shapes=list(scratch),
        compiler_params=PARAMS,
    )


def body(
    sample_heights, depth, land_sea, batch_order, obs_value, obs_error, obs_tile, obs_cell, loc_level
):
    members, rows, cols = sample_heights.shape
    ncol = lax.axis_size("col")
    nrow = lax.axis_size("row")
    devices = nrow * ncol
    strides, row_strides = strides_of(ncol), strides_of(nrow)
    groups = members // 8
    half = groups // 2
    height = members + 8
    me = jnp.stack([lax.axis_index("row"), lax.axis_index("col")]).astype(jnp.int32)

    def out(*shape, dtype=F32):
        return jax.ShapeDtypeStruct(shape, dtype)

    record_rows = BATCH_COUNT * devices + FIELDS * BATCH_COUNT
    sea = land_sea.astype(F32)
    coef = jnp.stack([0.01 * depth.astype(F32) * sea, sea])
    share = obs_cell.shape[1]
    order = jnp.pad(batch_order.astype(F32)[None], ((0, 7), (0, share - BATCH_COUNT)))
    observed = jnp.concatenate(
        [obs_tile[:, :, 0].astype(F32), obs_cell.astype(F32), obs_value, obs_error, order]
    )
    to_right, to_left, record = call(
        prep_kernel,
        (out(half + 1, rows, cols), out(half + 1, rows, cols), out(record_rows, cols)),
        [VMEM] * 4,
    )(sample_heights, coef, loc_level[:, :, 0, :], observed)
    left, right = shift_pair(to_left, to_right, "col")

    def slab(start):
        cut = lambda a: lax.slice_in_dim(a, start, start + HALO, axis=1)
        return jnp.concatenate([cut(a) for a in (sample_heights, coef, left, right)], axis=0)

    up, down = shift_pair(slab(0), slab(rows - HALO), "row")
    records = lax.all_to_all(
        jnp.broadcast_to(record, (ncol, *record.shape)), "col", split_axis=0, concat_axis=0, tiled=True
    )

    ext = rows + 2 * HALO
    tall = ext + 2 * HALO
    state = call(
        forecast_kernel,
        out(members, rows, cols),
        [VMEM] * 6,
        [
            pltpu.VMEM((members, tall, cols), F32),
            pltpu.VMEM((members, tall, cols), F32),
            pltpu.VMEM((members, ext, cols), F32),
            pltpu.VMEM((2 * groups, tall, cols), F32),
            pltpu.VMEM((2 * groups, tall, cols), F32),
            pltpu.VMEM((2 * groups, ext, cols), F32),
            pltpu.VMEM((2, tall, cols), F32),
            pltpu.VMEM((4, tall, cols), F32),
            pltpu.VMEM((10, ext, cols), F32),
            pltpu.VMEM((2, 10, ext, cols), F32),
            pltpu.VMEM((groups, ext, cols), F32),
        ],
    )(sample_heights, coef, left, right, up, down)

    mine = call(
        functools.partial(extract_kernel, obs_cell.shape[1]),
        out(BATCH_COUNT * members + FIELDS * BATCH_COUNT, cols),
        [SMEM, VMEM, VMEM],
        [pltpu.VMEM((8, cols), F32)],
    )(me, records, state)
    seen = gather_over(mine, "col")

    sums = call(
        functools.partial(first_kernel, members), out(height, members * ncol), [VMEM] * 2
    )(*seen)
    wide = max(LANES, 3 * devices)

    def compose_of(batches, given, trans):
        args = (me, records, *given) + (() if trans is None else (trans,))
        return call(
            functools.partial(compose_kernel, batches),
            out(members, members, cols),
            [SMEM] + [VMEM] * (len(args) - 1),
        )(*args)

    def moved_of(batches, target, given, z):
        args = (me, records, *seen, *given) + (() if z is None else (z,))
        return call(
            functools.partial(moved_kernel, strides, batches, target),
            out(ncol, members, cols),
            [SMEM] + [VMEM] * (len(args) - 1),
        )(*args)

    def next_of(batch, every, z):
        args = (me, *every, records, *seen) + (() if z is None else (z,))
        got = call(
            functools.partial(next_kernel, strides, row_strides, batch),
            (
                out(height, members * ncol),
                out(members * height, wide, dtype=BF16),
                out(members, LANES),
            ),
            [SMEM] + [VMEM] * (len(args) - 1),
        )(*args)
        return got[0], got[1:]

    def exchange(sums, beside):
        return gather_over(sums, "row", beside)

    every, _ = exchange(sums, ())
    sums, first = next_of(0, every, None)
    every, (z2, trans) = exchange(
        sums, (moved_of((0,), 2, first, None), compose_of((0,), first, None))
    )
    sums, second = next_of(1, every, z2)
    every, (z3,) = exchange(sums, (moved_of((0, 1), 3, first + second, None),))
    sums, third = next_of(2, every, z3)
    every, (trans,) = exchange(sums, (compose_of((1, 2), second + third, trans),))
    return call(
        functools.partial(final_kernel, row_strides),
        out(members, rows, cols),
        [SMEM] + [VMEM] * 5,
        [
            pltpu.VMEM((members * height, wide), BF16),
            pltpu.VMEM((members, members, cols), F32),
            pltpu.VMEM((rows, members, cols), F32),
        ],
    )(me, *every, records, trans, state)


def solution(mesh):
    return jax.shard_map(
        body,
        mesh=mesh,
        in_specs=(
            P(None, "row", "col"),
            P("row", "col"),
            P("row", "col"),
            P(),
            P(None, ("row", "col")),
            P(None, ("row", "col")),
            P(None, ("row", "col"), None),
            P(None, ("row", "col")),
            P(None, "row", "col", None),
        ),
        out_specs=P(None, "row", "col"),
        check_vma=False,
    )
```

profile of v0, /device:TPU:0, one launch (start us, length us, event | category | flops | bytes accessed | tf_op | source)
XLA Modules:
  0.0 129.0 jit_solution(6083638600049577879)
XLA Ops:
  5.5 1.6 %copy-done = f32[32,128,128]{2,1,0:T(8,128)S(1)} copy-done((f32[32,128,128]{2,1,0:T(8,128)S(1)}, f32[32,128,128]{2,1,0:T(8,128)}, u32[]{:S(2)}) %copy-start) | copy-done | bytes 2097176
  8.5 4.9 %collective-permute-start = (f32[3,128,128]{2,1,0:T(8,128)S(1)}, f32[3,128,128]{2,1,0:T(8,128)S(1)}, u32[]{:S(2)}, u32[]{:S(2)}) collective-permute-start(f32[3,128,128]{2,1,0:T(8,128)S(1)} %get-tuple-element.25), channel_id=1, source_target_pairs={{0,1},{1,2},{2,3},{3,4},{4,5},{5,6},{6,7},{8,9},{9,10},{10,11},{11... | collective-permute-start | bytes 589832 | tf_op jit(solution)/shard_map/ppermute | solution.py:68
  15.5 7.0 %all-to-all-start = ((f32[8,144,128]{2,1,0:T(8,128)}), f32[8,144,128]{2,1,0:T(8,128)S(1)}, u32[]{:S(2)}, u32[]{:S(2)}) async-start(f32[8,144,128]{2,1,0:T(8,128)} %broadcast_in_dim.22), calls=%async_computation | async-start | bytes 1179648 | tf_op jit(solution)/shard_map/all_to_all | solution.py:731
  26.2 3.6 %collective-permute-done.3.down_ref = f32[40,8,128]{2,1,0:T(8,128)S(1)} collective-permute-done((f32[40,8,128]{2,1,0:T(8,128)S(1)}, f32[40,8,128]{2,1,0:T(8,128)S(1)}, u32[]{:S(2)}, u32[]{:S(2)}) %collective-permute-start.3) | collective-permute-done | bytes 163872 | tf_op jit(solution)/shard_map/ppermute | solution.py:68
  29.9 1.6 %copy-done.1 = f32[32,128,128]{2,1,0:T(8,128)S(1)} copy-done((f32[32,128,128]{2,1,0:T(8,128)S(1)}, f32[32,128,128]{2,1,0:T(8,128)}, u32[]{:S(2)}) %copy-start.1) | copy-done | bytes 2097176
  31.5 19.3 %shard_map.92.state_ref = f32[32,128,128]{2,1,0:T(8,128)S(1)} custom-call(f32[32,128,128]{2,1,0:T(8,128)S(1)} %copy-done.1, f32[2,128,128]{2,1,0:T(8,128)S(1)} %pad_maximum_fusion.1.coef_ref, f32[3,128,128]{2,1,0:T(8,128)S(1)} %collective-permute-done.left_ref, f32[3,128,128]{2,1,0:T(8,128)S(1)} %collective-permute-done.1.right_ref, ...), custom_call_target="tpu_custom_call" | custom-call | tf_op jit(solution)/shard_map/pallas_call | solution.py:737
  50.8 4.6 %shard_map.93 = f32[144,128]{1,0:T(8,128)S(1)} custom-call(s32[2]{0:T(128)S(1)} %pad_add_fusion.me_ref.refs_0_, f32[8,144,128]{2,1,0:T(8,128)S(1)} %all-to-all-done.record_ref.refs_3_.refs_1_, f32[32,128,128]{2,1,0:T(8,128)S(1)} %shard_map.92.state_ref), custom_call_target="tpu_custom_call" | custom-call | tf_op jit(solution)/shard_map/pallas_call | solution.py:756
  55.4 3.0 %collective-permute-start.4 = (f32[1,144,128]{2,1,0:T(8,128)S(1)}, f32[1,144,128]{2,1,0:T(8,128)S(1)}, u32[]{:S(2)}, u32[]{:S(2)}) collective-permute-start(f32[1,144,128]{2,1,0:T(8,128)S(1)} %bitcast.18), channel_id=1, source_target_pairs={{0,4},{1,5},{2,6},{3,7},{4,0},{5,1},{6,2},{7,3},{8,12},{9,13},{10,... | collective-permute-start | bytes 221192 | tf_op jit(solution)/shard_map/ppermute | solution.py:58
  58.4 2.3 %collective-permute-done.4 = f32[1,144,128]{2,1,0:T(8,128)S(1)} collective-permute-done((f32[1,144,128]{2,1,0:T(8,128)S(1)}, f32[1,144,128]{2,1,0:T(8,128)S(1)}, u32[]{:S(2)}, u32[]{:S(2)}) %collective-permute-start.4) | collective-permute-done | bytes 73760 | tf_op jit(solution)/shard_map/ppermute | solution.py:58
  60.8 2.1 %collective-permute-start.5 = (f32[2,144,128]{2,1,0:T(8,128)S(1)}, f32[2,144,128]{2,1,0:T(8,128)S(1)}, u32[]{:S(2)}, u32[]{:S(2)}) collective-permute-start(f32[2,144,128]{2,1,0:T(8,128)S(1)} %pad_maximum_fusion.4), channel_id=1, source_target_pairs={{0,2},{1,3},{2,0},{3,1},{4,6},{5,7},{6,4},{7,5},{8,10},{9,11},{10,... | collective-permute-start | bytes 442376 | tf_op jit(solution)/shard_map/ppermute | solution.py:58
  62.9 3.1 %collective-permute-done.5 = f32[2,144,128]{2,1,0:T(8,128)S(1)} collective-permute-done((f32[2,144,128]{2,1,0:T(8,128)S(1)}, f32[2,144,128]{2,1,0:T(8,128)S(1)}, u32[]{:S(2)}, u32[]{:S(2)}) %collective-permute-start.5) | collective-permute-done | bytes 147488 | tf_op jit(solution)/shard_map/ppermute | solution.py:58
  66.0 2.1 %collective-permute-start.6 = (f32[4,144,128]{2,1,0:T(8,128)S(1)}, f32[4,144,128]{2,1,0:T(8,128)S(1)}, u32[]{:S(2)}, u32[]{:S(2)}) collective-permute-start(f32[4,144,128]{2,1,0:T(8,128)S(1)} %pad_maximum_fusion.low_ref.refs_4_.refs_2_), channel_id=1, source_target_pairs={{0,1},{1,0},{2,3},{3,2},{4,5},{5,4},{6,7},{7,6},{8,9},{9,8},{10,11... | collective-permute-start | bytes 884744 | tf_op jit(solution)/shard_map/ppermute | solution.py:58
  68.1 6.9 %collective-permute-done.6.high_ref.refs_5_.refs_3_ = f32[4,144,128]{2,1,0:T(8,128)S(1)} collective-permute-done((f32[4,144,128]{2,1,0:T(8,128)S(1)}, f32[4,144,128]{2,1,0:T(8,128)S(1)}, u32[]{:S(2)}, u32[]{:S(2)}) %collective-permute-start.6) | collective-permute-done | bytes 294944 | tf_op jit(solution)/shard_map/ppermute | solution.py:58
  75.6 1.8 %collective-permute-start.7 = (f32[1,40,256]{2,1,0:T(8,128)S(1)}, f32[1,40,256]{2,1,0:T(8,128)S(1)}, u32[]{:S(2)}, u32[]{:S(2)}) collective-permute-start(f32[1,40,256]{2,1,0:T(8,128)S(1)} %bitcast.21), channel_id=1, source_target_pairs={{0,16},{8,24},{16,0},{24,8},{1,17},{9,25},{17,1},{25,9},{2,18},{10... | collective-permute-start | bytes 122888 | tf_op jit(solution)/shard_map/ppermute | solution.py:58
  77.3 2.6 %collective-permute-done.7 = f32[1,40,256]{2,1,0:T(8,128)S(1)} collective-permute-done((f32[1,40,256]{2,1,0:T(8,128)S(1)}, f32[1,40,256]{2,1,0:T(8,128)S(1)}, u32[]{:S(2)}, u32[]{:S(2)}) %collective-permute-start.7) | collective-permute-done | bytes 40992 | tf_op jit(solution)/shard_map/ppermute | solution.py:58
  81.2 4.5 %shard_map.95 = (f32[40,256]{1,0:T(8,128)S(1)}, bf16[1280,128]{1,0:T(8,128)(2,1)S(1)}, f32[32,128]{1,0:T(8,128)S(1)}) custom-call(s32[2]{0:T(128)S(1)} %pad_add_fusion.me_ref.refs_0_, f32[2,40,256]{2,1,0:T(8,128)S(1)} %pad_maximum_fusion.5.refs_1_, f32[2,40,256]{2,1,0:T(8,128)S(1)} %collective-permute-done.8.refs_2_, ...), custom_call_target="tpu_custom_call" | custom-call | tf_op jit(solution)/shard_map/pallas_call | solution.py:787
  85.7 1.4 %collective-permute-start.9 = (f32[1,40,256]{2,1,0:T(8,128)S(1)}, f32[1,40,256]{2,1,0:T(8,128)S(1)}, u32[]{:S(2)}, u32[]{:S(2)}) collective-permute-start(f32[1,40,256]{2,1,0:T(8,128)S(1)} %bitcast.27), channel_id=1, source_target_pairs={{0,16},{8,24},{16,0},{24,8},{1,17},{9,25},{17,1},{25,9},{2,18},{10... | collective-permute-start | bytes 122888 | tf_op jit(solution)/shard_map/ppermute | solution.py:58
  87.2 3.3 %shard_map.96.refs_6_ = f32[8,32,128]{2,1,0:T(8,128)S(1)} custom-call(s32[2]{0:T(128)S(1)} %pad_add_fusion.me_ref.refs_0_, f32[8,144,128]{2,1,0:T(8,128)S(1)} %all-to-all-done.record_ref.refs_3_.refs_1_, f32[4,144,128]{2,1,0:T(8,128)S(1)} %pad_maximum_fusion.low_ref.refs_4_.refs_2_, f32[4,144,128]{2,1,0:T(8,128)S(1)} %collective-permute-done.6.high_ref.refs_5_.refs_3_, ...), custom_call_target="tpu_custom_call" | custom-call | tf_op jit(solution)/shard_map/pallas_call | solution.py:779
  93.2 4.5 %shard_map.98 = (f32[40,256]{1,0:T(8,128)S(1)}, bf16[1280,128]{1,0:T(8,128)(2,1)S(1)}, f32[32,128]{1,0:T(8,128)S(1)}) custom-call(s32[2]{0:T(128)S(1)} %pad_add_fusion.me_ref.refs_0_, f32[2,40,256]{2,1,0:T(8,128)S(1)} %pad_maximum_fusion.6.refs_1_, f32[2,40,256]{2,1,0:T(8,128)S(1)} %collective-permute-done.10.refs_2_, ...), custom_call_target="tpu_custom_call" | custom-call | tf_op jit(solution)/shard_map/pallas_call | solution.py:787
  98.3 6.2 %shard_map.99.refs_6_ = f32[8,32,128]{2,1,0:T(8,128)S(1)} custom-call(s32[2]{0:T(128)S(1)} %pad_add_fusion.me_ref.refs_0_, f32[8,144,128]{2,1,0:T(8,128)S(1)} %all-to-all-done.record_ref.refs_3_.refs_1_, f32[4,144,128]{2,1,0:T(8,128)S(1)} %pad_maximum_fusion.low_ref.refs_4_.refs_2_, f32[4,144,128]{2,1,0:T(8,128)S(1)} %collective-permute-done.6.high_ref.refs_5_.refs_3_, ...), custom_call_target="tpu_custom_call" | custom-call | tf_op jit(solution)/shard_map/pallas_call | solution.py:779
  105.9 4.5 %shard_map.100 = (f32[40,256]{1,0:T(8,128)S(1)}, bf16[1280,128]{1,0:T(8,128)(2,1)S(1)}, f32[32,128]{1,0:T(8,128)S(1)}) custom-call(s32[2]{0:T(128)S(1)} %pad_add_fusion.me_ref.refs_0_, f32[2,40,256]{2,1,0:T(8,128)S(1)} %pad_maximum_fusion.7.refs_1_, f32[2,40,256]{2,1,0:T(8,128)S(1)} %collective-permute-done.12.refs_2_, ...), custom_call_target="tpu_custom_call" | custom-call | tf_op jit(solution)/shard_map/pallas_call | solution.py:787
  110.4 1.4 %collective-permute-start.13 = (f32[1,40,256]{2,1,0:T(8,128)S(1)}, f32[1,40,256]{2,1,0:T(8,128)S(1)}, u32[]{:S(2)}, u32[]{:S(2)}) collective-permute-start(f32[1,40,256]{2,1,0:T(8,128)S(1)} %bitcast.23), channel_id=1, source_target_pairs={{0,16},{8,24},{16,0},{24,8},{1,17},{9,25},{17,1},{25,9},{2,18},{10... | collective-permute-start | bytes 122888 | tf_op jit(solution)/shard_map/ppermute | solution.py:58
  111.9 4.9 %shard_map.101.trans_ref = f32[32,32,128]{2,1,0:T(8,128)S(1)} custom-call(s32[2]{0:T(128)S(1)} %pad_add_fusion.me_ref.refs_0_, f32[8,144,128]{2,1,0:T(8,128)S(1)} %all-to-all-done.record_ref.refs_3_.refs_1_, bf16[1280,128]{1,0:T(8,128)(2,1)S(1)} %get-tuple-element.33.refs_6_.refs_0_, f32[32,128]{1,0:T(8,128)S(1)} %get-tuple-element.34.refs_7_.refs_1_, ...), custom_call_target="tpu_custom_call" | custom-call | tf_op jit(solution)/shard_map/pallas_call | solution.py:771
  118.1 10.9 %shard_map.102 = f32[32,128,128]{2,1,0:T(8,128)} custom-call(s32[2]{0:T(128)S(1)} %pad_add_fusion.me_ref.refs_0_, f32[2,40,256]{2,1,0:T(8,128)S(1)} %pad_maximum_fusion.8.lows_ref, f32[2,40,256]{2,1,0:T(8,128)S(1)} %collective-permute-done.14.highs_ref, f32[8,144,128]{2,1,0:T(8,128)S(1)} %all-to-all-done.record_ref.refs_3_.refs_1_, ...), custom_call_target="tpu_custom_call" | custom-call | tf_op jit(solution)/shard_map/pallas_call | solution.py:810
  (47 shorter events, 20.6 us)
Async XLA Ops:
  5.5 1.6 %copy-start = (f32[32,128,128]{2,1,0:T(8,128)S(1)}, f32[32,128,128]{2,1,0:T(8,128)}, u32[]{:S(2)}) copy-start(f32[32,128,128]{2,1,0:T(8,128)} %h_ref.3) | copy-start | bytes 6291460
  8.5 15.0 %collective-permute-start = (f32[3,128,128]{2,1,0:T(8,128)S(1)}, f32[3,128,128]{2,1,0:T(8,128)S(1)}, u32[]{:S(2)}, u32[]{:S(2)}) collective-permute-start(f32[3,128,128]{2,1,0:T(8,128)S(1)} %get-tuple-element.25), channel_id=1, source_target_pairs={{0,1},{1,2},{2,3},{3,4},{4,5},{5,6},{6,7},{8,9},{9,10},{10,11},{11... | collective-permute-start | bytes 589832 | tf_op jit(solution)/shard_map/ppermute | solution.py:68
  13.4 10.1 %collective-permute-start.1 = (f32[3,128,128]{2,1,0:T(8,128)S(1)}, f32[3,128,128]{2,1,0:T(8,128)S(1)}, u32[]{:S(2)}, u32[]{:S(2)}) collective-permute-start(f32[3,128,128]{2,1,0:T(8,128)S(1)} %get-tuple-element.26), channel_id=1, source_target_pairs={{1,0},{2,1},{3,2},{4,3},{5,4},{6,5},{7,6},{9,8},{10,9},{11,10},{12... | collective-permute-start | bytes 589832 | tf_op jit(solution)/shard_map/ppermute | solution.py:68
  15.5 35.3 %all-to-all-start = ((f32[8,144,128]{2,1,0:T(8,128)}), f32[8,144,128]{2,1,0:T(8,128)S(1)}, u32[]{:S(2)}, u32[]{:S(2)}) async-start(f32[8,144,128]{2,1,0:T(8,128)} %broadcast_in_dim.22), calls=%async_computation | async-start | bytes 1179648 | tf_op jit(solution)/shard_map/all_to_all | solution.py:731
  23.5 2.7 %collective-permute-start.2 = (f32[40,8,128]{2,1,0:T(8,128)S(1)}, f32[40,8,128]{2,1,0:T(8,128)S(1)}, u32[]{:S(2)}, u32[]{:S(2)}) collective-permute-start(f32[40,8,128]{2,1,0:T(8,128)S(1)} %pad_maximum_fusion.2), channel_id=1, source_target_pairs={{0,8},{8,16},{16,24},{1,9},{9,17},{17,25},{2,10},{10,18},{18,26},{... | collective-permute-start | bytes 491528 | tf_op jit(solution)/shard_map/ppermute | solution.py:68
  24.9 5.0 %collective-permute-start.3 = (f32[40,8,128]{2,1,0:T(8,128)S(1)}, f32[40,8,128]{2,1,0:T(8,128)S(1)}, u32[]{:S(2)}, u32[]{:S(2)}) collective-permute-start(f32[40,8,128]{2,1,0:T(8,128)S(1)} %pad_maximum_fusion.3), channel_id=1, source_target_pairs={{8,0},{16,8},{24,16},{9,1},{17,9},{25,17},{10,2},{18,10},{26,18},{... | collective-permute-start | bytes 491528 | tf_op jit(solution)/shard_map/ppermute | solution.py:68
  29.9 1.6 %copy-start.1 = (f32[32,128,128]{2,1,0:T(8,128)S(1)}, f32[32,128,128]{2,1,0:T(8,128)}, u32[]{:S(2)}) copy-start(f32[32,128,128]{2,1,0:T(8,128)} %h_ref.3) | copy-start | bytes 6291460
  55.4 5.3 %collective-permute-start.4 = (f32[1,144,128]{2,1,0:T(8,128)S(1)}, f32[1,144,128]{2,1,0:T(8,128)S(1)}, u32[]{:S(2)}, u32[]{:S(2)}) collective-permute-start(f32[1,144,128]{2,1,0:T(8,128)S(1)} %bitcast.18), channel_id=1, source_target_pairs={{0,4},{1,5},{2,6},{3,7},{4,0},{5,1},{6,2},{7,3},{8,12},{9,13},{10,... | collective-permute-start | bytes 221192 | tf_op jit(solution)/shard_map/ppermute | solution.py:58
  60.8 5.2 %collective-permute-start.5 = (f32[2,144,128]{2,1,0:T(8,128)S(1)}, f32[2,144,128]{2,1,0:T(8,128)S(1)}, u32[]{:S(2)}, u32[]{:S(2)}) collective-permute-start(f32[2,144,128]{2,1,0:T(8,128)S(1)} %pad_maximum_fusion.4), channel_id=1, source_target_pairs={{0,2},{1,3},{2,0},{3,1},{4,6},{5,7},{6,4},{7,5},{8,10},{9,11},{10,... | collective-permute-start | bytes 442376 | tf_op jit(solution)/shard_map/ppermute | solution.py:58
  66.0 8.9 %collective-permute-start.6 = (f32[4,144,128]{2,1,0:T(8,128)S(1)}, f32[4,144,128]{2,1,0:T(8,128)S(1)}, u32[]{:S(2)}, u32[]{:S(2)}) collective-permute-start(f32[4,144,128]{2,1,0:T(8,128)S(1)} %pad_maximum_fusion.low_ref.refs_4_.refs_2_), channel_id=1, source_target_pairs={{0,1},{1,0},{2,3},{3,2},{4,5},{5,4},{6,7},{7,6},{8,9},{9,8},{10,11... | collective-permute-start | bytes 884744 | tf_op jit(solution)/shard_map/ppermute | solution.py:58
  75.6 4.4 %collective-permute-start.7 = (f32[1,40,256]{2,1,0:T(8,128)S(1)}, f32[1,40,256]{2,1,0:T(8,128)S(1)}, u32[]{:S(2)}, u32[]{:S(2)}) collective-permute-start(f32[1,40,256]{2,1,0:T(8,128)S(1)} %bitcast.21), channel_id=1, source_target_pairs={{0,16},{8,24},{16,0},{24,8},{1,17},{9,25},{17,1},{25,9},{2,18},{10... | collective-permute-start | bytes 122888 | tf_op jit(solution)/shard_map/ppermute | solution.py:58
  79.9 1.3 collective-permute-start.8
  85.7 6.1 %collective-permute-start.9 = (f32[1,40,256]{2,1,0:T(8,128)S(1)}, f32[1,40,256]{2,1,0:T(8,128)S(1)}, u32[]{:S(2)}, u32[]{:S(2)}) collective-permute-start(f32[1,40,256]{2,1,0:T(8,128)S(1)} %bitcast.27), channel_id=1, source_target_pairs={{0,16},{8,24},{16,0},{24,8},{1,17},{9,25},{17,1},{25,9},{2,18},{10... | collective-permute-start | bytes 122888 | tf_op jit(solution)/shard_map/ppermute | solution.py:58
  91.8 1.3 %collective-permute-start.10 = (f32[2,40,256]{2,1,0:T(8,128)S(1)}, f32[2,40,256]{2,1,0:T(8,128)S(1)}, u32[]{:S(2)}, u32[]{:S(2)}) collective-permute-start(f32[2,40,256]{2,1,0:T(8,128)S(1)} %pad_maximum_fusion.6.refs_1_), channel_id=1, source_target_pairs={{0,8},{8,0},{16,24},{24,16},{1,9},{9,1},{17,25},{25,17},{2,10},{10... | collective-permute-start | bytes 245768 | tf_op jit(solution)/shard_map/ppermute | solution.py:58
  97.7 6.9 %collective-permute-start.11 = (f32[1,40,256]{2,1,0:T(8,128)S(1)}, f32[1,40,256]{2,1,0:T(8,128)S(1)}, u32[]{:S(2)}, u32[]{:S(2)}) collective-permute-start(f32[1,40,256]{2,1,0:T(8,128)S(1)} %bitcast.25), channel_id=1, source_target_pairs={{0,16},{8,24},{16,0},{24,8},{1,17},{9,25},{17,1},{25,9},{2,18},{10... | collective-permute-start | bytes 122888 | tf_op jit(solution)/shard_map/ppermute | solution.py:58
  104.6 1.3 %collective-permute-start.12 = (f32[2,40,256]{2,1,0:T(8,128)S(1)}, f32[2,40,256]{2,1,0:T(8,128)S(1)}, u32[]{:S(2)}, u32[]{:S(2)}) collective-permute-start(f32[2,40,256]{2,1,0:T(8,128)S(1)} %pad_maximum_fusion.7.refs_1_), channel_id=1, source_target_pairs={{0,8},{8,0},{16,24},{24,16},{1,9},{9,1},{17,25},{25,17},{2,10},{10... | collective-permute-start | bytes 245768 | tf_op jit(solution)/shard_map/ppermute | solution.py:58
  110.4 6.3 %collective-permute-start.13 = (f32[1,40,256]{2,1,0:T(8,128)S(1)}, f32[1,40,256]{2,1,0:T(8,128)S(1)}, u32[]{:S(2)}, u32[]{:S(2)}) collective-permute-start(f32[1,40,256]{2,1,0:T(8,128)S(1)} %bitcast.23), channel_id=1, source_target_pairs={{0,16},{8,24},{16,0},{24,8},{1,17},{9,25},{17,1},{25,9},{2,18},{10... | collective-permute-start | bytes 122888 | tf_op jit(solution)/shard_map/ppermute | solution.py:58
  116.8 1.3 %collective-permute-start.14 = (f32[2,40,256]{2,1,0:T(8,128)S(1)}, f32[2,40,256]{2,1,0:T(8,128)S(1)}, u32[]{:S(2)}, u32[]{:S(2)}) collective-permute-start(f32[2,40,256]{2,1,0:T(8,128)S(1)} %pad_maximum_fusion.8.lows_ref), channel_id=1, source_target_pairs={{0,8},{8,0},{16,24},{24,16},{1,9},{9,1},{17,25},{25,17},{2,10},{10... | collective-permute-start | bytes 245768 | tf_op jit(solution)/shard_map/ppermute | solution.py:58
where the time goes:
time: 130 us; the launch traced here: 129 us
  Pallas kernels  66.1 us (51%)
  starting transfers between devices  28.3 us (22%)
  waiting for transfers between devices  23.6 us (18%)
  local copies, waits for them, and re-layouts  6.74 us (5%)
  other arithmetic  3.94 us (3%)
    ppermute x11, waiting for transfers between devices, gather_over(): other = lax.ppermute(held, axis, [(i, i ^ stride) for i in range(n)])  20 us
    pallas_call x1, Pallas kernels, body(): call(forecast_kernel, out(members, rows, cols), [VMEM] * 6, [pltpu.VMEM((...  19.3 us
    pallas_call x3, Pallas kernels, next_of(): call(functools.partial(next_kernel, strides, row_strides, batch), (out(he...  13.6 us
    ppermute x11, starting transfers between devices, gather_over(): other = lax.ppermute(held, axis, [(i, i ^ stride) for i in range(n)])  12.6 us
    pallas_call x1, Pallas kernels, body(): call(functools.partial(final_kernel, row_strides), out(members, rows, col...  10.9 us
    pallas_call x2, Pallas kernels, moved_of(): call(functools.partial(moved_kernel, strides, batches, target), out(ncol,...  9.51 us
    all_to_all x1, starting transfers between devices, body(): lax.all_to_all(jnp.broadcast_to(record, (ncol, *record.shape)), 'col', sp...  6.96 us
    ppermute x2, starting transfers between devices, shift_pair(): lax.ppermute(high_send, axis, forward)  6.18 us
  transfers between devices with their start and end apart: 16, of which 9 were waited for; matrix products, arithmetic and copies ran while one was open for 2% of the time, Pallas kernels for 27%

commit v1 on v0

--- a/solution.py
+++ b/solution.py
@@ -19,7 +19,7 @@
 BF16 = jnp.bfloat16
 SMEM = pl.BlockSpec(memory_space=pltpu.SMEM)
 VMEM = pl.BlockSpec(memory_space=pltpu.VMEM)
-PARAMS = pltpu.CompilerParams(vmem_limit_bytes=48 * 1024 * 1024)
+ANY = pl.BlockSpec(memory_space=pl.ANY)
 
 
 def iota(shape, dim):
@@ -81,35 +81,59 @@
     return hi, mid, rest - mid
 
 
-def prep_kernel(h_ref, coef_ref, loc_ref, obs_ref, to_right_ref, to_left_ref, record_ref):
+def prep_kernel(
+    h_hbm, depth_hbm, sea_hbm, loc_hbm, tile_hbm, cell_hbm, val_hbm, err_hbm, order_hbm,
+    to_right_ref, to_left_ref, record_ref, coef_ref,
+    h_ref, depth_ref, sea_ref, loc_ref, tile_ref, cell_ref, val_ref, err_ref, order_ref, sems,
+):
     members, rows, lanes = h_ref.shape
     groups = members // 8
     half = groups // 2
+    pairs = (
+        (order_hbm, order_ref),
+        (tile_hbm, tile_ref),
+        (cell_hbm, cell_ref),
+        (val_hbm, val_ref),
+        (err_hbm, err_ref),
+        (loc_hbm, loc_ref),
+        (depth_hbm, depth_ref),
+        (sea_hbm, sea_ref),
+    )
+    small = [
+        pltpu.make_async_copy(source, target, sems.at[i])
+        for i, (source, target) in enumerate(pairs)
+    ]
+    large = [
+        pltpu.make_async_copy(
+            h_hbm.at[pl.ds(8 * g, 8)], h_ref.at[pl.ds(8 * g, 8)], sems.at[len(pairs) + g]
+        )
+        for g in range(groups)
+    ]
+    for copy in small + large:
+        copy.start()
     seg = iota((rows, lanes), 1) // SEG
     first = iota((rows, lanes), 1) % SEG < HALO
-    kappa, sea = coef_ref[0], coef_ref[1]
-
-    devices = loc_ref.shape[2]
+    for copy in small[:6]:
+        copy.wait()
+
+    devices = loc_ref.shape[1]
     base = BATCH_COUNT * devices
     fields = FIELDS * BATCH_COUNT
-    width = obs_ref.shape[1]
+    width = val_ref.shape[1]
     record_ref[base:, :] = jnp.zeros((fields, lanes), F32)
-
-    def chosen(k, values):
-        order = obs_ref[fields : fields + 1, k : k + 1]
-        out = values[0]
-        for b in range(1, BATCH_COUNT):
-            out = jnp.where(order == b, values[b], out)
-        return out
-
     for k in range(BATCH_COUNT):
-        level = chosen(k, [loc_ref[b].astype(F32) for b in range(BATCH_COUNT)])
-        record_ref[k * devices : (k + 1) * devices, :] = level.T
-        for f in range(FIELDS):
-            row = f * BATCH_COUNT
-            record_ref[base + row + k : base + row + k + 1, 0:width] = chosen(
-                k, [obs_ref[row + b : row + b + 1, :] for b in range(BATCH_COUNT)]
-            )
+        batch = order_ref[k]
+        record_ref[k * devices : (k + 1) * devices, :] = loc_ref[batch].astype(F32)
+        for f, ref in enumerate((tile_ref, cell_ref, val_ref, err_ref)):
+            row = base + f * BATCH_COUNT + k
+            record_ref[row : row + 1, 0:width] = ref[pl.ds(batch, 1), :].astype(F32)
+
+    for copy in small[6:]:
+        copy.wait()
+    sea = sea_ref[...].astype(F32)
+    kappa = 0.01 * depth_ref[...].astype(F32) * sea
+    coef_ref[0] = kappa
+    coef_ref[1] = sea
 
     def pack(pick):
         out = None
@@ -123,6 +147,8 @@
         to_left_ref[g] = jnp.where(first, pltpu.roll(b, lanes - HALO, axis=1), a)
 
     send(half, pack(lambda q: kappa), pack(lambda q: sea))
+    for copy in large:
+        copy.wait()
     for g in range(half):
         send(g, pack(lambda q: h_ref[8 * g + q]), pack(lambda q: h_ref[8 * (g + half) + q]))
 
@@ -131,7 +157,7 @@
     h_ref, coef_ref, left_ref, right_ref, up_ref, down_ref, out_ref,
     a_ref, b_ref, rhs_ref, sa_ref, sb_ref, srhs_ref, k_ref, sk_ref, w_ref, sw_ref, edge_ref,
 ):
-    members, rows, lanes = h_ref.shape
+    members, rows, lanes = out_ref.shape
     groups = members // 8
     half = groups // 2
     ext = rows + 2 * HALO
@@ -140,23 +166,22 @@
     block = 16
     starts = list(range(0, ext, block))
 
-    def fill(ref, index, upper, centre, lower):
-        ref[index, pl.ds(pad, HALO), :] = upper
-        ref[index, pl.ds(inner, rows), :] = centre
-        ref[index, pl.ds(inner + rows, HALO), :] = lower
-
     for ref in (k_ref, sk_ref):
         for i in range(ref.shape[0]):
             ref[i, pl.ds(0, pad), :] = jnp.zeros((pad, lanes), F32)
             ref[i, pl.ds(pad + ext, pad), :] = jnp.zeros((pad, lanes), F32)
     for i in range(2):
-        fill(k_ref, i, up_ref[members + i], coef_ref[i], down_ref[members + i])
+        k_ref[i, pl.ds(pad, HALO), :] = up_ref[members + i]
+        k_ref[i, pl.ds(inner, rows), :] = coef_ref[i]
+        k_ref[i, pl.ds(inner + rows, HALO), :] = down_ref[members + i]
 
     @pl.loop(0, members)
     def _(m):
-        fill(a_ref, m, up_ref[m], h_ref[m], down_ref[m])
-
-    def strips(start, pick, at, number):
+        a_ref[m, pl.ds(pad, HALO), :] = up_ref[m]
+        a_ref[m, pl.ds(inner, rows), :] = h_ref[m]
+        a_ref[m, pl.ds(inner + rows, HALO), :] = down_ref[m]
+
+    def strips(start, first_row, at, number):
         shape = (block, lanes)
         seg = iota(shape, 1) // SEG
         first = iota(shape, 1) % SEG < HALO
@@ -176,7 +201,11 @@
 
         own = None
         for q in range(8):
-            rolled = pltpu.roll(pick(q), q * SEG + HALO, axis=1)
+            if number:
+                value = a_ref[first_row + q, pl.ds(pad + start, block), :]
+            else:
+                value = k_ref[first_row, pl.ds(pad + start, block), :]
+            rolled = pltpu.roll(value, q * SEG + HALO, axis=1)
             own = rolled if own is None else jnp.where(seg == q, rolled, own)
         source = at % half if number else half
         from_left = incoming(0, source)
@@ -189,11 +218,11 @@
     for start in starts:
         rows_here = pl.ds(pad + start, block)
         for i in range(2):
-            lo, hi = strips(start, lambda q: k_ref[i, rows_here, :], i, 0)
+            lo, hi = strips(start, i, i, 0)
             sk_ref[2 * i, rows_here, :] = lo
             sk_ref[2 * i + 1, rows_here, :] = hi
         for g in range(groups):
-            lo, hi = strips(start, lambda q: a_ref[8 * g + q, rows_here, :], g, groups)
+            lo, hi = strips(start, 8 * g, g, groups)
             sa_ref[g, rows_here, :] = lo
             sa_ref[groups + g, rows_here, :] = hi
 
@@ -506,6 +535,16 @@
     return jnp.where(lane1 == members, 1.0 / (members - 1), out)
 
 
+def product3(left, right):
+    lhi, llo, _ = split3(left)
+    rhi, rlo, _ = split3(right)
+    return jnp.dot(
+        jnp.concatenate([lhi, lhi, llo], axis=1).astype(BF16),
+        jnp.concatenate([rhi, rlo, rhi], axis=0).astype(BF16),
+        preferred_element_type=F32,
+    )
+
+
 def apply_sums(spread, levels, z, height):
     at = jnp.dot(spread, levels, preferred_element_type=F32)
     total = None
@@ -543,9 +582,7 @@
             )
         z = jnp.concatenate([read(i) for i in pair], axis=1)
         sums = apply_sums(spread, jnp.concatenate(levels, axis=1), z, height)
-        z = z + jnp.dot(
-            solved[:, 0:height], sums, precision=HIGH, preferred_element_type=F32
-        )
+        z = z + product3(solved[:, 0:height], sums)
         out += [z[:, 0:LANES], z[:, LANES:]]
     return out
 
@@ -622,9 +659,7 @@
                     term = at[m * height : (m + 1) * height, :] * trans_ref[i, m : m + 1, :]
                     total = term if total is None else total + term
                 sums.append(total)
-        change = jnp.dot(
-            gain, jnp.concatenate(sums, axis=1), precision=HIGH, preferred_element_type=F32
-        )
+        change = product3(gain, jnp.concatenate(sums, axis=1))
         for n, i in enumerate((j, j + 1)):
             part = change[:, n * lanes : (n + 1) * lanes]
             if batch == 0:
@@ -647,11 +682,24 @@
         )
 
 
+def split_kernel(state_ref, out_ref):
+    members, rows, _ = state_ref.shape
+
+    @pl.loop(0, rows // 8)
+    def _(b):
+        start = pl.multiple_of(b * 8, 8)
+        turned = jnp.swapaxes(state_ref[:, pl.ds(start, 8), :], 0, 1)
+        for i in range(8):
+            hi, lo, _ = split3(turned[i])
+            out_ref[start + i] = jnp.concatenate([hi, lo], axis=0).astype(BF16)
+
+
 def final_kernel(
     row_strides, me_ref, lows_ref, highs_ref, record_ref, trans_ref, state_ref, out_ref,
     spread_ref, whole_ref, turned_ref,
 ):
-    members, rows, lanes = state_ref.shape
+    rows, lanes = state_ref.shape[0], state_ref.shape[2]
+    members = state_ref.shape[1] // 2
     height, width = lows_ref.shape[1:]
     ncol = width // members
     devices = 2 * lows_ref.shape[0] * ncol
@@ -668,27 +716,23 @@
     @pl.loop(0, rows // 8)
     def _(b):
         start = pl.multiple_of(b * 8, 8)
-        turned = jnp.swapaxes(state_ref[:, pl.ds(start, 8), :], 0, 1)
         done = []
         for i in range(8):
-            hi, lo, _ = split3(turned[i])
-            right = jnp.concatenate([hi, lo, hi, jnp.zeros_like(hi)], axis=0).astype(BF16)
-            done.append(
-                jnp.dot(
-                    turned_ref[start + i].astype(BF16), right, preferred_element_type=F32
-                )
-            )
+            both = state_ref[start + i]
+            right = jnp.concatenate([both, both[0:members]], axis=0)
+            left = turned_ref[start + i][:, 0 : 3 * members].astype(BF16)
+            done.append(jnp.dot(left, right, preferred_element_type=F32))
         out_ref[:, pl.ds(start, 8), :] = jnp.swapaxes(jnp.stack(done), 0, 1)
 
 
-def call(kernel, out_shape, in_specs, scratch=(), flops=10**6):
+def call(kernel, out_shape, in_specs, scratch=(), limit=48, out_specs=None):
     return pl.pallas_call(
         kernel,
         out_shape=out_shape,
         in_specs=in_specs,
-        out_specs=jax.tree.map(lambda _: VMEM, out_shape),
+        out_specs=out_specs or jax.tree.map(lambda _: VMEM, out_shape),
         scratch_shapes=list(scratch),
-        compiler_params=PARAMS,
+        compiler_params=pltpu.CompilerParams(vmem_limit_bytes=limit * 1024 * 1024),
     )
 
 
@@ -709,18 +753,28 @@
         return jax.ShapeDtypeStruct(shape, dtype)
 
     record_rows = BATCH_COUNT * devices + FIELDS * BATCH_COUNT
-    sea = land_sea.astype(F32)
-    coef = jnp.stack([0.01 * depth.astype(F32) * sea, sea])
     share = obs_cell.shape[1]
-    order = jnp.pad(batch_order.astype(F32)[None], ((0, 7), (0, share - BATCH_COUNT)))
-    observed = jnp.concatenate(
-        [obs_tile[:, :, 0].astype(F32), obs_cell.astype(F32), obs_value, obs_error, order]
+    to_right, to_left, record, coef = call(
+        prep_kernel,
+        (out(half + 1, rows, cols), out(half + 1, rows, cols), out(record_rows, cols), out(2, rows, cols)),
+        [ANY] * 9,
+        [
+            pltpu.VMEM((members, rows, cols), F32),
+            pltpu.VMEM((rows, cols), jnp.int32),
+            pltpu.VMEM((rows, cols), jnp.int32),
+            pltpu.VMEM((BATCH_COUNT, devices, rows), jnp.int32),
+            pltpu.VMEM((BATCH_COUNT, share), jnp.int32),
+            pltpu.VMEM((BATCH_COUNT, share), jnp.int32),
+            pltpu.VMEM((BATCH_COUNT, share), F32),
+            pltpu.VMEM((BATCH_COUNT, share), F32),
+            pltpu.SMEM((BATCH_COUNT,), jnp.int32),
+            pltpu.SemaphoreType.DMA((8 + groups,)),
+        ],
+        limit=58,
+    )(
+        sample_heights, depth, land_sea, jnp.transpose(loc_level[:, :, 0, :], (0, 2, 1)), obs_tile[:, :, 0], obs_cell,
+        obs_value, obs_error, batch_order,
     )
-    to_right, to_left, record = call(
-        prep_kernel,
-        (out(half + 1, rows, cols), out(half + 1, rows, cols), out(record_rows, cols)),
-        [VMEM] * 4,
-    )(sample_heights, coef, loc_level[:, :, 0, :], observed)
     left, right = shift_pair(to_left, to_right, "col")
 
     def slab(start):
@@ -752,14 +806,14 @@
             pltpu.VMEM((groups, ext, cols), F32),
         ],
     )(sample_heights, coef, left, right, up, down)
-
     mine = call(
-        functools.partial(extract_kernel, obs_cell.shape[1]),
+        functools.partial(extract_kernel, share),
         out(BATCH_COUNT * members + FIELDS * BATCH_COUNT, cols),
         [SMEM, VMEM, VMEM],
         [pltpu.VMEM((8, cols), F32)],
     )(me, records, state)
     seen = gather_over(mine, "col")
+    parts = call(split_kernel, out(rows, 2 * members, cols, dtype=BF16), [VMEM])(state)
 
     sums = call(
         functools.partial(first_kernel, members), out(height, members * ncol), [VMEM] * 2
@@ -800,13 +854,13 @@
 
     every, _ = exchange(sums, ())
     sums, first = next_of(0, every, None)
-    every, (z2, trans) = exchange(
-        sums, (moved_of((0,), 2, first, None), compose_of((0,), first, None))
-    )
+    every, (z2,) = exchange(sums, (moved_of((0,), 2, first, None),))
+    trans = compose_of((0,), first, None)
     sums, second = next_of(1, every, z2)
     every, (z3,) = exchange(sums, (moved_of((0, 1), 3, first + second, None),))
     sums, third = next_of(2, every, z3)
-    every, (trans,) = exchange(sums, (compose_of((1, 2), second + third, trans),))
+    every, (trans,) = exchange(sums, (compose_of((1,), second, trans),))
+    trans = compose_of((2,), third, trans)
     return call(
         functools.partial(final_kernel, row_strides),
         out(members, rows, cols),
@@ -816,7 +870,7 @@
             pltpu.VMEM((members, members, cols), F32),
             pltpu.VMEM((rows, members, cols), F32),
         ],
-    )(me, *every, records, trans, state)
+    )(me, *every, records, trans, parts)
 
 
 def solution(mesh):

time: 130 us -> 124 us (0.954)
  other arithmetic: 3.94 us -> 0.18 us
  local copies, waits for them, and re-layouts: 6.74 us -> 4.33 us
  Pallas kernels: 66.1 us -> 68 us
    unnamed x5 -> x4, local copies, waits for them, and re-layouts: 4.15 us -> 1.6 us
    pallas_call x1, Pallas kernels: 1.36 us -> 3.34 us  [body(): call(prep_kernel, (out(half + 1, rows, cols), out(half + 1, rows, cols),...]
    another operation x4 -> x0, other arithmetic: 1.74 us -> none  [body(): coef = jnp.stack([0.01 * depth.astype(F32) * sea, sea])]
    convert_element_type x2 -> x0, other arithmetic: 1.37 us -> none  [the longest x1 0.68 us: body(): obs_tile[:, :, 0].astype(F32)]
    pallas_call x1 -> x2, Pallas kernels: 4.63 us -> 5.4 us  [the longest x1 4.63 us: body(): call(functools.partial(extract_kernel, share), out(BATCH_COUNT * members...]
    pallas_call x2 -> x3, Pallas kernels: 6.17 us -> 6.18 us  [compose_of(): call(functools.partial(compose_kernel, batches), out(members, members, co...]
  transfers between devices with their start and end apart: 16 -> 16, of which waited for: 9 -> 8; matrix products, arithmetic and copies ran while one was open for 2% -> 2% of each run, Pallas kernels for 27% -> 28%
where the time goes in v1:
time: 124 us
  Pallas kernels  68 us (55%)
  starting transfers between devices  28.5 us (23%)
  waiting for transfers between devices  22.4 us (18%)
  local copies, waits for them, and re-layouts  4.33 us (3%)
    pallas_call x1, Pallas kernels, body(): call(forecast_kernel, out(members, rows, cols), [VMEM] * 6, [pltpu.VMEM((...  19.3 us
    ppermute x11, waiting for transfers between devices, gather_over(): other = lax.ppermute(held, axis, [(i, i ^ stride) for i in range(n)])  18.8 us
    pallas_call x3, Pallas kernels, next_of(): call(functools.partial(next_kernel, strides, row_strides, batch), (out(he...  13.7 us
    ppermute x11, starting transfers between devices, gather_over(): other = lax.ppermute(held, axis, [(i, i ^ stride) for i in range(n)])  12.6 us
    pallas_call x1, Pallas kernels, body(): call(functools.partial(final_kernel, row_strides), out(members, rows, col...  10.6 us
    pallas_call x2, Pallas kernels, moved_of(): call(functools.partial(moved_kernel, strides, batches, target), out(ncol,...  8.85 us
    all_to_all x1, starting transfers between devices, body(): lax.all_to_all(jnp.broadcast_to(record, (ncol, *record.shape)), 'col', sp...  6.96 us
    ppermute x2, starting transfers between devices, shift_pair(): lax.ppermute(high_send, axis, forward)  6.31 us
  transfers between devices with their start and end apart: 16, of which 8 were waited for; matrix products, arithmetic and copies ran while one was open for 2% of the time, Pallas kernels for 28%

profile of v1, /device:TPU:0, one launch (start us, length us, event | category | flops | bytes accessed | tf_op | source)
XLA Modules:
  0.0 123.6 jit_solution(992941406697860895)
XLA Ops:
  0.0 3.3 %shard_map.91 = (f32[3,128,128]{2,1,0:T(8,128)}, f32[3,128,128]{2,1,0:T(8,128)}, f32[144,128]{1,0:T(8,128)}, f32[2,128,128]{2,1,0:T(8,128)}) custom-call(f32[32,128,128]{2,1,0:T(8,128)} %h_ref.1, s32[128,128]{1,0:T(8,128)} %depth_hbm.1, s32[128,128]{1,0:T(8,128)} %sea_hbm.1, s32[4,32,128]{2,1,0:T(8,128)} %bitcast.22, s32[4,64]{1,0:T(4,128)} %bitcast.23, ...), custom_call_target="tpu_custom_call" | custom-call | tf_op jit(solution)/shard_map/pallas_call | solution.py:757
  3.4 5.0 %collective-permute-start = (f32[3,128,128]{2,1,0:T(8,128)}, f32[3,128,128]{2,1,0:T(8,128)S(1)}, u32[]{:S(2)}, u32[]{:S(2)}) collective-permute-start(f32[3,128,128]{2,1,0:T(8,128)} %get-tuple-element.26), channel_id=1, source_target_pairs={{0,1},{1,2},{2,3},{3,4},{4,5},{5,6},{6,7},{8,9},{9,10},{10,11},{11... | collective-permute-start | bytes 589832 | tf_op jit(solution)/shard_map/ppermute | solution.py:68
  9.7 1.7 %broadcast_in_dim.18 = f32[8,144,128]{2,1,0:T(8,128)} broadcast(f32[144,128]{1,0:T(8,128)} %get-tuple-element.24), dimensions={1,2} | broadcast | bytes 663552 | tf_op jit(solution)/shard_map/broadcast_in_dim | solution.py:786
  11.4 7.0 %all-to-all-start = ((f32[8,144,128]{2,1,0:T(8,128)}), f32[8,144,128]{2,1,0:T(8,128)S(1)}, u32[]{:S(2)}, u32[]{:S(2)}) async-start(f32[8,144,128]{2,1,0:T(8,128)} %broadcast_in_dim.18), calls=%async_computation | async-start | bytes 1179648 | tf_op jit(solution)/shard_map/all_to_all | solution.py:785
  22.2 3.6 %collective-permute-done.3.down_ref = f32[40,8,128]{2,1,0:T(8,128)S(1)} collective-permute-done((f32[40,8,128]{2,1,0:T(8,128)S(1)}, f32[40,8,128]{2,1,0:T(8,128)S(1)}, u32[]{:S(2)}, u32[]{:S(2)}) %collective-permute-start.3) | collective-permute-done | bytes 163872 | tf_op jit(solution)/shard_map/ppermute | solution.py:68
  25.8 1.6 %copy-done = f32[32,128,128]{2,1,0:T(8,128)S(1)} copy-done((f32[32,128,128]{2,1,0:T(8,128)S(1)}, f32[32,128,128]{2,1,0:T(8,128)}, u32[]{:S(2)}) %copy-start) | copy-done | bytes 2097176
  27.4 19.3 %shard_map.92.state_ref = f32[32,128,128]{2,1,0:T(8,128)S(1)} custom-call(f32[32,128,128]{2,1,0:T(8,128)S(1)} %copy-done, f32[2,128,128]{2,1,0:T(8,128)S(1)} %copy-done.1, f32[3,128,128]{2,1,0:T(8,128)S(1)} %collective-permute-done.left_ref, f32[3,128,128]{2,1,0:T(8,128)S(1)} %collective-permute-done.1.right_ref, ...), custom_call_target="tpu_custom_call" | custom-call | tf_op jit(solution)/shard_map/pallas_call | solution.py:791
  46.7 4.6 %shard_map.93 = f32[144,128]{1,0:T(8,128)S(1)} custom-call(s32[2]{0:T(128)S(1)} %pad_add_fusion.me_ref.refs_0_, f32[8,144,128]{2,1,0:T(8,128)S(1)} %all-to-all-done.record_ref.refs_3_.refs_1_, f32[32,128,128]{2,1,0:T(8,128)S(1)} %shard_map.92.state_ref), custom_call_target="tpu_custom_call" | custom-call | tf_op jit(solution)/shard_map/pallas_call | solution.py:809
  51.4 3.0 %collective-permute-start.4 = (f32[1,144,128]{2,1,0:T(8,128)S(1)}, f32[1,144,128]{2,1,0:T(8,128)S(1)}, u32[]{:S(2)}, u32[]{:S(2)}) collective-permute-start(f32[1,144,128]{2,1,0:T(8,128)S(1)} %bitcast.11), channel_id=1, source_target_pairs={{0,4},{1,5},{2,6},{3,7},{4,0},{5,1},{6,2},{7,3},{8,12},{9,13},{10,... | collective-permute-start | bytes 221192 | tf_op jit(solution)/shard_map/ppermute | solution.py:58
  54.3 2.3 %collective-permute-done.4 = f32[1,144,128]{2,1,0:T(8,128)S(1)} collective-permute-done((f32[1,144,128]{2,1,0:T(8,128)S(1)}, f32[1,144,128]{2,1,0:T(8,128)S(1)}, u32[]{:S(2)}, u32[]{:S(2)}) %collective-permute-start.4) | collective-permute-done | bytes 73760 | tf_op jit(solution)/shard_map/ppermute | solution.py:58
  56.7 2.1 %collective-permute-start.5 = (f32[2,144,128]{2,1,0:T(8,128)S(1)}, f32[2,144,128]{2,1,0:T(8,128)S(1)}, u32[]{:S(2)}, u32[]{:S(2)}) collective-permute-start(f32[2,144,128]{2,1,0:T(8,128)S(1)} %pad_maximum_fusion.3), channel_id=1, source_target_pairs={{0,2},{1,3},{2,0},{3,1},{4,6},{5,7},{6,4},{7,5},{8,10},{9,11},{10,... | collective-permute-start | bytes 442376 | tf_op jit(solution)/shard_map/ppermute | solution.py:58
  58.8 3.1 %collective-permute-done.5 = f32[2,144,128]{2,1,0:T(8,128)S(1)} collective-permute-done((f32[2,144,128]{2,1,0:T(8,128)S(1)}, f32[2,144,128]{2,1,0:T(8,128)S(1)}, u32[]{:S(2)}, u32[]{:S(2)}) %collective-permute-start.5) | collective-permute-done | bytes 147488 | tf_op jit(solution)/shard_map/ppermute | solution.py:58
  61.9 2.1 %collective-permute-start.6 = (f32[4,144,128]{2,1,0:T(8,128)S(1)}, f32[4,144,128]{2,1,0:T(8,128)S(1)}, u32[]{:S(2)}, u32[]{:S(2)}) collective-permute-start(f32[4,144,128]{2,1,0:T(8,128)S(1)} %pad_maximum_fusion.low_ref.refs_4_.refs_2_), channel_id=1, source_target_pairs={{0,1},{1,0},{2,3},{3,2},{4,5},{5,4},{6,7},{7,6},{8,9},{9,8},{10,11... | collective-permute-start | bytes 884744 | tf_op jit(solution)/shard_map/ppermute | solution.py:58
  64.0 6.9 %collective-permute-done.6.high_ref.refs_5_.refs_3_ = f32[4,144,128]{2,1,0:T(8,128)S(1)} collective-permute-done((f32[4,144,128]{2,1,0:T(8,128)S(1)}, f32[4,144,128]{2,1,0:T(8,128)S(1)}, u32[]{:S(2)}, u32[]{:S(2)}) %collective-permute-start.6) | collective-permute-done | bytes 294944 | tf_op jit(solution)/shard_map/ppermute | solution.py:58
  71.5 1.8 %collective-permute-start.7 = (f32[1,40,256]{2,1,0:T(8,128)S(1)}, f32[1,40,256]{2,1,0:T(8,128)S(1)}, u32[]{:S(2)}, u32[]{:S(2)}) collective-permute-start(f32[1,40,256]{2,1,0:T(8,128)S(1)} %bitcast.14), channel_id=1, source_target_pairs={{0,16},{8,24},{16,0},{24,8},{1,17},{9,25},{17,1},{25,9},{2,18},{10... | collective-permute-start | bytes 122888 | tf_op jit(solution)/shard_map/ppermute | solution.py:58
  73.2 2.6 %collective-permute-done.7 = f32[1,40,256]{2,1,0:T(8,128)S(1)} collective-permute-done((f32[1,40,256]{2,1,0:T(8,128)S(1)}, f32[1,40,256]{2,1,0:T(8,128)S(1)}, u32[]{:S(2)}, u32[]{:S(2)}) %collective-permute-start.7) | collective-permute-done | bytes 40992 | tf_op jit(solution)/shard_map/ppermute | solution.py:58
  77.1 4.5 %shard_map.95 = (f32[40,256]{1,0:T(8,128)S(1)}, bf16[1280,128]{1,0:T(8,128)(2,1)S(1)}, f32[32,128]{1,0:T(8,128)S(1)}) custom-call(s32[2]{0:T(128)S(1)} %pad_add_fusion.me_ref.refs_0_, f32[2,40,256]{2,1,0:T(8,128)S(1)} %pad_maximum_fusion.4.refs_1_, f32[2,40,256]{2,1,0:T(8,128)S(1)} %collective-permute-done.8.refs_2_, ...), custom_call_target="tpu_custom_call" | custom-call | tf_op jit(solution)/shard_map/pallas_call | solution.py:841
  83.0 3.2 %shard_map.96.refs_6_ = f32[8,32,128]{2,1,0:T(8,128)S(1)} custom-call(s32[2]{0:T(128)S(1)} %pad_add_fusion.me_ref.refs_0_, f32[8,144,128]{2,1,0:T(8,128)S(1)} %all-to-all-done.record_ref.refs_3_.refs_1_, f32[4,144,128]{2,1,0:T(8,128)S(1)} %pad_maximum_fusion.low_ref.refs_4_.refs_2_, f32[4,144,128]{2,1,0:T(8,128)S(1)} %collective-permute-done.6.high_ref.refs_5_.refs_3_, ...), custom_call_target="tpu_custom_call" | custom-call | tf_op jit(solution)/shard_map/pallas_call | solution.py:833
  87.6 4.5 %shard_map.97 = (f32[40,256]{1,0:T(8,128)S(1)}, bf16[1280,128]{1,0:T(8,128)(2,1)S(1)}, f32[32,128]{1,0:T(8,128)S(1)}) custom-call(s32[2]{0:T(128)S(1)} %pad_add_fusion.me_ref.refs_0_, f32[2,40,256]{2,1,0:T(8,128)S(1)} %pad_maximum_fusion.5.refs_1_, f32[2,40,256]{2,1,0:T(8,128)S(1)} %collective-permute-done.10.refs_2_, ...), custom_call_target="tpu_custom_call" | custom-call | tf_op jit(solution)/shard_map/pallas_call | solution.py:841
  92.9 5.7 %shard_map.98.refs_6_ = f32[8,32,128]{2,1,0:T(8,128)S(1)} custom-call(s32[2]{0:T(128)S(1)} %pad_add_fusion.me_ref.refs_0_, f32[8,144,128]{2,1,0:T(8,128)S(1)} %all-to-all-done.record_ref.refs_3_.refs_1_, f32[4,144,128]{2,1,0:T(8,128)S(1)} %pad_maximum_fusion.low_ref.refs_4_.refs_2_, f32[4,144,128]{2,1,0:T(8,128)S(1)} %collective-permute-done.6.high_ref.refs_5_.refs_3_, ...), custom_call_target="tpu_custom_call" | custom-call | tf_op jit(solution)/shard_map/pallas_call | solution.py:833
  99.9 4.7 %shard_map.99 = (f32[40,256]{1,0:T(8,128)S(1)}, bf16[1280,128]{1,0:T(8,128)(2,1)S(1)}, f32[32,128]{1,0:T(8,128)S(1)}) custom-call(s32[2]{0:T(128)S(1)} %pad_add_fusion.me_ref.refs_0_, f32[2,40,256]{2,1,0:T(8,128)S(1)} %pad_maximum_fusion.6.refs_1_, f32[2,40,256]{2,1,0:T(8,128)S(1)} %collective-permute-done.12.refs_2_, ...), custom_call_target="tpu_custom_call" | custom-call | tf_op jit(solution)/shard_map/pallas_call | solution.py:841
  106.9 2.6 %shard_map.101.refs_2_ = f32[32,32,128]{2,1,0:T(8,128)S(1)} custom-call(s32[2]{0:T(128)S(1)} %pad_add_fusion.me_ref.refs_0_, f32[8,144,128]{2,1,0:T(8,128)S(1)} %all-to-all-done.record_ref.refs_3_.refs_1_, bf16[1280,128]{1,0:T(8,128)(2,1)S(1)} %get-tuple-element.34.refs_6_.refs_0_, f32[32,128]{1,0:T(8,128)S(1)} %get-tuple-element.35.refs_7_.refs_1_, ...), custom_call_target="tpu_custom_call" | custom-call | tf_op jit(solution)/shard_map/pallas_call | solution.py:825
  110.4 2.6 %shard_map.102.trans_ref = f32[32,32,128]{2,1,0:T(8,128)S(1)} custom-call(s32[2]{0:T(128)S(1)} %pad_add_fusion.me_ref.refs_0_, f32[8,144,128]{2,1,0:T(8,128)S(1)} %all-to-all-done.record_ref.refs_3_.refs_1_, bf16[1280,128]{1,0:T(8,128)(2,1)S(1)} %get-tuple-element.40.refs_0_, f32[32,128]{1,0:T(8,128)S(1)} %get-tuple-element.41.refs_1_, ...), custom_call_target="tpu_custom_call" | custom-call | tf_op jit(solution)/shard_map/pallas_call | solution.py:825
  113.0 10.6 %shard_map.104 = f32[32,128,128]{2,1,0:T(8,128)} custom-call(s32[2]{0:T(128)S(1)} %pad_add_fusion.me_ref.refs_0_, f32[2,40,256]{2,1,0:T(8,128)S(1)} %pad_maximum_fusion.7.lows_ref, f32[2,40,256]{2,1,0:T(8,128)S(1)} %collective-permute-done.14.highs_ref, f32[8,144,128]{2,1,0:T(8,128)S(1)} %all-to-all-done.record_ref.refs_3_.refs_1_, ...), custom_call_target="tpu_custom_call" | custom-call | tf_op jit(solution)/shard_map/pallas_call | solution.py:864
  (40 shorter events, 15.0 us)
Async XLA Ops:
  3.3 16.0 %copy-start.1 = (f32[2,128,128]{2,1,0:T(8,128)S(1)}, f32[2,128,128]{2,1,0:T(8,128)}, u32[]{:S(2)}) copy-start(f32[2,128,128]{2,1,0:T(8,128)} %get-tuple-element.25.coef_ref) | copy-start | bytes 393220
  3.4 16.0 %collective-permute-start = (f32[3,128,128]{2,1,0:T(8,128)}, f32[3,128,128]{2,1,0:T(8,128)S(1)}, u32[]{:S(2)}, u32[]{:S(2)}) collective-permute-start(f32[3,128,128]{2,1,0:T(8,128)} %get-tuple-element.26), channel_id=1, source_target_pairs={{0,1},{1,2},{2,3},{3,4},{4,5},{5,6},{6,7},{8,9},{9,10},{10,11},{11... | collective-permute-start | bytes 589832 | tf_op jit(solution)/shard_map/ppermute | solution.py:68
  8.4 11.0 %collective-permute-start.1 = (f32[3,128,128]{2,1,0:T(8,128)}, f32[3,128,128]{2,1,0:T(8,128)S(1)}, u32[]{:S(2)}, u32[]{:S(2)}) collective-permute-start(f32[3,128,128]{2,1,0:T(8,128)} %get-tuple-element.27), channel_id=1, source_target_pairs={{1,0},{2,1},{3,2},{4,3},{5,4},{6,5},{7,6},{9,8},{10,9},{11,10},{12... | collective-permute-start | bytes 589832 | tf_op jit(solution)/shard_map/ppermute | solution.py:68
  11.4 35.3 %all-to-all-start = ((f32[8,144,128]{2,1,0:T(8,128)}), f32[8,144,128]{2,1,0:T(8,128)S(1)}, u32[]{:S(2)}, u32[]{:S(2)}) async-start(f32[8,144,128]{2,1,0:T(8,128)} %broadcast_in_dim.18), calls=%async_computation | async-start | bytes 1179648 | tf_op jit(solution)/shard_map/all_to_all | solution.py:785
  19.5 2.7 %collective-permute-start.2 = (f32[40,8,128]{2,1,0:T(8,128)S(1)}, f32[40,8,128]{2,1,0:T(8,128)S(1)}, u32[]{:S(2)}, u32[]{:S(2)}) collective-permute-start(f32[40,8,128]{2,1,0:T(8,128)S(1)} %pad_maximum_fusion.1), channel_id=1, source_target_pairs={{0,8},{8,16},{16,24},{1,9},{9,17},{17,25},{2,10},{10,18},{18,26},{... | collective-permute-start | bytes 491528 | tf_op jit(solution)/shard_map/ppermute | solution.py:68
  20.8 5.0 %collective-permute-start.3 = (f32[40,8,128]{2,1,0:T(8,128)S(1)}, f32[40,8,128]{2,1,0:T(8,128)S(1)}, u32[]{:S(2)}, u32[]{:S(2)}) collective-permute-start(f32[40,8,128]{2,1,0:T(8,128)S(1)} %pad_maximum_fusion.2), channel_id=1, source_target_pairs={{8,0},{16,8},{24,16},{9,1},{17,9},{25,17},{10,2},{18,10},{26,18},{... | collective-permute-start | bytes 491528 | tf_op jit(solution)/shard_map/ppermute | solution.py:68
  25.8 1.6 %copy-start = (f32[32,128,128]{2,1,0:T(8,128)S(1)}, f32[32,128,128]{2,1,0:T(8,128)}, u32[]{:S(2)}) copy-start(f32[32,128,128]{2,1,0:T(8,128)} %h_ref.1) | copy-start | bytes 6291460
  51.4 5.3 %collective-permute-start.4 = (f32[1,144,128]{2,1,0:T(8,128)S(1)}, f32[1,144,128]{2,1,0:T(8,128)S(1)}, u32[]{:S(2)}, u32[]{:S(2)}) collective-permute-start(f32[1,144,128]{2,1,0:T(8,128)S(1)} %bitcast.11), channel_id=1, source_target_pairs={{0,4},{1,5},{2,6},{3,7},{4,0},{5,1},{6,2},{7,3},{8,12},{9,13},{10,... | collective-permute-start | bytes 221192 | tf_op jit(solution)/shard_map/ppermute | solution.py:58
  56.7 5.2 %collective-permute-start.5 = (f32[2,144,128]{2,1,0:T(8,128)S(1)}, f32[2,144,128]{2,1,0:T(8,128)S(1)}, u32[]{:S(2)}, u32[]{:S(2)}) collective-permute-start(f32[2,144,128]{2,1,0:T(8,128)S(1)} %pad_maximum_fusion.3), channel_id=1, source_target_pairs={{0,2},{1,3},{2,0},{3,1},{4,6},{5,7},{6,4},{7,5},{8,10},{9,11},{10,... | collective-permute-start | bytes 442376 | tf_op jit(solution)/shard_map/ppermute | solution.py:58
  61.9 8.9 %collective-permute-start.6 = (f32[4,144,128]{2,1,0:T(8,128)S(1)}, f32[4,144,128]{2,1,0:T(8,128)S(1)}, u32[]{:S(2)}, u32[]{:S(2)}) collective-permute-start(f32[4,144,128]{2,1,0:T(8,128)S(1)} %pad_maximum_fusion.low_ref.refs_4_.refs_2_), channel_id=1, source_target_pairs={{0,1},{1,0},{2,3},{3,2},{4,5},{5,4},{6,7},{7,6},{8,9},{9,8},{10,11... | collective-permute-start | bytes 884744 | tf_op jit(solution)/shard_map/ppermute | solution.py:58
  71.5 4.4 %collective-permute-start.7 = (f32[1,40,256]{2,1,0:T(8,128)S(1)}, f32[1,40,256]{2,1,0:T(8,128)S(1)}, u32[]{:S(2)}, u32[]{:S(2)}) collective-permute-start(f32[1,40,256]{2,1,0:T(8,128)S(1)} %bitcast.14), channel_id=1, source_target_pairs={{0,16},{8,24},{16,0},{24,8},{1,17},{9,25},{17,1},{25,9},{2,18},{10... | collective-permute-start | bytes 122888 | tf_op jit(solution)/shard_map/ppermute | solution.py:58
  75.9 1.3 %collective-permute-start.8 = (f32[2,40,256]{2,1,0:T(8,128)S(1)}, f32[2,40,256]{2,1,0:T(8,128)S(1)}, u32[]{:S(2)}, u32[]{:S(2)}) collective-permute-start(f32[2,40,256]{2,1,0:T(8,128)S(1)} %pad_maximum_fusion.4.refs_1_), channel_id=1, source_target_pairs={{0,8},{8,0},{16,24},{24,16},{1,9},{9,1},{17,25},{25,17},{2,10},{10... | collective-permute-start | bytes 245768 | tf_op jit(solution)/shard_map/ppermute | solution.py:58
  81.6 4.6 %collective-permute-start.9 = (f32[1,40,256]{2,1,0:T(8,128)S(1)}, f32[1,40,256]{2,1,0:T(8,128)S(1)}, u32[]{:S(2)}, u32[]{:S(2)}) collective-permute-start(f32[1,40,256]{2,1,0:T(8,128)S(1)} %bitcast.20), channel_id=1, source_target_pairs={{0,16},{8,24},{16,0},{24,8},{1,17},{9,25},{17,1},{25,9},{2,18},{10... | collective-permute-start | bytes 122888 | tf_op jit(solution)/shard_map/ppermute | solution.py:58
  86.2 1.3 %collective-permute-start.10 = (f32[2,40,256]{2,1,0:T(8,128)S(1)}, f32[2,40,256]{2,1,0:T(8,128)S(1)}, u32[]{:S(2)}, u32[]{:S(2)}) collective-permute-start(f32[2,40,256]{2,1,0:T(8,128)S(1)} %pad_maximum_fusion.5.refs_1_), channel_id=1, source_target_pairs={{0,8},{8,0},{16,24},{24,16},{1,9},{9,1},{17,25},{25,17},{2,10},{10... | collective-permute-start | bytes 245768 | tf_op jit(solution)/shard_map/ppermute | solution.py:58
  92.1 6.5 %collective-permute-start.11 = (f32[1,40,256]{2,1,0:T(8,128)S(1)}, f32[1,40,256]{2,1,0:T(8,128)S(1)}, u32[]{:S(2)}, u32[]{:S(2)}) collective-permute-start(f32[1,40,256]{2,1,0:T(8,128)S(1)} %bitcast.18), channel_id=1, source_target_pairs={{0,16},{8,24},{16,0},{24,8},{1,17},{9,25},{17,1},{25,9},{2,18},{10... | collective-permute-start | bytes 122888 | tf_op jit(solution)/shard_map/ppermute | solution.py:58
  98.6 1.3 %collective-permute-start.12 = (f32[2,40,256]{2,1,0:T(8,128)S(1)}, f32[2,40,256]{2,1,0:T(8,128)S(1)}, u32[]{:S(2)}, u32[]{:S(2)}) collective-permute-start(f32[2,40,256]{2,1,0:T(8,128)S(1)} %pad_maximum_fusion.6.refs_1_), channel_id=1, source_target_pairs={{0,8},{8,0},{16,24},{24,16},{1,9},{9,1},{17,25},{25,17},{2,10},{10... | collective-permute-start | bytes 245768 | tf_op jit(solution)/shard_map/ppermute | solution.py:58
  104.6 4.9 %collective-permute-start.13 = (f32[1,40,256]{2,1,0:T(8,128)S(1)}, f32[1,40,256]{2,1,0:T(8,128)S(1)}, u32[]{:S(2)}, u32[]{:S(2)}) collective-permute-start(f32[1,40,256]{2,1,0:T(8,128)S(1)} %bitcast.16), channel_id=1, source_target_pairs={{0,16},{8,24},{16,0},{24,8},{1,17},{9,25},{17,1},{25,9},{2,18},{10... | collective-permute-start | bytes 122888 | tf_op jit(solution)/shard_map/ppermute | solution.py:58
  109.6 3.4 %collective-permute-start.14 = (f32[2,40,256]{2,1,0:T(8,128)S(1)}, f32[2,40,256]{2,1,0:T(8,128)S(1)}, u32[]{:S(2)}, u32[]{:S(2)}) collective-permute-start(f32[2,40,256]{2,1,0:T(8,128)S(1)} %pad_maximum_fusion.7.lows_ref), channel_id=1, source_target_pairs={{0,8},{8,0},{16,24},{24,16},{1,9},{9,1},{17,25},{25,17},{2,10},{10... | collective-permute-start | bytes 245768 | tf_op jit(solution)/shard_map/ppermute | solution.py:58

commit v2 on v1

--- a/solution.py
+++ b/solution.py
@@ -48,17 +48,18 @@
     return out
 
 
-def gather_over(block, axis, beside=None):
+def gather_over(block, axis, early=(), late=()):
     n = lax.axis_size(axis)
     held = block[None]
     strides = strides_of(n)
     for stride in strides:
-        if stride == strides[-1] and beside is not None:
-            held, beside = lax.optimization_barrier((held, beside))
+        if stride == strides[-1]:
+            held, early = lax.optimization_barrier((held, early))
         other = lax.ppermute(held, axis, [(i, i ^ stride) for i in range(n)])
         if stride != strides[-1]:
             held = jnp.concatenate([held, other], axis=0)
-    return (held, other) if beside is None else ((held, other), beside)
+    other, late = lax.optimization_barrier((other, late))
+    return (held, other), early, late
 
 
 def shift_pair(low_send, high_send, axis):
@@ -351,11 +352,12 @@
     me = me_ref[1]
     stacked = jnp.concatenate([record_ref[p, base:, :] for p in range(ncol)], axis=0)
     pieces = [
-        stacked[i * lanes : (i + 1) * lanes, :].T for i in range(ncol * fields // lanes)
+        stacked[i * lanes : (i + 1) * lanes, :].T[0:owner_share]
+        for i in range(ncol * fields // lanes)
     ]
-    lane = iota((lanes, lanes), 1)
-    triangle = (lane < iota((lanes, lanes), 0)).astype(BF16)
-    valid = iota((lanes, lanes), 0) < owner_share
+    lane = iota((owner_share, lanes), 1)
+    square = (owner_share, owner_share)
+    triangle = (iota(square, 1) < iota(square, 0)).astype(BF16)
     slot = (lane % capacity).astype(F32)
 
     def spread(f, k):
@@ -369,7 +371,7 @@
     base = BATCH_COUNT * members
     out_ref[base + 3 * BATCH_COUNT :, :] = jnp.zeros((BATCH_COUNT, lanes), F32)
     for k in range(BATCH_COUNT):
-        mine = valid & (spread(0, k) == me.astype(F32))
+        mine = spread(0, k) == me.astype(F32)
         rank = jnp.dot(triangle, mine.astype(BF16), preferred_element_type=F32)
         hot = mine & (rank == slot)
 
@@ -378,10 +380,13 @@
 
         cell = spread(1, k).astype(jnp.int32)
         x = cell // lanes
-        error = jnp.where(hot, spread(3, k), 1.0)
-        for n, values in enumerate((1.0 / error, spread(2, k), (x + 1).astype(F32))):
+        error = slotted(spread(3, k))
+        taken = error > 0.0
+        weight = jnp.where(taken, 1.0 / jnp.where(taken, error, 1.0), 0.0)
+        place = slotted((x + 1).astype(F32)) - 1.0
+        for n, values in enumerate((weight, slotted(spread(2, k)), place)):
             row = base + n * BATCH_COUNT + k
-            out_ref[row : row + 1, :] = slotted(values) - (1.0 if n == 2 else 0.0)
+            out_ref[row : row + 1, :] = values
         meta_ref[k : k + 1, :] = slotted((cell - x * lanes).astype(F32))
 
     level = iota((8, lanes), 0)
@@ -493,11 +498,14 @@
             spread_ref[pl.ds(m * height, height), :] = value.astype(BF16)
 
 
+def stacked(scaled):
+    devices = scaled.shape[0]
+    copies = max(3, LANES // devices)
+    return jnp.concatenate([scaled] * 3 + [jnp.zeros_like(scaled)] * (copies - 3), axis=0)
+
+
 def copies_of(levels):
-    devices = levels.shape[0]
-    copies = max(3, LANES // devices)
-    scaled = (levels * 0.125).astype(BF16)
-    return jnp.concatenate([scaled] * 3 + [jnp.zeros_like(scaled)] * (copies - 3), axis=0)
+    return stacked((levels * 0.125).astype(BF16))
 
 
 def solve_sums(bands, ncol):
@@ -532,16 +540,24 @@
                 columns[t] = jnp.where(row == k, part, columns[t] - column * part)
     gain = a[members : members + 1, :] * (1.0 / (members - 1))
     out = jnp.where(lane1 < members, -0.5 * a[0:members, :] + gain, 0.0)
-    return jnp.where(lane1 == members, 1.0 / (members - 1), out)
-
-
-def product3(left, right):
-    lhi, llo, _ = split3(left)
-    rhi, rlo, _ = split3(right)
+    out = jnp.where(lane1 == members, 1.0 / (members - 1), out)
+    hi, lo, _ = split3(out)
+    deep = height + 8
+    stack = jnp.concatenate(
+        [hi[:, 0:deep], hi[:, 0:deep], lo[:, 0:deep], jnp.zeros((members, 2 * lanes - 3 * deep), F32)],
+        axis=1,
+    )
+    return stack.astype(BF16)
+
+
+def product3(stack, right):
+    height, width = right.shape
+    hi, lo, _ = split3(right)
+    zero = jnp.zeros((8, width), F32)
+    hi, lo = (jnp.concatenate([part, zero], axis=0).astype(BF16) for part in (hi, lo))
+    deep = 3 * (height + 8)
     return jnp.dot(
-        jnp.concatenate([lhi, lhi, llo], axis=1).astype(BF16),
-        jnp.concatenate([rhi, rlo, rhi], axis=0).astype(BF16),
-        preferred_element_type=F32,
+        stack[:, 0:deep], jnp.concatenate([hi, lo, hi], axis=0), preferred_element_type=F32
     )
 
 
@@ -554,35 +570,33 @@
     return total
 
 
-def levels_at(rows, batch, devices, place):
-    lanes = LANES
-    hot = (iota((lanes, lanes), 0) == place.astype(jnp.int32)).astype(BF16)
-    table = rows[batch * devices : (batch + 1) * devices, :].astype(BF16)
-    return jnp.dot(table, hot, preferred_element_type=F32)
-
-
-def moved(strides, me, record_ref, seen, spread, solved, batch, target, devices, read):
-    ncol = 2 * seen[0].shape[0]
-    members = solved.shape[0]
-    height = members + 8
-    place = BATCH_COUNT * members + 2 * BATCH_COUNT + target
+def levels_kernel(strides, me_ref, record_ref, low_ref, high_ref, *out_refs):
+    seen = (low_ref, high_ref)
+    ncol, height, lanes = record_ref.shape
+    devices = (height - FIELDS * BATCH_COUNT) // BATCH_COUNT
+    members = (low_ref.shape[1] - FIELDS * BATCH_COUNT) // BATCH_COUNT
+    base = BATCH_COUNT * members + 2 * BATCH_COUNT
+    for p in range(ncol):
+        offset = sum(((p >> bit) & 1) * stride for bit, stride in enumerate(strides))
+        rows = record_ref.at[jnp.bitwise_xor(me_ref[1], offset)]
+        at = 0
+        for target in range(1, BATCH_COUNT):
+            place = seen_rows(seen, p)[base + target : base + target + 1, :]
+            hot = (iota((lanes, lanes), 0) == place.astype(jnp.int32)).astype(BF16)
+            table = (rows[0 : target * devices, :] * 0.125).astype(BF16)
+            found = jnp.dot(table, hot, preferred_element_type=F32)
+            for batch in range(target):
+                part = found[batch * devices : (batch + 1) * devices, :].astype(BF16)
+                out_refs[at][p // 2, :, (p % 2) * lanes : (p % 2 + 1) * lanes] = stacked(part)
+                at += 1
+
+
+def moved(levels_ref, spread, solved, read):
     out = []
-    for p in range(0, ncol, 2):
-        pair = (p, p + 1)
-        levels = []
-        for i in pair:
-            offset = sum(((i >> bit) & 1) * stride for bit, stride in enumerate(strides))
-            levels.append(
-                copies_of(
-                    levels_at(
-                        record_ref.at[jnp.bitwise_xor(me, offset)], batch, devices,
-                        seen_rows(seen, i)[place : place + 1, :],
-                    )
-                )
-            )
-        z = jnp.concatenate([read(i) for i in pair], axis=1)
-        sums = apply_sums(spread, jnp.concatenate(levels, axis=1), z, height)
-        z = z + product3(solved[:, 0:height], sums)
+    for p in range(levels_ref.shape[0]):
+        z = jnp.concatenate([read(2 * p), read(2 * p + 1)], axis=1)
+        sums = apply_sums(spread, levels_ref[p], z, z.shape[0] + 8)
+        z = z + product3(solved, sums)
         out += [z[:, 0:LANES], z[:, LANES:]]
     return out
 
@@ -593,23 +607,19 @@
     return lambda i: seen_rows(seen, i)[target * members : (target + 1) * members, :]
 
 
-def next_kernel(strides, row_strides, batch, *refs):
-    me_ref, lows_ref, highs_ref, record_ref = refs[:4]
+def next_kernel(row_strides, batch, *refs):
+    me_ref, lows_ref, highs_ref, levels_ref = refs[:4]
     seen = refs[4:6]
     z_ref = refs[6] if batch else None
     out_ref, spread_ref, solved_ref = refs[-3:]
     ncol = 2 * seen[0].shape[0]
     members = solved_ref.shape[0]
-    devices = 2 * ncol * lows_ref.shape[0]
     bands = bands_of(row_strides, me_ref[0], lows_ref, highs_ref)
     spread_sums(bands, spread_ref, ncol)
     solved = solve_sums(bands, ncol)
     solved_ref[...] = solved
     target = batch + 1
-    zs = moved(
-        strides, me_ref[1], record_ref, seen, spread_ref[...], solved, batch, target, devices,
-        reader(seen, z_ref, members, target),
-    )
+    zs = moved(levels_ref, spread_ref[...], solved, reader(seen, z_ref, members, target))
     parts = []
     meta = BATCH_COUNT * members + target
     for p in range(ncol):
@@ -624,22 +634,11 @@
     out_ref[...] = band_sums(ncol, parts)
 
 
-def moved_kernel(strides, batches, target, *refs):
-    me_ref, record_ref = refs[:2]
-    seen = refs[2:4]
-    given = refs[4 : 4 + 2 * len(batches)]
-    z_ref = refs[4 + 2 * len(batches)] if len(refs) == 6 + 2 * len(batches) else None
+def moved_kernel(target, levels_ref, spread_ref, solved_ref, *refs):
     out_ref = refs[-1]
-    members = given[1].shape[0]
-    devices = (record_ref.shape[1] - FIELDS * BATCH_COUNT) // BATCH_COUNT
-    read = reader(seen, z_ref, members, target)
-    for n, batch in enumerate(batches):
-        zs = moved(
-            strides, me_ref[1], record_ref, seen, given[2 * n][...], given[2 * n + 1][...],
-            batch, target, devices, read,
-        )
-        read = zs.__getitem__
-    for p, z in enumerate(zs):
+    z_ref = refs[0] if len(refs) == 2 else None
+    read = reader(refs[0:2], z_ref, solved_ref.shape[0], target)
+    for p, z in enumerate(moved(levels_ref, spread_ref[...], solved_ref[...], read)):
         out_ref[p] = z
 
 
@@ -647,7 +646,6 @@
     members = solved.shape[0]
     at = jnp.dot(spread, levels, preferred_element_type=F32)
     lanes = LANES
-    gain = solved[:, 0:height]
     for j in range(0, members, 2):
         sums = []
         for i in (j, j + 1):
@@ -659,7 +657,7 @@
                     term = at[m * height : (m + 1) * height, :] * trans_ref[i, m : m + 1, :]
                     total = term if total is None else total + term
                 sums.append(total)
-        change = product3(gain, jnp.concatenate(sums, axis=1))
+        change = product3(solved, jnp.concatenate(sums, axis=1))
         for n, i in enumerate((j, j + 1)):
             part = change[:, n * lanes : (n + 1) * lanes]
             if batch == 0:
@@ -695,8 +693,8 @@
 
 
 def final_kernel(
-    row_strides, me_ref, lows_ref, highs_ref, record_ref, trans_ref, state_ref, out_ref,
-    spread_ref, whole_ref, turned_ref,
+    row_strides, me_ref, lows_ref, highs_ref, record_ref, trans_ref, state_ref, out_hbm,
+    spread_ref, whole_ref, turned_ref, out_ref, sems,
 ):
     rows, lanes = state_ref.shape[0], state_ref.shape[2]
     members = state_ref.shape[1] // 2
@@ -711,18 +709,32 @@
     compose(spread_ref[...], solved, levels, batch, trans_ref, whole_ref, height)
     for i in range(members):
         hi, lo, _ = split3(whole_ref[:, i, :])
-        turned_ref[:, i, :] = jnp.concatenate([hi, hi, lo, jnp.zeros_like(hi)], axis=0).T
-
-    @pl.loop(0, rows // 8)
-    def _(b):
-        start = pl.multiple_of(b * 8, 8)
-        done = []
-        for i in range(8):
-            both = state_ref[start + i]
-            right = jnp.concatenate([both, both[0:members]], axis=0)
-            left = turned_ref[start + i][:, 0 : 3 * members].astype(BF16)
-            done.append(jnp.dot(left, right, preferred_element_type=F32))
-        out_ref[:, pl.ds(start, 8), :] = jnp.swapaxes(jnp.stack(done), 0, 1)
+        turned_ref[i] = jnp.concatenate([hi, hi, lo, jnp.zeros_like(hi)], axis=0).T
+
+    share = rows // sems.shape[0]
+    copies = []
+    for c in range(sems.shape[0]):
+
+        @pl.loop(c * share // 8, (c + 1) * share // 8)
+        def _(b):
+            start = pl.multiple_of(b * 8, 8)
+            lefts = jnp.swapaxes(turned_ref[:, pl.ds(start, 8), :], 0, 1).astype(BF16)
+            done = []
+            for i in range(8):
+                both = state_ref[start + i]
+                right = jnp.concatenate([both, both[0:members]], axis=0)
+                done.append(
+                    jnp.dot(lefts[i][:, 0 : 3 * members], right, preferred_element_type=F32)
+                )
+            out_ref[:, pl.ds(start, 8), :] = jnp.swapaxes(jnp.stack(done), 0, 1)
+
+        part = pl.ds(c * share, share)
+        copies.append(
+            pltpu.make_async_copy(out_ref.at[:, part, :], out_hbm.at[:, part, :], sems.at[c])
+        )
+        copies[-1].start()
+    for copy in copies:
+        copy.wait()
 
 
 def call(kernel, out_shape, in_specs, scratch=(), limit=48, out_specs=None):
@@ -812,7 +824,7 @@
         [SMEM, VMEM, VMEM],
         [pltpu.VMEM((8, cols), F32)],
     )(me, records, state)
-    seen = gather_over(mine, "col")
+    seen, _, _ = gather_over(mine, "col")
     parts = call(split_kernel, out(rows, 2 * members, cols, dtype=BF16), [VMEM])(state)
 
     sums = call(
@@ -828,39 +840,45 @@
             [SMEM] + [VMEM] * (len(args) - 1),
         )(*args)
 
-    def moved_of(batches, target, given, z):
-        args = (me, records, *seen, *given) + (() if z is None else (z,))
+    def moved_of(batch, target, given, z):
+        args = (levels[(batch, target)], *given) + (seen if z is None else (z,))
         return call(
-            functools.partial(moved_kernel, strides, batches, target),
+            functools.partial(moved_kernel, target),
             out(ncol, members, cols),
-            [SMEM] + [VMEM] * (len(args) - 1),
+            [VMEM] * len(args),
         )(*args)
 
     def next_of(batch, every, z):
-        args = (me, *every, records, *seen) + (() if z is None else (z,))
+        args = (me, *every, levels[(batch, batch + 1)], *seen) + (() if z is None else (z,))
         got = call(
-            functools.partial(next_kernel, strides, row_strides, batch),
+            functools.partial(next_kernel, row_strides, batch),
             (
                 out(height, members * ncol),
                 out(members * height, wide, dtype=BF16),
-                out(members, LANES),
+                out(members, 2 * LANES, dtype=BF16),
             ),
             [SMEM] + [VMEM] * (len(args) - 1),
         )(*args)
         return got[0], got[1:]
 
-    def exchange(sums, beside):
-        return gather_over(sums, "row", beside)
-
-    every, _ = exchange(sums, ())
+    pairs = [(b, k) for k in range(1, BATCH_COUNT) for b in range(k)]
+    found = call(
+        functools.partial(levels_kernel, strides),
+        tuple(out(ncol // 2, wide, 2 * LANES, dtype=BF16) for _ in pairs),
+        [SMEM] + [VMEM] * 3,
+    )(me, records, *seen)
+    every, (found, parts), _ = gather_over(sums, "row", (found, parts))
+    levels = dict(zip(pairs, found))
     sums, first = next_of(0, every, None)
-    every, (z2,) = exchange(sums, (moved_of((0,), 2, first, None),))
-    trans = compose_of((0,), first, None)
+    every, z2, trans = gather_over(
+        sums, "row", moved_of(0, 2, first, None), compose_of((0,), first, None)
+    )
     sums, second = next_of(1, every, z2)
-    every, (z3,) = exchange(sums, (moved_of((0, 1), 3, first + second, None),))
-    sums, third = next_of(2, every, z3)
-    every, (trans,) = exchange(sums, (compose_of((1,), second, trans),))
-    trans = compose_of((2,), third, trans)
+    z3 = moved_of(0, 3, first, None)
+    every, z3, z3_late = gather_over(sums, "row", z3, moved_of(1, 3, second, z3))
+    sums, third = next_of(2, every, z3_late)
+    trans = compose_of((1,), second, trans)
+    every, _, trans = gather_over(sums, "row", trans, compose_of((2,), third, trans))
     return call(
         functools.partial(final_kernel, row_strides),
         out(members, rows, cols),
@@ -868,8 +886,11 @@
         [
             pltpu.VMEM((members * height, wide), BF16),
             pltpu.VMEM((members, members, cols), F32),
-            pltpu.VMEM((rows, members, cols), F32),
+            pltpu.VMEM((members, rows, cols), F32),
+            pltpu.VMEM((members, rows, cols), F32),
+            pltpu.SemaphoreType.DMA((4,)),
         ],
+        out_specs=ANY,
     )(me, *every, records, trans, parts)
 
 

time: 124 us -> 117 us (0.944)
  Pallas kernels: 68 us -> 63.5 us
  waiting for transfers between devices: 22.4 us -> 19.3 us
    pallas_call x5 -> x7, Pallas kernels: 22.5 us -> 19.2 us  [the longest x3 12.1 us: next_of(): call(functools.partial(next_kernel, row_strides, batch), (out(height, mem...]
    ppermute x11, waiting for transfers between devices: 18.8 us -> 15.6 us  [gather_over(): other = lax.ppermute(held, axis, [(i, i ^ stride) for i in range(n)])]
  transfers between devices with their start and end apart: 16 -> 16, of which waited for: 8 -> 9; matrix products, arithmetic and copies ran while one was open for 2% -> 2% of each run, Pallas kernels for 28% -> 29%
where the time goes in v2:
time: 117 us
  Pallas kernels  63.5 us (54%)
  starting transfers between devices  29.3 us (25%)
  waiting for transfers between devices  19.3 us (16%)
  local copies, waits for them, and re-layouts  4.33 us (4%)
    pallas_call x1, Pallas kernels, body(): call(forecast_kernel, out(members, rows, cols), [VMEM] * 6, [pltpu.VMEM((...  19.3 us
    ppermute x11, waiting for transfers between devices, gather_over(): other = lax.ppermute(held, axis, [(i, i ^ stride) for i in range(n)])  15.6 us
    ppermute x11, starting transfers between devices, gather_over(): other = lax.ppermute(held, axis, [(i, i ^ stride) for i in range(n)])  13.5 us
    pallas_call x3, Pallas kernels, next_of(): call(functools.partial(next_kernel, row_strides, batch), (out(height, mem...  12.1 us
    pallas_call x1, Pallas kernels, body(): call(functools.partial(final_kernel, row_strides), out(members, rows, col...  9.36 us
    all_to_all x1, starting transfers between devices, body(): lax.all_to_all(jnp.broadcast_to(record, (ncol, *record.shape)), 'col', sp...  6.96 us
    ppermute x2, starting transfers between devices, shift_pair(): lax.ppermute(high_send, axis, forward)  6.31 us
    pallas_call x3, Pallas kernels, compose_of(): call(functools.partial(compose_kernel, batches), out(members, members, co...  6.28 us
  transfers between devices with their start and end apart: 16, of which 9 were waited for; matrix products, arithmetic and copies ran while one was open for 2% of the time, Pallas kernels for 29%

profile of v2, /device:TPU:0, one launch (start us, length us, event | category | flops | bytes accessed | tf_op | source)
XLA Modules:
  0.0 117.0 jit_solution(17807859439505565265)
XLA Ops:
  0.0 3.3 %shard_map.91 = (f32[3,128,128]{2,1,0:T(8,128)}, f32[3,128,128]{2,1,0:T(8,128)}, f32[144,128]{1,0:T(8,128)}, f32[2,128,128]{2,1,0:T(8,128)}) custom-call(f32[32,128,128]{2,1,0:T(8,128)} %h_ref.1, s32[128,128]{1,0:T(8,128)} %depth_hbm.1, s32[128,128]{1,0:T(8,128)} %sea_hbm.1, s32[4,32,128]{2,1,0:T(8,128)} %bitcast.22, s32[4,64]{1,0:T(4,128)} %bitcast.23, ...), custom_call_target="tpu_custom_call" | custom-call | tf_op jit(solution)/shard_map/pallas_call | solution.py:769
  3.3 5.0 %collective-permute-start = (f32[3,128,128]{2,1,0:T(8,128)}, f32[3,128,128]{2,1,0:T(8,128)S(1)}, u32[]{:S(2)}, u32[]{:S(2)}) collective-permute-start(f32[3,128,128]{2,1,0:T(8,128)} %get-tuple-element.44), channel_id=1, source_target_pairs={{0,1},{1,2},{2,3},{3,4},{4,5},{5,6},{6,7},{8,9},{9,10},{10,11},{11... | collective-permute-start | bytes 589832 | tf_op jit(solution)/shard_map/ppermute | solution.py:69
  9.7 1.7 %broadcast_in_dim.18 = f32[8,144,128]{2,1,0:T(8,128)} broadcast(f32[144,128]{1,0:T(8,128)} %get-tuple-element.42), dimensions={1,2} | broadcast | bytes 663552 | tf_op jit(solution)/shard_map/broadcast_in_dim | solution.py:798
  11.4 7.0 %all-to-all-start = ((f32[8,144,128]{2,1,0:T(8,128)}), f32[8,144,128]{2,1,0:T(8,128)S(1)}, u32[]{:S(2)}, u32[]{:S(2)}) async-start(f32[8,144,128]{2,1,0:T(8,128)} %broadcast_in_dim.18), calls=%async_computation | async-start | bytes 1179648 | tf_op jit(solution)/shard_map/all_to_all | solution.py:797
  22.1 3.6 %collective-permute-done.3.down_ref = f32[40,8,128]{2,1,0:T(8,128)S(1)} collective-permute-done((f32[40,8,128]{2,1,0:T(8,128)S(1)}, f32[40,8,128]{2,1,0:T(8,128)S(1)}, u32[]{:S(2)}, u32[]{:S(2)}) %collective-permute-start.3) | collective-permute-done | bytes 163872 | tf_op jit(solution)/shard_map/ppermute | solution.py:69
  25.8 1.6 %copy-done = f32[32,128,128]{2,1,0:T(8,128)S(1)} copy-done((f32[32,128,128]{2,1,0:T(8,128)S(1)}, f32[32,128,128]{2,1,0:T(8,128)}, u32[]{:S(2)}) %copy-start) | copy-done | bytes 2097176
  27.4 19.3 %shard_map.92.state_ref = f32[32,128,128]{2,1,0:T(8,128)S(1)} custom-call(f32[32,128,128]{2,1,0:T(8,128)S(1)} %copy-done, f32[2,128,128]{2,1,0:T(8,128)S(1)} %copy-done.1, f32[3,128,128]{2,1,0:T(8,128)S(1)} %collective-permute-done.left_ref, f32[3,128,128]{2,1,0:T(8,128)S(1)} %collective-permute-done.1.right_ref, ...), custom_call_target="tpu_custom_call" | custom-call | tf_op jit(solution)/shard_map/pallas_call | solution.py:803
  46.7 4.4 %shard_map.93 = f32[144,128]{1,0:T(8,128)S(1)} custom-call(s32[2]{0:T(128)S(1)} %pad_add_fusion.me_ref.refs_0_, f32[8,144,128]{2,1,0:T(8,128)S(1)} %all-to-all-done.record_ref, f32[32,128,128]{2,1,0:T(8,128)S(1)} %shard_map.92.state_ref), custom_call_target="tpu_custom_call" | custom-call | tf_op jit(solution)/shard_map/pallas_call | solution.py:821
  51.1 3.0 %collective-permute-start.4 = (f32[1,144,128]{2,1,0:T(8,128)S(1)}, f32[1,144,128]{2,1,0:T(8,128)S(1)}, u32[]{:S(2)}, u32[]{:S(2)}) collective-permute-start(f32[1,144,128]{2,1,0:T(8,128)S(1)} %bitcast.11), channel_id=1, source_target_pairs={{0,4},{1,5},{2,6},{3,7},{4,0},{5,1},{6,2},{7,3},{8,12},{9,13},{10,... | collective-permute-start | bytes 221192 | tf_op jit(solution)/shard_map/ppermute | solution.py:58
  54.1 2.3 %collective-permute-done.4 = f32[1,144,128]{2,1,0:T(8,128)S(1)} collective-permute-done((f32[1,144,128]{2,1,0:T(8,128)S(1)}, f32[1,144,128]{2,1,0:T(8,128)S(1)}, u32[]{:S(2)}, u32[]{:S(2)}) %collective-permute-start.4) | collective-permute-done | bytes 73760 | tf_op jit(solution)/shard_map/ppermute | solution.py:58
  56.5 2.1 %collective-permute-start.5 = (f32[2,144,128]{2,1,0:T(8,128)S(1)}, f32[2,144,128]{2,1,0:T(8,128)S(1)}, u32[]{:S(2)}, u32[]{:S(2)}) collective-permute-start(f32[2,144,128]{2,1,0:T(8,128)S(1)} %pad_maximum_fusion.3), channel_id=1, source_target_pairs={{0,2},{1,3},{2,0},{3,1},{4,6},{5,7},{6,4},{7,5},{8,10},{9,11},{10,... | collective-permute-start | bytes 442376 | tf_op jit(solution)/shard_map/ppermute | solution.py:58
  58.6 3.1 %collective-permute-done.5 = f32[2,144,128]{2,1,0:T(8,128)S(1)} collective-permute-done((f32[2,144,128]{2,1,0:T(8,128)S(1)}, f32[2,144,128]{2,1,0:T(8,128)S(1)}, u32[]{:S(2)}, u32[]{:S(2)}) %collective-permute-start.5) | collective-permute-done | bytes 147488 | tf_op jit(solution)/shard_map/ppermute | solution.py:58
  61.7 2.1 %collective-permute-start.6 = (f32[4,144,128]{2,1,0:T(8,128)S(1)}, f32[4,144,128]{2,1,0:T(8,128)S(1)}, u32[]{:S(2)}, u32[]{:S(2)}) collective-permute-start(f32[4,144,128]{2,1,0:T(8,128)S(1)} %pad_maximum_fusion.low_ref.refs_4_.refs_0_), channel_id=1, source_target_pairs={{0,1},{1,0},{2,3},{3,2},{4,5},{5,4},{6,7},{7,6},{8,9},{9,8},{10,11... | collective-permute-start | bytes 884744 | tf_op jit(solution)/shard_map/ppermute | solution.py:58
  63.8 6.9 %collective-permute-done.6.high_ref.refs_5_.refs_1_ = f32[4,144,128]{2,1,0:T(8,128)S(1)} collective-permute-done((f32[4,144,128]{2,1,0:T(8,128)S(1)}, f32[4,144,128]{2,1,0:T(8,128)S(1)}, u32[]{:S(2)}, u32[]{:S(2)}) %collective-permute-start.6) | collective-permute-done | bytes 294944 | tf_op jit(solution)/shard_map/ppermute | solution.py:58
  71.3 1.8 %collective-permute-start.7 = (f32[1,40,256]{2,1,0:T(8,128)S(1)}, f32[1,40,256]{2,1,0:T(8,128)S(1)}, u32[]{:S(2)}, u32[]{:S(2)}) collective-permute-start(f32[1,40,256]{2,1,0:T(8,128)S(1)} %bitcast.14), channel_id=1, source_target_pairs={{0,16},{8,24},{16,0},{24,8},{1,17},{9,25},{17,1},{25,9},{2,18},{10... | collective-permute-start | bytes 122888 | tf_op jit(solution)/shard_map/ppermute | solution.py:58
  76.9 3.9 %shard_map.97 = (f32[40,256]{1,0:T(8,128)S(1)}, bf16[1280,128]{1,0:T(8,128)(2,1)S(1)}, bf16[32,256]{1,0:T(8,128)(2,1)S(1)}) custom-call(s32[2]{0:T(128)S(1)} %pad_add_fusion.me_ref.refs_0_, f32[2,40,256]{2,1,0:T(8,128)S(1)} %pad_maximum_fusion.4.refs_1_, f32[2,40,256]{2,1,0:T(8,128)S(1)} %collective-permute-done.8.refs_2_, ...), custom_call_target="tpu_custom_call" | custom-call | tf_op jit(solution)/shard_map/pallas_call | solution.py:853
  82.3 2.1 %shard_map.98.refs_6_ = f32[8,32,128]{2,1,0:T(8,128)S(1)} custom-call(bf16[4,128,256]{2,1,0:T(8,128)(2,1)S(1)} %get-tuple-element.55.levels_ref, bf16[1280,128]{1,0:T(8,128)(2,1)S(1)} %get-tuple-element.56.spread_ref.refs_0_, bf16[32,256]{1,0:T(8,128)(2,1)S(1)} %get-tuple-element.57.solved_ref.refs_1_, ...), custom_call_target="tpu_custom_call" | custom-call | tf_op jit(solution)/shard_map/pallas_call | solution.py:845
  86.2 4.0 %shard_map.100 = (f32[40,256]{1,0:T(8,128)S(1)}, bf16[1280,128]{1,0:T(8,128)(2,1)S(1)}, bf16[32,256]{1,0:T(8,128)(2,1)S(1)}) custom-call(s32[2]{0:T(128)S(1)} %pad_add_fusion.me_ref.refs_0_, f32[2,40,256]{2,1,0:T(8,128)S(1)} %pad_maximum_fusion.5.refs_1_, f32[2,40,256]{2,1,0:T(8,128)S(1)} %collective-permute-done.10.refs_2_, ...), custom_call_target="tpu_custom_call" | custom-call | tf_op jit(solution)/shard_map/pallas_call | solution.py:853
  91.6 2.1 %shard_map.101.refs_0_ = f32[8,32,128]{2,1,0:T(8,128)S(1)} custom-call(bf16[4,128,256]{2,1,0:T(8,128)(2,1)S(1)} %get-tuple-element.63.levels_ref, bf16[1280,128]{1,0:T(8,128)(2,1)S(1)} %get-tuple-element.56.spread_ref.refs_0_, bf16[32,256]{1,0:T(8,128)(2,1)S(1)} %get-tuple-element.57.solved_ref.refs_1_, ...), custom_call_target="tpu_custom_call" | custom-call | tf_op jit(solution)/shard_map/pallas_call | solution.py:845
  94.2 2.1 %shard_map.102.refs_6_ = f32[8,32,128]{2,1,0:T(8,128)S(1)} custom-call(bf16[4,128,256]{2,1,0:T(8,128)(2,1)S(1)} %get-tuple-element.65.levels_ref, bf16[1280,128]{1,0:T(8,128)(2,1)S(1)} %get-tuple-element.66.spread_ref.refs_0_, bf16[32,256]{1,0:T(8,128)(2,1)S(1)} %get-tuple-element.67.solved_ref.refs_1_, f32[8,32,128]{2,1,0:T(8,128)S(1)} %shard_map.101.refs_0_), custom_call_target="tpu_custom_call" | custom-call | tf_op jit(solution)/shard_map/pallas_call | solution.py:845
  96.3 4.2 %shard_map.103 = (f32[40,256]{1,0:T(8,128)S(1)}, bf16[1280,128]{1,0:T(8,128)(2,1)S(1)}, bf16[32,256]{1,0:T(8,128)(2,1)S(1)}) custom-call(s32[2]{0:T(128)S(1)} %pad_add_fusion.me_ref.refs_0_, f32[2,40,256]{2,1,0:T(8,128)S(1)} %pad_maximum_fusion.6.refs_1_, f32[2,40,256]{2,1,0:T(8,128)S(1)} %collective-permute-done.12.refs_2_, ...), custom_call_target="tpu_custom_call" | custom-call | tf_op jit(solution)/shard_map/pallas_call | solution.py:853
  101.9 2.6 %shard_map.104.refs_2_ = f32[32,32,128]{2,1,0:T(8,128)S(1)} custom-call(s32[2]{0:T(128)S(1)} %pad_add_fusion.me_ref.refs_0_, f32[8,144,128]{2,1,0:T(8,128)S(1)} %all-to-all-done.record_ref, bf16[1280,128]{1,0:T(8,128)(2,1)S(1)} %get-tuple-element.66.spread_ref.refs_0_, bf16[32,256]{1,0:T(8,128)(2,1)S(1)} %get-tuple-element.67.solved_ref.refs_1_, ...), custom_call_target="tpu_custom_call" | custom-call | tf_op jit(solution)/shard_map/pallas_call | solution.py:837
  104.8 2.6 %shard_map.105.trans_ref = f32[32,32,128]{2,1,0:T(8,128)S(1)} custom-call(s32[2]{0:T(128)S(1)} %pad_add_fusion.me_ref.refs_0_, f32[8,144,128]{2,1,0:T(8,128)S(1)} %all-to-all-done.record_ref, bf16[1280,128]{1,0:T(8,128)(2,1)S(1)} %get-tuple-element.74.refs_0_, bf16[32,256]{1,0:T(8,128)(2,1)S(1)} %get-tuple-element.75.refs_1_, ...), custom_call_target="tpu_custom_call" | custom-call | tf_op jit(solution)/shard_map/pallas_call | solution.py:837
  107.4 9.4 %shard_map.106 = f32[32,128,128]{2,1,0:T(8,128)} custom-call(s32[2]{0:T(128)S(1)} %pad_add_fusion.me_ref.refs_0_, f32[2,40,256]{2,1,0:T(8,128)S(1)} %pad_maximum_fusion.7.lows_ref, f32[2,40,256]{2,1,0:T(8,128)S(1)} %collective-permute-done.14.highs_ref, f32[8,144,128]{2,1,0:T(8,128)S(1)} %all-to-all-done.record_ref, ...), custom_call_target="tpu_custom_call" | custom-call | tf_op jit(solution)/shard_map/pallas_call | solution.py:882
  (42 shorter events, 16.5 us)
Async XLA Ops:
  3.3 16.0 %copy-start.1 = (f32[2,128,128]{2,1,0:T(8,128)S(1)}, f32[2,128,128]{2,1,0:T(8,128)}, u32[]{:S(2)}) copy-start(f32[2,128,128]{2,1,0:T(8,128)} %get-tuple-element.43.coef_ref) | copy-start | bytes 393220
  3.3 16.0 %collective-permute-start = (f32[3,128,128]{2,1,0:T(8,128)}, f32[3,128,128]{2,1,0:T(8,128)S(1)}, u32[]{:S(2)}, u32[]{:S(2)}) collective-permute-start(f32[3,128,128]{2,1,0:T(8,128)} %get-tuple-element.44), channel_id=1, source_target_pairs={{0,1},{1,2},{2,3},{3,4},{4,5},{5,6},{6,7},{8,9},{9,10},{10,11},{11... | collective-permute-start | bytes 589832 | tf_op jit(solution)/shard_map/ppermute | solution.py:69
  8.4 11.0 %collective-permute-start.1 = (f32[3,128,128]{2,1,0:T(8,128)}, f32[3,128,128]{2,1,0:T(8,128)S(1)}, u32[]{:S(2)}, u32[]{:S(2)}) collective-permute-start(f32[3,128,128]{2,1,0:T(8,128)} %get-tuple-element.45), channel_id=1, source_target_pairs={{1,0},{2,1},{3,2},{4,3},{5,4},{6,5},{7,6},{9,8},{10,9},{11,10},{12... | collective-permute-start | bytes 589832 | tf_op jit(solution)/shard_map/ppermute | solution.py:69
  11.4 35.3 %all-to-all-start = ((f32[8,144,128]{2,1,0:T(8,128)}), f32[8,144,128]{2,1,0:T(8,128)S(1)}, u32[]{:S(2)}, u32[]{:S(2)}) async-start(f32[8,144,128]{2,1,0:T(8,128)} %broadcast_in_dim.18), calls=%async_computation | async-start | bytes 1179648 | tf_op jit(solution)/shard_map/all_to_all | solution.py:797
  19.4 2.7 %collective-permute-start.2 = (f32[40,8,128]{2,1,0:T(8,128)S(1)}, f32[40,8,128]{2,1,0:T(8,128)S(1)}, u32[]{:S(2)}, u32[]{:S(2)}) collective-permute-start(f32[40,8,128]{2,1,0:T(8,128)S(1)} %pad_maximum_fusion.1), channel_id=1, source_target_pairs={{0,8},{8,16},{16,24},{1,9},{9,17},{17,25},{2,10},{10,18},{18,26},{... | collective-permute-start | bytes 491528 | tf_op jit(solution)/shard_map/ppermute | solution.py:69
  20.8 5.0 %collective-permute-start.3 = (f32[40,8,128]{2,1,0:T(8,128)S(1)}, f32[40,8,128]{2,1,0:T(8,128)S(1)}, u32[]{:S(2)}, u32[]{:S(2)}) collective-permute-start(f32[40,8,128]{2,1,0:T(8,128)S(1)} %pad_maximum_fusion.2), channel_id=1, source_target_pairs={{8,0},{16,8},{24,16},{9,1},{17,9},{25,17},{10,2},{18,10},{26,18},{... | collective-permute-start | bytes 491528 | tf_op jit(solution)/shard_map/ppermute | solution.py:69
  25.8 1.6 %copy-start = (f32[32,128,128]{2,1,0:T(8,128)S(1)}, f32[32,128,128]{2,1,0:T(8,128)}, u32[]{:S(2)}) copy-start(f32[32,128,128]{2,1,0:T(8,128)} %h_ref.1) | copy-start | bytes 6291460
  51.1 5.3 %collective-permute-start.4 = (f32[1,144,128]{2,1,0:T(8,128)S(1)}, f32[1,144,128]{2,1,0:T(8,128)S(1)}, u32[]{:S(2)}, u32[]{:S(2)}) collective-permute-start(f32[1,144,128]{2,1,0:T(8,128)S(1)} %bitcast.11), channel_id=1, source_target_pairs={{0,4},{1,5},{2,6},{3,7},{4,0},{5,1},{6,2},{7,3},{8,12},{9,13},{10,... | collective-permute-start | bytes 221192 | tf_op jit(solution)/shard_map/ppermute | solution.py:58
  56.5 5.2 %collective-permute-start.5 = (f32[2,144,128]{2,1,0:T(8,128)S(1)}, f32[2,144,128]{2,1,0:T(8,128)S(1)}, u32[]{:S(2)}, u32[]{:S(2)}) collective-permute-start(f32[2,144,128]{2,1,0:T(8,128)S(1)} %pad_maximum_fusion.3), channel_id=1, source_target_pairs={{0,2},{1,3},{2,0},{3,1},{4,6},{5,7},{6,4},{7,5},{8,10},{9,11},{10,... | collective-permute-start | bytes 442376 | tf_op jit(solution)/shard_map/ppermute | solution.py:58
  61.7 8.9 %collective-permute-start.6 = (f32[4,144,128]{2,1,0:T(8,128)S(1)}, f32[4,144,128]{2,1,0:T(8,128)S(1)}, u32[]{:S(2)}, u32[]{:S(2)}) collective-permute-start(f32[4,144,128]{2,1,0:T(8,128)S(1)} %pad_maximum_fusion.low_ref.refs_4_.refs_0_), channel_id=1, source_target_pairs={{0,1},{1,0},{2,3},{3,2},{4,5},{5,4},{6,7},{7,6},{8,9},{9,8},{10,11... | collective-permute-start | bytes 884744 | tf_op jit(solution)/shard_map/ppermute | solution.py:58
  71.3 4.4 %collective-permute-start.7 = (f32[1,40,256]{2,1,0:T(8,128)S(1)}, f32[1,40,256]{2,1,0:T(8,128)S(1)}, u32[]{:S(2)}, u32[]{:S(2)}) collective-permute-start(f32[1,40,256]{2,1,0:T(8,128)S(1)} %bitcast.14), channel_id=1, source_target_pairs={{0,16},{8,24},{16,0},{24,8},{1,17},{9,25},{17,1},{25,9},{2,18},{10... | collective-permute-start | bytes 122888 | tf_op jit(solution)/shard_map/ppermute | solution.py:58
  75.6 1.3 %collective-permute-start.8 = (f32[2,40,256]{2,1,0:T(8,128)S(1)}, f32[2,40,256]{2,1,0:T(8,128)S(1)}, u32[]{:S(2)}, u32[]{:S(2)}) collective-permute-start(f32[2,40,256]{2,1,0:T(8,128)S(1)} %pad_maximum_fusion.4.refs_1_), channel_id=1, source_target_pairs={{0,8},{8,0},{16,24},{24,16},{1,9},{9,1},{17,25},{25,17},{2,10},{10... | collective-permute-start | bytes 245768 | tf_op jit(solution)/shard_map/ppermute | solution.py:58
  80.9 4.0 %collective-permute-start.9 = (f32[1,40,256]{2,1,0:T(8,128)S(1)}, f32[1,40,256]{2,1,0:T(8,128)S(1)}, u32[]{:S(2)}, u32[]{:S(2)}) collective-permute-start(f32[1,40,256]{2,1,0:T(8,128)S(1)} %bitcast.20), channel_id=1, source_target_pairs={{0,16},{8,24},{16,0},{24,8},{1,17},{9,25},{17,1},{25,9},{2,18},{10... | collective-permute-start | bytes 122888 | tf_op jit(solution)/shard_map/ppermute | solution.py:58
  84.9 1.3 %collective-permute-start.10 = (f32[2,40,256]{2,1,0:T(8,128)S(1)}, f32[2,40,256]{2,1,0:T(8,128)S(1)}, u32[]{:S(2)}, u32[]{:S(2)}) collective-permute-start(f32[2,40,256]{2,1,0:T(8,128)S(1)} %pad_maximum_fusion.5.refs_1_), channel_id=1, source_target_pairs={{0,8},{8,0},{16,24},{24,16},{1,9},{9,1},{17,25},{25,17},{2,10},{10... | collective-permute-start | bytes 245768 | tf_op jit(solution)/shard_map/ppermute | solution.py:58
  90.1 4.0 %collective-permute-start.11 = (f32[1,40,256]{2,1,0:T(8,128)S(1)}, f32[1,40,256]{2,1,0:T(8,128)S(1)}, u32[]{:S(2)}, u32[]{:S(2)}) collective-permute-start(f32[1,40,256]{2,1,0:T(8,128)S(1)} %bitcast.18), channel_id=1, source_target_pairs={{0,16},{8,24},{16,0},{24,8},{1,17},{9,25},{17,1},{25,9},{2,18},{10... | collective-permute-start | bytes 122888 | tf_op jit(solution)/shard_map/ppermute | solution.py:58
  94.2 2.1 %collective-permute-start.12 = (f32[2,40,256]{2,1,0:T(8,128)S(1)}, f32[2,40,256]{2,1,0:T(8,128)S(1)}, u32[]{:S(2)}, u32[]{:S(2)}) collective-permute-start(f32[2,40,256]{2,1,0:T(8,128)S(1)} %pad_maximum_fusion.6.refs_1_), channel_id=1, source_target_pairs={{0,8},{8,0},{16,24},{24,16},{1,9},{9,1},{17,25},{25,17},{2,10},{10... | collective-permute-start | bytes 245768 | tf_op jit(solution)/shard_map/ppermute | solution.py:58
  100.5 4.0 %collective-permute-start.13 = (f32[1,40,256]{2,1,0:T(8,128)S(1)}, f32[1,40,256]{2,1,0:T(8,128)S(1)}, u32[]{:S(2)}, u32[]{:S(2)}) collective-permute-start(f32[1,40,256]{2,1,0:T(8,128)S(1)} %bitcast.16), channel_id=1, source_target_pairs={{0,16},{8,24},{16,0},{24,8},{1,17},{9,25},{17,1},{25,9},{2,18},{10... | collective-permute-start | bytes 122888 | tf_op jit(solution)/shard_map/ppermute | solution.py:58
  104.5 2.9 %collective-permute-start.14 = (f32[2,40,256]{2,1,0:T(8,128)S(1)}, f32[2,40,256]{2,1,0:T(8,128)S(1)}, u32[]{:S(2)}, u32[]{:S(2)}) collective-permute-start(f32[2,40,256]{2,1,0:T(8,128)S(1)} %pad_maximum_fusion.7.lows_ref), channel_id=1, source_target_pairs={{0,8},{8,0},{16,24},{24,16},{1,9},{9,1},{17,25},{25,17},{2,10},{10... | collective-permute-start | bytes 245768 | tf_op jit(solution)/shard_map/ppermute | solution.py:58

commit v3 on v2

--- a/solution.py
+++ b/solution.py
@@ -154,8 +154,52 @@
         send(g, pack(lambda q: h_ref[8 * g + q]), pack(lambda q: h_ref[8 * (g + half) + q]))
 
 
+def strip_pair(pick, incoming, second):
+    values = [pick(q) for q in range(8)]
+    shape = values[0].shape
+    lanes = shape[1]
+    seg = iota(shape, 1) // SEG
+    first = iota(shape, 1) % SEG < HALO
+    own = None
+    for q in range(8):
+        rolled = pltpu.roll(values[q], q * SEG + HALO, axis=1)
+        own = rolled if own is None else jnp.where(seg == q, rolled, own)
+    from_left, from_right = incoming(0), incoming(1)
+    if second:
+        from_left = pltpu.roll(from_left, lanes - HALO, axis=1)
+        from_right = pltpu.roll(from_right, HALO, axis=1)
+    return jnp.where(first, from_left, own), jnp.where(first, own, from_right)
+
+
+def strips_kernel(h_ref, coef_ref, left_ref, right_ref, out_ref, out_k_ref, held_ref):
+    members, rows, lanes = h_ref.shape
+    groups = members // 8
+    half = groups // 2
+    block = 32
+
+    @pl.loop(0, members)
+    def _(m):
+        held_ref[m] = h_ref[m]
+
+    @pl.loop(0, rows // block)
+    def _(b):
+        here = pl.ds(pl.multiple_of(b * block, block), block)
+        for i in range(2):
+            out_k_ref[2 * i, here, :], out_k_ref[2 * i + 1, here, :] = strip_pair(
+                lambda q: coef_ref[i, here, :],
+                lambda w: (left_ref, right_ref)[w][half, here, :],
+                i == 1,
+            )
+        for g in range(groups):
+            out_ref[g, here, :], out_ref[groups + g, here, :] = strip_pair(
+                lambda q: h_ref[8 * g + q, here, :],
+                lambda w: (left_ref, right_ref)[w][g % half, here, :],
+                g >= half,
+            )
+
+
 def forecast_kernel(
-    h_ref, coef_ref, left_ref, right_ref, up_ref, down_ref, out_ref,
+    h_ref, coef_ref, own_ref, own_k_ref, up_ref, down_ref, out_ref,
     a_ref, b_ref, rhs_ref, sa_ref, sb_ref, srhs_ref, k_ref, sk_ref, w_ref, sw_ref, edge_ref,
 ):
     members, rows, lanes = out_ref.shape
@@ -182,50 +226,24 @@
         a_ref[m, pl.ds(inner, rows), :] = h_ref[m]
         a_ref[m, pl.ds(inner + rows, HALO), :] = down_ref[m]
 
-    def strips(start, first_row, at, number):
-        shape = (block, lanes)
-        seg = iota(shape, 1) // SEG
-        first = iota(shape, 1) % SEG < HALO
-
-        def incoming(which, g):
-            base = members + 2 + which * (half + 1) + g
-            ref = (left_ref, right_ref)[which]
-            parts = []
-            for s in range(start, start + block, HALO):
-                if s < HALO:
-                    parts.append(up_ref[base])
-                elif s >= rows + HALO:
-                    parts.append(down_ref[base])
-                else:
-                    parts.append(ref[g, pl.ds(s - HALO, HALO), :])
-            return jnp.concatenate(parts, axis=0)
-
-        own = None
-        for q in range(8):
-            if number:
-                value = a_ref[first_row + q, pl.ds(pad + start, block), :]
-            else:
-                value = k_ref[first_row, pl.ds(pad + start, block), :]
-            rolled = pltpu.roll(value, q * SEG + HALO, axis=1)
-            own = rolled if own is None else jnp.where(seg == q, rolled, own)
-        source = at % half if number else half
-        from_left = incoming(0, source)
-        from_right = incoming(1, source)
-        if at >= half if number else at:
-            from_left = pltpu.roll(from_left, lanes - HALO, axis=1)
-            from_right = pltpu.roll(from_right, HALO, axis=1)
-        return jnp.where(first, from_left, own), jnp.where(first, own, from_right)
-
-    for start in starts:
-        rows_here = pl.ds(pad + start, block)
+    for ref, start in ((up_ref, pad), (down_ref, inner + rows)):
+        here = pl.ds(start, HALO)
         for i in range(2):
-            lo, hi = strips(start, i, i, 0)
-            sk_ref[2 * i, rows_here, :] = lo
-            sk_ref[2 * i + 1, rows_here, :] = hi
+            sk_ref[2 * i, here, :], sk_ref[2 * i + 1, here, :] = strip_pair(
+                lambda q: ref[members + i],
+                lambda w: ref[members + 2 + w * (half + 1) + half],
+                i == 1,
+            )
         for g in range(groups):
-            lo, hi = strips(start, 8 * g, g, groups)
-            sa_ref[g, rows_here, :] = lo
-            sa_ref[groups + g, rows_here, :] = hi
+            sa_ref[g, here, :], sa_ref[groups + g, here, :] = strip_pair(
+                lambda q: ref[8 * g + q],
+                lambda w: ref[members + 2 + w * (half + 1) + g % half],
+                g >= half,
+            )
+    for i in range(4):
+        sk_ref[i, pl.ds(inner, rows), :] = own_k_ref[i]
+    for i in range(2 * groups):
+        sa_ref[i, pl.ds(inner, rows), :] = own_ref[i]
 
     lane = iota((block, lanes), 1)
     is_last = lane == lanes - 1
@@ -800,6 +818,11 @@
 
     ext = rows + 2 * HALO
     tall = ext + 2 * HALO
+    own, own_k, held = call(
+        strips_kernel,
+        (out(2 * groups, rows, cols), out(4, rows, cols), out(members, rows, cols)),
+        [VMEM] * 4,
+    )(sample_heights, coef, left, right)
     state = call(
         forecast_kernel,
         out(members, rows, cols),
@@ -817,7 +840,7 @@
             pltpu.VMEM((2, 10, ext, cols), F32),
             pltpu.VMEM((groups, ext, cols), F32),
         ],
-    )(sample_heights, coef, left, right, up, down)
+    )(held, coef, own, own_k, up, down)
     mine = call(
         functools.partial(extract_kernel, share),
         out(BATCH_COUNT * members + FIELDS * BATCH_COUNT, cols),

time: 117 us -> 116 us (level)
  local copies, waits for them, and re-layouts: 4.33 us -> 1.78 us
  waiting for transfers between devices: 19.3 us -> 17.9 us
  other arithmetic: 0.18 us -> 1.51 us
    unnamed x4, local copies, waits for them, and re-layouts: 1.6 us -> 0.01 us
    pallas_call x0 -> x1, Pallas kernels: none -> 1.37 us  [body(): call(strips_kernel, (out(2 * groups, rows, cols), out(4, rows, cols), out...]
    concatenate x2, other arithmetic: 0.03 us -> 1.36 us  [slab(): jnp.concatenate([cut(a) for a in (sample_heights, coef, left, right)], ax...]
    ppermute x2, waiting for transfers between devices: 3.63 us -> 2.45 us  [shift_pair(): lax.ppermute(low_send, axis, backward)]
  transfers between devices with their start and end apart: 16 -> 16, of which waited for: 9 -> 9; matrix products, arithmetic and copies ran while one was open for 2% -> 3% of each run, Pallas kernels for 29% -> 30%
where the time goes in v3:
time: 116 us; the launch traced here: 115 us
  Pallas kernels  64.1 us (55%)
  starting transfers between devices  29.5 us (25%)
  waiting for transfers between devices  17.9 us (15%)
  local copies, waits for them, and re-layouts  1.78 us (2%)
  other arithmetic  1.51 us (1%)
    pallas_call x1, Pallas kernels, body(): call(forecast_kernel, out(members, rows, cols), [VMEM] * 6, [pltpu.VMEM((...  18.4 us
    ppermute x11, waiting for transfers between devices, gather_over(): other = lax.ppermute(held, axis, [(i, i ^ stride) for i in range(n)])  15.5 us
    ppermute x11, starting transfers between devices, gather_over(): other = lax.ppermute(held, axis, [(i, i ^ stride) for i in range(n)])  13.7 us
    pallas_call x3, Pallas kernels, next_of(): call(functools.partial(next_kernel, row_strides, batch), (out(height, mem...  12.1 us
    pallas_call x1, Pallas kernels, body(): call(functools.partial(final_kernel, row_strides), out(members, rows, col...  9.36 us
    all_to_all x1, starting transfers between devices, body(): lax.all_to_all(jnp.broadcast_to(record, (ncol, *record.shape)), 'col', sp...  6.96 us
    ppermute x2, starting transfers between devices, shift_pair(): lax.ppermute(high_send, axis, forward)  6.3 us
    pallas_call x3, Pallas kernels, compose_of(): call(functools.partial(compose_kernel, batches), out(members, members, co...  6.28 us
  transfers between devices with their start and end apart: 16, of which 9 were waited for; matrix products, arithmetic and copies ran while one was open for 3% of the time, Pallas kernels for 30%

profile of v3, /device:TPU:0, one launch (start us, length us, event | category | flops | bytes accessed | tf_op | source)
XLA Modules:
  0.0 115.2 jit_solution(2730228412599658141)
XLA Ops:
  0.0 3.5 %shard_map.91 = (f32[3,128,128]{2,1,0:T(8,128)}, f32[3,128,128]{2,1,0:T(8,128)}, f32[144,128]{1,0:T(8,128)}, f32[2,128,128]{2,1,0:T(8,128)}) custom-call(f32[32,128,128]{2,1,0:T(8,128)} %h_ref.1, s32[128,128]{1,0:T(8,128)} %depth_hbm.1, s32[128,128]{1,0:T(8,128)} %sea_hbm.1, s32[4,32,128]{2,1,0:T(8,128)} %bitcast.22, s32[4,64]{1,0:T(4,128)} %bitcast.23, ...), custom_call_target="tpu_custom_call" | custom-call | tf_op jit(solution)/shard_map/pallas_call | solution.py:787
  3.5 5.0 %collective-permute-start = (f32[3,128,128]{2,1,0:T(8,128)}, f32[3,128,128]{2,1,0:T(8,128)S(1)}, u32[]{:S(2)}, u32[]{:S(2)}) collective-permute-start(f32[3,128,128]{2,1,0:T(8,128)} %get-tuple-element.47), channel_id=1, source_target_pairs={{0,1},{1,2},{2,3},{3,4},{4,5},{5,6},{6,7},{8,9},{9,10},{10,11},{11... | collective-permute-start | bytes 589832 | tf_op jit(solution)/shard_map/ppermute | solution.py:69
  9.8 1.7 %broadcast_in_dim.18 = f32[8,144,128]{2,1,0:T(8,128)} broadcast(f32[144,128]{1,0:T(8,128)} %get-tuple-element.45), dimensions={1,2} | broadcast | bytes 663552 | tf_op jit(solution)/shard_map/broadcast_in_dim | solution.py:816
  11.6 7.0 %all-to-all-start = ((f32[8,144,128]{2,1,0:T(8,128)}), f32[8,144,128]{2,1,0:T(8,128)S(1)}, u32[]{:S(2)}, u32[]{:S(2)}) async-start(f32[8,144,128]{2,1,0:T(8,128)} %broadcast_in_dim.18), calls=%async_computation | async-start | bytes 1179648 | tf_op jit(solution)/shard_map/all_to_all | solution.py:815
  24.0 2.4 %collective-permute-done.3.down_ref = f32[40,8,128]{2,1,0:T(8,128)S(1)} collective-permute-done((f32[40,8,128]{2,1,0:T(8,128)}, f32[40,8,128]{2,1,0:T(8,128)S(1)}, u32[]{:S(2)}, u32[]{:S(2)}) %collective-permute-start.3) | collective-permute-done | bytes 163872 | tf_op jit(solution)/shard_map/ppermute | solution.py:69
  26.5 18.4 %shard_map.93.state_ref = f32[32,128,128]{2,1,0:T(8,128)S(1)} custom-call(f32[32,128,128]{2,1,0:T(8,128)S(1)} %get-tuple-element.49.h_ref, f32[2,128,128]{2,1,0:T(8,128)S(1)} %copy-done.1, f32[8,128,128]{2,1,0:T(8,128)S(1)} %get-tuple-element.50.own_ref, f32[4,128,128]{2,1,0:T(8,128)S(1)} %get-tuple-element.51.own_k_ref, ...), custom_call_target="tpu_custom_call" | custom-call | tf_op jit(solution)/shard_map/pallas_call | solution.py:826
  44.9 4.4 %shard_map.94 = f32[144,128]{1,0:T(8,128)S(1)} custom-call(s32[2]{0:T(128)S(1)} %pad_add_fusion.me_ref.refs_0_, f32[8,144,128]{2,1,0:T(8,128)S(1)} %all-to-all-done.record_ref, f32[32,128,128]{2,1,0:T(8,128)S(1)} %shard_map.93.state_ref), custom_call_target="tpu_custom_call" | custom-call | tf_op jit(solution)/shard_map/pallas_call | solution.py:844
  49.3 3.0 %collective-permute-start.4 = (f32[1,144,128]{2,1,0:T(8,128)S(1)}, f32[1,144,128]{2,1,0:T(8,128)S(1)}, u32[]{:S(2)}, u32[]{:S(2)}) collective-permute-start(f32[1,144,128]{2,1,0:T(8,128)S(1)} %bitcast.11), channel_id=1, source_target_pairs={{0,4},{1,5},{2,6},{3,7},{4,0},{5,1},{6,2},{7,3},{8,12},{9,13},{10,... | collective-permute-start | bytes 221192 | tf_op jit(solution)/shard_map/ppermute | solution.py:58
  52.3 2.3 %collective-permute-done.4 = f32[1,144,128]{2,1,0:T(8,128)S(1)} collective-permute-done((f32[1,144,128]{2,1,0:T(8,128)S(1)}, f32[1,144,128]{2,1,0:T(8,128)S(1)}, u32[]{:S(2)}, u32[]{:S(2)}) %collective-permute-start.4) | collective-permute-done | bytes 73760 | tf_op jit(solution)/shard_map/ppermute | solution.py:58
  54.7 2.1 %collective-permute-start.5 = (f32[2,144,128]{2,1,0:T(8,128)S(1)}, f32[2,144,128]{2,1,0:T(8,128)S(1)}, u32[]{:S(2)}, u32[]{:S(2)}) collective-permute-start(f32[2,144,128]{2,1,0:T(8,128)S(1)} %pad_maximum_fusion.3), channel_id=1, source_target_pairs={{0,2},{1,3},{2,0},{3,1},{4,6},{5,7},{6,4},{7,5},{8,10},{9,11},{10,... | collective-permute-start | bytes 442376 | tf_op jit(solution)/shard_map/ppermute | solution.py:58
  56.7 3.1 %collective-permute-done.5 = f32[2,144,128]{2,1,0:T(8,128)S(1)} collective-permute-done((f32[2,144,128]{2,1,0:T(8,128)S(1)}, f32[2,144,128]{2,1,0:T(8,128)S(1)}, u32[]{:S(2)}, u32[]{:S(2)}) %collective-permute-start.5) | collective-permute-done | bytes 147488 | tf_op jit(solution)/shard_map/ppermute | solution.py:58
  59.9 2.1 %collective-permute-start.6 = (f32[4,144,128]{2,1,0:T(8,128)S(1)}, f32[4,144,128]{2,1,0:T(8,128)S(1)}, u32[]{:S(2)}, u32[]{:S(2)}) collective-permute-start(f32[4,144,128]{2,1,0:T(8,128)S(1)} %pad_maximum_fusion.low_ref.refs_4_.refs_0_), channel_id=1, source_target_pairs={{0,1},{1,0},{2,3},{3,2},{4,5},{5,4},{6,7},{7,6},{8,9},{9,8},{10,11... | collective-permute-start | bytes 884744 | tf_op jit(solution)/shard_map/ppermute | solution.py:58
  62.0 6.9 %collective-permute-done.6.high_ref.refs_5_.refs_1_ = f32[4,144,128]{2,1,0:T(8,128)S(1)} collective-permute-done((f32[4,144,128]{2,1,0:T(8,128)S(1)}, f32[4,144,128]{2,1,0:T(8,128)S(1)}, u32[]{:S(2)}, u32[]{:S(2)}) %collective-permute-start.6) | collective-permute-done | bytes 294944 | tf_op jit(solution)/shard_map/ppermute | solution.py:58
  69.5 1.8 %collective-permute-start.7 = (f32[1,40,256]{2,1,0:T(8,128)S(1)}, f32[1,40,256]{2,1,0:T(8,128)S(1)}, u32[]{:S(2)}, u32[]{:S(2)}) collective-permute-start(f32[1,40,256]{2,1,0:T(8,128)S(1)} %bitcast.14), channel_id=1, source_target_pairs={{0,16},{8,24},{16,0},{24,8},{1,17},{9,25},{17,1},{25,9},{2,18},{10... | collective-permute-start | bytes 122888 | tf_op jit(solution)/shard_map/ppermute | solution.py:58
  75.1 3.9 %shard_map.98 = (f32[40,256]{1,0:T(8,128)S(1)}, bf16[1280,128]{1,0:T(8,128)(2,1)S(1)}, bf16[32,256]{1,0:T(8,128)(2,1)S(1)}) custom-call(s32[2]{0:T(128)S(1)} %pad_add_fusion.me_ref.refs_0_, f32[2,40,256]{2,1,0:T(8,128)S(1)} %pad_maximum_fusion.4.refs_1_, f32[2,40,256]{2,1,0:T(8,128)S(1)} %collective-permute-done.8.refs_2_, ...), custom_call_target="tpu_custom_call" | custom-call | tf_op jit(solution)/shard_map/pallas_call | solution.py:876
  79.0 1.5 %collective-permute-start.9 = (f32[1,40,256]{2,1,0:T(8,128)S(1)}, f32[1,40,256]{2,1,0:T(8,128)S(1)}, u32[]{:S(2)}, u32[]{:S(2)}) collective-permute-start(f32[1,40,256]{2,1,0:T(8,128)S(1)} %bitcast.20), channel_id=1, source_target_pairs={{0,16},{8,24},{16,0},{24,8},{1,17},{9,25},{17,1},{25,9},{2,18},{10... | collective-permute-start | bytes 122888 | tf_op jit(solution)/shard_map/ppermute | solution.py:58
  80.5 2.1 %shard_map.99.refs_6_ = f32[8,32,128]{2,1,0:T(8,128)S(1)} custom-call(bf16[4,128,256]{2,1,0:T(8,128)(2,1)S(1)} %get-tuple-element.61.levels_ref, bf16[1280,128]{1,0:T(8,128)(2,1)S(1)} %get-tuple-element.62.spread_ref.refs_0_, bf16[32,256]{1,0:T(8,128)(2,1)S(1)} %get-tuple-element.63.solved_ref.refs_1_, ...), custom_call_target="tpu_custom_call" | custom-call | tf_op jit(solution)/shard_map/pallas_call | solution.py:868
  84.4 4.0 %shard_map.101 = (f32[40,256]{1,0:T(8,128)S(1)}, bf16[1280,128]{1,0:T(8,128)(2,1)S(1)}, bf16[32,256]{1,0:T(8,128)(2,1)S(1)}) custom-call(s32[2]{0:T(128)S(1)} %pad_add_fusion.me_ref.refs_0_, f32[2,40,256]{2,1,0:T(8,128)S(1)} %pad_maximum_fusion.5.refs_1_, f32[2,40,256]{2,1,0:T(8,128)S(1)} %collective-permute-done.10.refs_2_, ...), custom_call_target="tpu_custom_call" | custom-call | tf_op jit(solution)/shard_map/pallas_call | solution.py:876
  89.8 2.1 %shard_map.102.refs_0_ = f32[8,32,128]{2,1,0:T(8,128)S(1)} custom-call(bf16[4,128,256]{2,1,0:T(8,128)(2,1)S(1)} %get-tuple-element.69.levels_ref, bf16[1280,128]{1,0:T(8,128)(2,1)S(1)} %get-tuple-element.62.spread_ref.refs_0_, bf16[32,256]{1,0:T(8,128)(2,1)S(1)} %get-tuple-element.63.solved_ref.refs_1_, ...), custom_call_target="tpu_custom_call" | custom-call | tf_op jit(solution)/shard_map/pallas_call | solution.py:868
  92.4 2.1 %shard_map.103.refs_6_ = f32[8,32,128]{2,1,0:T(8,128)S(1)} custom-call(bf16[4,128,256]{2,1,0:T(8,128)(2,1)S(1)} %get-tuple-element.71.levels_ref, bf16[1280,128]{1,0:T(8,128)(2,1)S(1)} %get-tuple-element.72.spread_ref.refs_0_, bf16[32,256]{1,0:T(8,128)(2,1)S(1)} %get-tuple-element.73.solved_ref.refs_1_, f32[8,32,128]{2,1,0:T(8,128)S(1)} %shard_map.102.refs_0_), custom_call_target="tpu_custom_call" | custom-call | tf_op jit(solution)/shard_map/pallas_call | solution.py:868
  94.5 4.2 %shard_map.104 = (f32[40,256]{1,0:T(8,128)S(1)}, bf16[1280,128]{1,0:T(8,128)(2,1)S(1)}, bf16[32,256]{1,0:T(8,128)(2,1)S(1)}) custom-call(s32[2]{0:T(128)S(1)} %pad_add_fusion.me_ref.refs_0_, f32[2,40,256]{2,1,0:T(8,128)S(1)} %pad_maximum_fusion.6.refs_1_, f32[2,40,256]{2,1,0:T(8,128)S(1)} %collective-permute-done.12.refs_2_, ...), custom_call_target="tpu_custom_call" | custom-call | tf_op jit(solution)/shard_map/pallas_call | solution.py:876
  100.1 2.6 %shard_map.105.refs_2_ = f32[32,32,128]{2,1,0:T(8,128)S(1)} custom-call(s32[2]{0:T(128)S(1)} %pad_add_fusion.me_ref.refs_0_, f32[8,144,128]{2,1,0:T(8,128)S(1)} %all-to-all-done.record_ref, bf16[1280,128]{1,0:T(8,128)(2,1)S(1)} %get-tuple-element.72.spread_ref.refs_0_, bf16[32,256]{1,0:T(8,128)(2,1)S(1)} %get-tuple-element.73.solved_ref.refs_1_, ...), custom_call_target="tpu_custom_call" | custom-call | tf_op jit(solution)/shard_map/pallas_call | solution.py:860
  103.0 2.6 %shard_map.106.trans_ref = f32[32,32,128]{2,1,0:T(8,128)S(1)} custom-call(s32[2]{0:T(128)S(1)} %pad_add_fusion.me_ref.refs_0_, f32[8,144,128]{2,1,0:T(8,128)S(1)} %all-to-all-done.record_ref, bf16[1280,128]{1,0:T(8,128)(2,1)S(1)} %get-tuple-element.80.refs_0_, bf16[32,256]{1,0:T(8,128)(2,1)S(1)} %get-tuple-element.81.refs_1_, ...), custom_call_target="tpu_custom_call" | custom-call | tf_op jit(solution)/shard_map/pallas_call | solution.py:860
  105.7 9.4 %shard_map.107 = f32[32,128,128]{2,1,0:T(8,128)} custom-call(s32[2]{0:T(128)S(1)} %pad_add_fusion.me_ref.refs_0_, f32[2,40,256]{2,1,0:T(8,128)S(1)} %pad_maximum_fusion.7.lows_ref, f32[2,40,256]{2,1,0:T(8,128)S(1)} %collective-permute-done.14.highs_ref, f32[8,144,128]{2,1,0:T(8,128)S(1)} %all-to-all-done.record_ref, ...), custom_call_target="tpu_custom_call" | custom-call | tf_op jit(solution)/shard_map/pallas_call | solution.py:905
  (43 shorter events, 16.7 us)
Async XLA Ops:
  0.0 18.5 %copy-start = (f32[32,128,128]{2,1,0:T(8,128)S(1)}, f32[32,128,128]{2,1,0:T(8,128)}, u32[]{:S(2)}) copy-start(f32[32,128,128]{2,1,0:T(8,128)} %h_ref.1) | copy-start | bytes 6291460
  3.5 15.1 %copy-start.1 = (f32[2,128,128]{2,1,0:T(8,128)S(1)}, f32[2,128,128]{2,1,0:T(8,128)}, u32[]{:S(2)}) copy-start(f32[2,128,128]{2,1,0:T(8,128)} %get-tuple-element.46.coef_ref) | copy-start | bytes 393220
  3.5 15.1 %collective-permute-start = (f32[3,128,128]{2,1,0:T(8,128)}, f32[3,128,128]{2,1,0:T(8,128)S(1)}, u32[]{:S(2)}, u32[]{:S(2)}) collective-permute-start(f32[3,128,128]{2,1,0:T(8,128)} %get-tuple-element.47), channel_id=1, source_target_pairs={{0,1},{1,2},{2,3},{3,4},{4,5},{5,6},{6,7},{8,9},{9,10},{10,11},{11... | collective-permute-start | bytes 589832 | tf_op jit(solution)/shard_map/ppermute | solution.py:69
  8.5 10.1 %collective-permute-start.1 = (f32[3,128,128]{2,1,0:T(8,128)}, f32[3,128,128]{2,1,0:T(8,128)S(1)}, u32[]{:S(2)}, u32[]{:S(2)}) collective-permute-start(f32[3,128,128]{2,1,0:T(8,128)} %get-tuple-element.48), channel_id=1, source_target_pairs={{1,0},{2,1},{3,2},{4,3},{5,4},{6,5},{7,6},{9,8},{10,9},{11,10},{12... | collective-permute-start | bytes 589832 | tf_op jit(solution)/shard_map/ppermute | solution.py:69
  11.6 33.3 %all-to-all-start = ((f32[8,144,128]{2,1,0:T(8,128)}), f32[8,144,128]{2,1,0:T(8,128)S(1)}, u32[]{:S(2)}, u32[]{:S(2)}) async-start(f32[8,144,128]{2,1,0:T(8,128)} %broadcast_in_dim.18), calls=%async_computation | async-start | bytes 1179648 | tf_op jit(solution)/shard_map/all_to_all | solution.py:815
  19.3 4.7 %collective-permute-start.2 = (f32[40,8,128]{2,1,0:T(8,128)}, f32[40,8,128]{2,1,0:T(8,128)S(1)}, u32[]{:S(2)}, u32[]{:S(2)}) collective-permute-start(f32[40,8,128]{2,1,0:T(8,128)} %pad_maximum_fusion.1), channel_id=1, source_target_pairs={{0,8},{8,16},{16,24},{1,9},{9,17},{17,25},{2,10},{10,18},{18,26},{... | collective-permute-start | bytes 491528 | tf_op jit(solution)/shard_map/ppermute | solution.py:69
  21.3 5.2 %collective-permute-start.3 = (f32[40,8,128]{2,1,0:T(8,128)}, f32[40,8,128]{2,1,0:T(8,128)S(1)}, u32[]{:S(2)}, u32[]{:S(2)}) collective-permute-start(f32[40,8,128]{2,1,0:T(8,128)} %pad_maximum_fusion.2), channel_id=1, source_target_pairs={{8,0},{16,8},{24,16},{9,1},{17,9},{25,17},{10,2},{18,10},{26,18},{... | collective-permute-start | bytes 491528 | tf_op jit(solution)/shard_map/ppermute | solution.py:69
  49.3 5.3 %collective-permute-start.4 = (f32[1,144,128]{2,1,0:T(8,128)S(1)}, f32[1,144,128]{2,1,0:T(8,128)S(1)}, u32[]{:S(2)}, u32[]{:S(2)}) collective-permute-start(f32[1,144,128]{2,1,0:T(8,128)S(1)} %bitcast.11), channel_id=1, source_target_pairs={{0,4},{1,5},{2,6},{3,7},{4,0},{5,1},{6,2},{7,3},{8,12},{9,13},{10,... | collective-permute-start | bytes 221192 | tf_op jit(solution)/shard_map/ppermute | solution.py:58
  54.7 5.2 %collective-permute-start.5 = (f32[2,144,128]{2,1,0:T(8,128)S(1)}, f32[2,144,128]{2,1,0:T(8,128)S(1)}, u32[]{:S(2)}, u32[]{:S(2)}) collective-permute-start(f32[2,144,128]{2,1,0:T(8,128)S(1)} %pad_maximum_fusion.3), channel_id=1, source_target_pairs={{0,2},{1,3},{2,0},{3,1},{4,6},{5,7},{6,4},{7,5},{8,10},{9,11},{10,... | collective-permute-start | bytes 442376 | tf_op jit(solution)/shard_map/ppermute | solution.py:58
  59.9 8.9 %collective-permute-start.6 = (f32[4,144,128]{2,1,0:T(8,128)S(1)}, f32[4,144,128]{2,1,0:T(8,128)S(1)}, u32[]{:S(2)}, u32[]{:S(2)}) collective-permute-start(f32[4,144,128]{2,1,0:T(8,128)S(1)} %pad_maximum_fusion.low_ref.refs_4_.refs_0_), channel_id=1, source_target_pairs={{0,1},{1,0},{2,3},{3,2},{4,5},{5,4},{6,7},{7,6},{8,9},{9,8},{10,11... | collective-permute-start | bytes 884744 | tf_op jit(solution)/shard_map/ppermute | solution.py:58
  69.5 4.4 %collective-permute-start.7 = (f32[1,40,256]{2,1,0:T(8,128)S(1)}, f32[1,40,256]{2,1,0:T(8,128)S(1)}, u32[]{:S(2)}, u32[]{:S(2)}) collective-permute-start(f32[1,40,256]{2,1,0:T(8,128)S(1)} %bitcast.14), channel_id=1, source_target_pairs={{0,16},{8,24},{16,0},{24,8},{1,17},{9,25},{17,1},{25,9},{2,18},{10... | collective-permute-start | bytes 122888 | tf_op jit(solution)/shard_map/ppermute | solution.py:58
  73.8 1.3 %collective-permute-start.8 = (f32[2,40,256]{2,1,0:T(8,128)S(1)}, f32[2,40,256]{2,1,0:T(8,128)S(1)}, u32[]{:S(2)}, u32[]{:S(2)}) collective-permute-start(f32[2,40,256]{2,1,0:T(8,128)S(1)} %pad_maximum_fusion.4.refs_1_), channel_id=1, source_target_pairs={{0,8},{8,0},{16,24},{24,16},{1,9},{9,1},{17,25},{25,17},{2,10},{10... | collective-permute-start | bytes 245768 | tf_op jit(solution)/shard_map/ppermute | solution.py:58
  79.0 4.0 %collective-permute-start.9 = (f32[1,40,256]{2,1,0:T(8,128)S(1)}, f32[1,40,256]{2,1,0:T(8,128)S(1)}, u32[]{:S(2)}, u32[]{:S(2)}) collective-permute-start(f32[1,40,256]{2,1,0:T(8,128)S(1)} %bitcast.20), channel_id=1, source_target_pairs={{0,16},{8,24},{16,0},{24,8},{1,17},{9,25},{17,1},{25,9},{2,18},{10... | collective-permute-start | bytes 122888 | tf_op jit(solution)/shard_map/ppermute | solution.py:58
  83.1 1.3 %collective-permute-start.10 = (f32[2,40,256]{2,1,0:T(8,128)S(1)}, f32[2,40,256]{2,1,0:T(8,128)S(1)}, u32[]{:S(2)}, u32[]{:S(2)}) collective-permute-start(f32[2,40,256]{2,1,0:T(8,128)S(1)} %pad_maximum_fusion.5.refs_1_), channel_id=1, source_target_pairs={{0,8},{8,0},{16,24},{24,16},{1,9},{9,1},{17,25},{25,17},{2,10},{10... | collective-permute-start | bytes 245768 | tf_op jit(solution)/shard_map/ppermute | solution.py:58
  88.3 4.0 %collective-permute-start.11 = (f32[1,40,256]{2,1,0:T(8,128)S(1)}, f32[1,40,256]{2,1,0:T(8,128)S(1)}, u32[]{:S(2)}, u32[]{:S(2)}) collective-permute-start(f32[1,40,256]{2,1,0:T(8,128)S(1)} %bitcast.18), channel_id=1, source_target_pairs={{0,16},{8,24},{16,0},{24,8},{1,17},{9,25},{17,1},{25,9},{2,18},{10... | collective-permute-start | bytes 122888 | tf_op jit(solution)/shard_map/ppermute | solution.py:58
  92.3 2.1 %collective-permute-start.12 = (f32[2,40,256]{2,1,0:T(8,128)S(1)}, f32[2,40,256]{2,1,0:T(8,128)S(1)}, u32[]{:S(2)}, u32[]{:S(2)}) collective-permute-start(f32[2,40,256]{2,1,0:T(8,128)S(1)} %pad_maximum_fusion.6.refs_1_), channel_id=1, source_target_pairs={{0,8},{8,0},{16,24},{24,16},{1,9},{9,1},{17,25},{25,17},{2,10},{10... | collective-permute-start | bytes 245768 | tf_op jit(solution)/shard_map/ppermute | solution.py:58
  98.6 4.1 %collective-permute-start.13 = (f32[1,40,256]{2,1,0:T(8,128)S(1)}, f32[1,40,256]{2,1,0:T(8,128)S(1)}, u32[]{:S(2)}, u32[]{:S(2)}) collective-permute-start(f32[1,40,256]{2,1,0:T(8,128)S(1)} %bitcast.16), channel_id=1, source_target_pairs={{0,16},{8,24},{16,0},{24,8},{1,17},{9,25},{17,1},{25,9},{2,18},{10... | collective-permute-start | bytes 122888 | tf_op jit(solution)/shard_map/ppermute | solution.py:58
  102.8 2.9 %collective-permute-start.14 = (f32[2,40,256]{2,1,0:T(8,128)S(1)}, f32[2,40,256]{2,1,0:T(8,128)S(1)}, u32[]{:S(2)}, u32[]{:S(2)}) collective-permute-start(f32[2,40,256]{2,1,0:T(8,128)S(1)} %pad_maximum_fusion.7.lows_ref), channel_id=1, source_target_pairs={{0,8},{8,0},{16,24},{24,16},{1,9},{9,1},{17,25},{25,17},{2,10},{10... | collective-permute-start | bytes 245768 | tf_op jit(solution)/shard_map/ppermute | solution.py:58

commit v4 on v3

--- a/solution.py
+++ b/solution.py
@@ -1,4 +1,5 @@
 import functools
+import itertools
 
 import jax
 import jax.numpy as jnp
@@ -487,7 +488,7 @@
     return out
 
 
-def spread_sums(bands, spread_ref, ncol):
+def spread_steps(bands, spread_ref, ncol):
     height, width = bands[0].shape
     nrow = len(bands)
     members = width // ncol
@@ -514,6 +515,7 @@
             else:
                 value = jnp.concatenate(split3(group), axis=1)
             spread_ref[pl.ds(m * height, height), :] = value.astype(BF16)
+        yield
 
 
 def stacked(scaled):
@@ -526,7 +528,7 @@
     return stacked((levels * 0.125).astype(BF16))
 
 
-def solve_sums(bands, ncol):
+def solve_steps(bands, ncol, result):
     height, width = bands[0].shape
     members = width // ncol
     lanes = LANES
@@ -556,6 +558,7 @@
             for t in range(s + 1, block):
                 part = columns[t][k : k + 1, :] * inverse
                 columns[t] = jnp.where(row == k, part, columns[t] - column * part)
+        yield
     gain = a[members : members + 1, :] * (1.0 / (members - 1))
     out = jnp.where(lane1 < members, -0.5 * a[0:members, :] + gain, 0.0)
     out = jnp.where(lane1 == members, 1.0 / (members - 1), out)
@@ -565,7 +568,15 @@
         [hi[:, 0:deep], hi[:, 0:deep], lo[:, 0:deep], jnp.zeros((members, 2 * lanes - 3 * deep), F32)],
         axis=1,
     )
-    return stack.astype(BF16)
+    result.append(stack.astype(BF16))
+
+
+def together(long, short, every):
+    for n, _ in enumerate(long):
+        if n % every == every - 1:
+            next(short, None)
+    for _ in short:
+        pass
 
 
 def product3(stack, right):
@@ -609,11 +620,16 @@
                 at += 1
 
 
-def moved(levels_ref, spread, solved, read):
-    out = []
+def sums_steps(levels_ref, spread_ref, read, found):
     for p in range(levels_ref.shape[0]):
         z = jnp.concatenate([read(2 * p), read(2 * p + 1)], axis=1)
-        sums = apply_sums(spread, levels_ref[p], z, z.shape[0] + 8)
+        found.append((z, apply_sums(spread_ref[...], levels_ref[p], z, z.shape[0] + 8)))
+        yield
+
+
+def moved(found, solved):
+    out = []
+    for z, sums in found:
         z = z + product3(solved, sums)
         out += [z[:, 0:LANES], z[:, LANES:]]
     return out
@@ -633,11 +649,19 @@
     ncol = 2 * seen[0].shape[0]
     members = solved_ref.shape[0]
     bands = bands_of(row_strides, me_ref[0], lows_ref, highs_ref)
-    spread_sums(bands, spread_ref, ncol)
-    solved = solve_sums(bands, ncol)
+    target = batch + 1
+    result, found = [], []
+    together(
+        itertools.chain(
+            spread_steps(bands, spread_ref, ncol),
+            sums_steps(levels_ref, spread_ref, reader(seen, z_ref, members, target), found),
+        ),
+        solve_steps(bands, ncol, result),
+        3,
+    )
+    solved = result[0]
     solved_ref[...] = solved
-    target = batch + 1
-    zs = moved(levels_ref, spread_ref[...], solved, reader(seen, z_ref, members, target))
+    zs = moved(found, solved)
     parts = []
     meta = BATCH_COUNT * members + target
     for p in range(ncol):
@@ -656,14 +680,15 @@
     out_ref = refs[-1]
     z_ref = refs[0] if len(refs) == 2 else None
     read = reader(refs[0:2], z_ref, solved_ref.shape[0], target)
-    for p, z in enumerate(moved(levels_ref, spread_ref[...], solved_ref[...], read)):
+    found = []
+    for _ in sums_steps(levels_ref, spread_ref, read, found):
+        pass
+    for p, z in enumerate(moved(found, solved_ref[...])):
         out_ref[p] = z
 
 
-def compose(spread, solved, levels, batch, trans_ref, dst_ref, height):
-    members = solved.shape[0]
-    at = jnp.dot(spread, levels, preferred_element_type=F32)
-    lanes = LANES
+def compose_sums(spread_ref, levels, batch, trans_ref, height, members, found):
+    at = jnp.dot(spread_ref[...], levels, preferred_element_type=F32)
     for j in range(0, members, 2):
         sums = []
         for i in (j, j + 1):
@@ -675,8 +700,16 @@
                     term = at[m * height : (m + 1) * height, :] * trans_ref[i, m : m + 1, :]
                     total = term if total is None else total + term
                 sums.append(total)
-        change = product3(solved, jnp.concatenate(sums, axis=1))
-        for n, i in enumerate((j, j + 1)):
+        found.append(jnp.concatenate(sums, axis=1))
+        yield
+
+
+def compose_end(found, solved, batch, trans_ref, dst_ref):
+    members, lanes = solved.shape[0], LANES
+    for j, sums in enumerate(found):
+        change = product3(solved, sums)
+        for n in range(2):
+            i = 2 * j + n
             part = change[:, n * lanes : (n + 1) * lanes]
             if batch == 0:
                 dst_ref[i] = part + (iota((members, lanes), 0) == i).astype(F32)
@@ -693,9 +726,10 @@
     for n, batch in enumerate(batches):
         levels = copies_of(record_ref[me_ref[1], batch * devices : (batch + 1) * devices, :])
         source = trans_ref if n == 0 else out_ref
-        compose(
-            given[2 * n][...], given[2 * n + 1][...], levels, batch, source, out_ref, members + 8
-        )
+        found = []
+        for _ in compose_sums(given[2 * n], levels, batch, source, members + 8, members, found):
+            pass
+        compose_end(found, given[2 * n + 1][...], batch, source, out_ref)
 
 
 def split_kernel(state_ref, out_ref):
@@ -721,10 +755,17 @@
     devices = 2 * lows_ref.shape[0] * ncol
     batch = BATCH_COUNT - 1
     bands = bands_of(row_strides, me_ref[0], lows_ref, highs_ref)
-    spread_sums(bands, spread_ref, ncol)
-    solved = solve_sums(bands, ncol)
     levels = copies_of(record_ref[me_ref[1], batch * devices : (batch + 1) * devices, :])
-    compose(spread_ref[...], solved, levels, batch, trans_ref, whole_ref, height)
+    result, found = [], []
+    together(
+        itertools.chain(
+            spread_steps(bands, spread_ref, ncol),
+            compose_sums(spread_ref, levels, batch, trans_ref, height, members, found),
+        ),
+        solve_steps(bands, ncol, result),
+        6,
+    )
+    compose_end(found, result[0], batch, trans_ref, whole_ref)
     for i in range(members):
         hi, lo, _ = split3(whole_ref[:, i, :])
         turned_ref[i] = jnp.concatenate([hi, hi, lo, jnp.zeros_like(hi)], axis=0).T
@@ -893,15 +934,18 @@
     every, (found, parts), _ = gather_over(sums, "row", (found, parts))
     levels = dict(zip(pairs, found))
     sums, first = next_of(0, every, None)
-    every, z2, trans = gather_over(
-        sums, "row", moved_of(0, 2, first, None), compose_of((0,), first, None)
+    every, (z2, z3), trans = gather_over(
+        sums,
+        "row",
+        (moved_of(0, 2, first, None), moved_of(0, 3, first, None)),
+        compose_of((0,), first, None),
     )
     sums, second = next_of(1, every, z2)
-    z3 = moved_of(0, 3, first, None)
-    every, z3, z3_late = gather_over(sums, "row", z3, moved_of(1, 3, second, z3))
-    sums, third = next_of(2, every, z3_late)
-    trans = compose_of((1,), second, trans)
-    every, _, trans = gather_over(sums, "row", trans, compose_of((2,), third, trans))
+    every, trans, z3 = gather_over(
+        sums, "row", compose_of((1,), second, trans), moved_of(1, 3, second, z3)
+    )
+    sums, third = next_of(2, every, z3)
+    every, trans, _ = gather_over(sums, "row", compose_of((2,), third, trans))
     return call(
         functools.partial(final_kernel, row_strides),
         out(members, rows, cols),

time: 116 us -> 112 us (0.966)
  Pallas kernels: 64.1 us -> 59.2 us
  waiting for transfers between devices: 17.9 us -> 19.2 us
    pallas_call x3, Pallas kernels: 6.21 us -> 2.89 us  [moved_of(): call(functools.partial(moved_kernel, target), out(ncol, members, cols), [...]
    pallas_call x3, Pallas kernels: 12.1 us -> 10.5 us  [next_of(): call(functools.partial(next_kernel, row_strides, batch), (out(height, mem...]
    ppermute x11, waiting for transfers between devices: 15.5 us -> 16.8 us  [gather_over(): other = lax.ppermute(held, axis, [(i, i ^ stride) for i in range(n)])]
  transfers between devices with their start and end apart: 16 -> 16, of which waited for: 9 -> 11; matrix products, arithmetic and copies ran while one was open for 3% -> 3% of each run, Pallas kernels for 30% -> 28%
where the time goes in v4:
time: 112 us; the launch traced here: 111 us
  Pallas kernels  59.2 us (53%)
  starting transfers between devices  29.4 us (26%)
  waiting for transfers between devices  19.2 us (17%)
  local copies, waits for them, and re-layouts  1.78 us (2%)
  other arithmetic  1.51 us (1%)
    pallas_call x1, Pallas kernels, body(): call(forecast_kernel, out(members, rows, cols), [VMEM] * 6, [pltpu.VMEM((...  18.4 us
    ppermute x11, waiting for transfers between devices, gather_over(): other = lax.ppermute(held, axis, [(i, i ^ stride) for i in range(n)])  16.8 us
    ppermute x11, starting transfers between devices, gather_over(): other = lax.ppermute(held, axis, [(i, i ^ stride) for i in range(n)])  13.6 us
    pallas_call x3, Pallas kernels, next_of(): call(functools.partial(next_kernel, row_strides, batch), (out(height, mem...  10.5 us
    pallas_call x1, Pallas kernels, body(): call(functools.partial(final_kernel, row_strides), out(members, rows, col...  9.31 us
    all_to_all x1, starting transfers between devices, body(): lax.all_to_all(jnp.broadcast_to(record, (ncol, *record.shape)), 'col', sp...  6.96 us
    ppermute x2, starting transfers between devices, shift_pair(): lax.ppermute(high_send, axis, forward)  6.3 us
    pallas_call x3, Pallas kernels, compose_of(): call(functools.partial(compose_kernel, batches), out(members, members, co...  6.27 us
  transfers between devices with their start and end apart: 16, of which 11 were waited for; matrix products, arithmetic and copies ran while one was open for 3% of the time, Pallas kernels for 28%

profile of v4, /device:TPU:0, one launch (start us, length us, event | category | flops | bytes accessed | tf_op | source)
XLA Modules:
  0.0 111.5 jit_solution(10576922840995027336)
XLA Ops:
  0.0 3.5 %shard_map.91 = (f32[3,128,128]{2,1,0:T(8,128)}, f32[3,128,128]{2,1,0:T(8,128)}, f32[144,128]{1,0:T(8,128)}, f32[2,128,128]{2,1,0:T(8,128)}) custom-call(f32[32,128,128]{2,1,0:T(8,128)} %h_ref.1, s32[128,128]{1,0:T(8,128)} %depth_hbm.1, s32[128,128]{1,0:T(8,128)} %sea_hbm.1, s32[4,32,128]{2,1,0:T(8,128)} %bitcast.22, s32[4,64]{1,0:T(4,128)} %bitcast.23, ...), custom_call_target="tpu_custom_call" | custom-call | tf_op jit(solution)/shard_map/pallas_call | solution.py:828
  3.5 5.0 %collective-permute-start = (f32[3,128,128]{2,1,0:T(8,128)}, f32[3,128,128]{2,1,0:T(8,128)S(1)}, u32[]{:S(2)}, u32[]{:S(2)}) collective-permute-start(f32[3,128,128]{2,1,0:T(8,128)} %get-tuple-element.48), channel_id=1, source_target_pairs={{0,1},{1,2},{2,3},{3,4},{4,5},{5,6},{6,7},{8,9},{9,10},{10,11},{11... | collective-permute-start | bytes 589832 | tf_op jit(solution)/shard_map/ppermute | solution.py:70
  9.8 1.7 %broadcast_in_dim.18 = f32[8,144,128]{2,1,0:T(8,128)} broadcast(f32[144,128]{1,0:T(8,128)} %get-tuple-element.46), dimensions={1,2} | broadcast | bytes 663552 | tf_op jit(solution)/shard_map/broadcast_in_dim | solution.py:857
  11.6 7.0 %all-to-all-start = ((f32[8,144,128]{2,1,0:T(8,128)}), f32[8,144,128]{2,1,0:T(8,128)S(1)}, u32[]{:S(2)}, u32[]{:S(2)}) async-start(f32[8,144,128]{2,1,0:T(8,128)} %broadcast_in_dim.18), calls=%async_computation | async-start | bytes 1179648 | tf_op jit(solution)/shard_map/all_to_all | solution.py:856
  22.6 1.4 %shard_map.92 = (f32[8,128,128]{2,1,0:T(8,128)S(1)}, f32[4,128,128]{2,1,0:T(8,128)S(1)}, f32[32,128,128]{2,1,0:T(8,128)S(1)}) custom-call(f32[32,128,128]{2,1,0:T(8,128)S(1)} %copy-done, f32[2,128,128]{2,1,0:T(8,128)S(1)} %copy-done.1, f32[3,128,128]{2,1,0:T(8,128)S(1)} %collective-permute-done.left_ref, f32[3,128,128]{2,1,0:T(8,128)S(1)} %collective-permute-done.1.right_ref), custom_call_target="tpu_custom_call" | custom-call | tf_op jit(solution)/shard_map/pallas_call | solution.py:862
  24.0 2.4 %collective-permute-done.3.down_ref = f32[40,8,128]{2,1,0:T(8,128)S(1)} collective-permute-done((f32[40,8,128]{2,1,0:T(8,128)}, f32[40,8,128]{2,1,0:T(8,128)S(1)}, u32[]{:S(2)}, u32[]{:S(2)}) %collective-permute-start.3) | collective-permute-done | bytes 163872 | tf_op jit(solution)/shard_map/ppermute | solution.py:70
  26.5 18.4 %shard_map.93.state_ref = f32[32,128,128]{2,1,0:T(8,128)S(1)} custom-call(f32[32,128,128]{2,1,0:T(8,128)S(1)} %get-tuple-element.50.h_ref, f32[2,128,128]{2,1,0:T(8,128)S(1)} %copy-done.1, f32[8,128,128]{2,1,0:T(8,128)S(1)} %get-tuple-element.51.own_ref, f32[4,128,128]{2,1,0:T(8,128)S(1)} %get-tuple-element.52.own_k_ref, ...), custom_call_target="tpu_custom_call" | custom-call | tf_op jit(solution)/shard_map/pallas_call | solution.py:867
  44.9 4.4 %shard_map.94 = f32[144,128]{1,0:T(8,128)S(1)} custom-call(s32[2]{0:T(128)S(1)} %pad_add_fusion.me_ref.refs_0_, f32[8,144,128]{2,1,0:T(8,128)S(1)} %all-to-all-done.record_ref, f32[32,128,128]{2,1,0:T(8,128)S(1)} %shard_map.93.state_ref), custom_call_target="tpu_custom_call" | custom-call | tf_op jit(solution)/shard_map/pallas_call | solution.py:885
  49.3 3.0 %collective-permute-start.4 = (f32[1,144,128]{2,1,0:T(8,128)S(1)}, f32[1,144,128]{2,1,0:T(8,128)S(1)}, u32[]{:S(2)}, u32[]{:S(2)}) collective-permute-start(f32[1,144,128]{2,1,0:T(8,128)S(1)} %bitcast.11), channel_id=1, source_target_pairs={{0,4},{1,5},{2,6},{3,7},{4,0},{5,1},{6,2},{7,3},{8,12},{9,13},{10,... | collective-permute-start | bytes 221192 | tf_op jit(solution)/shard_map/ppermute | solution.py:59
  52.3 2.3 %collective-permute-done.4 = f32[1,144,128]{2,1,0:T(8,128)S(1)} collective-permute-done((f32[1,144,128]{2,1,0:T(8,128)S(1)}, f32[1,144,128]{2,1,0:T(8,128)S(1)}, u32[]{:S(2)}, u32[]{:S(2)}) %collective-permute-start.4) | collective-permute-done | bytes 73760 | tf_op jit(solution)/shard_map/ppermute | solution.py:59
  54.7 2.1 %collective-permute-start.5 = (f32[2,144,128]{2,1,0:T(8,128)S(1)}, f32[2,144,128]{2,1,0:T(8,128)S(1)}, u32[]{:S(2)}, u32[]{:S(2)}) collective-permute-start(f32[2,144,128]{2,1,0:T(8,128)S(1)} %pad_maximum_fusion.3), channel_id=1, source_target_pairs={{0,2},{1,3},{2,0},{3,1},{4,6},{5,7},{6,4},{7,5},{8,10},{9,11},{10,... | collective-permute-start | bytes 442376 | tf_op jit(solution)/shard_map/ppermute | solution.py:59
  56.7 3.1 %collective-permute-done.5 = f32[2,144,128]{2,1,0:T(8,128)S(1)} collective-permute-done((f32[2,144,128]{2,1,0:T(8,128)S(1)}, f32[2,144,128]{2,1,0:T(8,128)S(1)}, u32[]{:S(2)}, u32[]{:S(2)}) %collective-permute-start.5) | collective-permute-done | bytes 147488 | tf_op jit(solution)/shard_map/ppermute | solution.py:59
  59.9 2.1 %collective-permute-start.6 = (f32[4,144,128]{2,1,0:T(8,128)S(1)}, f32[4,144,128]{2,1,0:T(8,128)S(1)}, u32[]{:S(2)}, u32[]{:S(2)}) collective-permute-start(f32[4,144,128]{2,1,0:T(8,128)S(1)} %pad_maximum_fusion.low_ref.refs_4_.refs_0_), channel_id=1, source_target_pairs={{0,1},{1,0},{2,3},{3,2},{4,5},{5,4},{6,7},{7,6},{8,9},{9,8},{10,11... | collective-permute-start | bytes 884744 | tf_op jit(solution)/shard_map/ppermute | solution.py:59
  62.0 6.9 %collective-permute-done.6.high_ref.refs_5_.refs_1_ = f32[4,144,128]{2,1,0:T(8,128)S(1)} collective-permute-done((f32[4,144,128]{2,1,0:T(8,128)S(1)}, f32[4,144,128]{2,1,0:T(8,128)S(1)}, u32[]{:S(2)}, u32[]{:S(2)}) %collective-permute-start.6) | collective-permute-done | bytes 294944 | tf_op jit(solution)/shard_map/ppermute | solution.py:59
  69.5 1.8 %collective-permute-start.7 = (f32[1,40,256]{2,1,0:T(8,128)S(1)}, f32[1,40,256]{2,1,0:T(8,128)S(1)}, u32[]{:S(2)}, u32[]{:S(2)}) collective-permute-start(f32[1,40,256]{2,1,0:T(8,128)S(1)} %bitcast.14), channel_id=1, source_target_pairs={{0,16},{8,24},{16,0},{24,8},{1,17},{9,25},{17,1},{25,9},{2,18},{10... | collective-permute-start | bytes 122888 | tf_op jit(solution)/shard_map/ppermute | solution.py:59
  75.1 3.5 %shard_map.98 = (f32[40,256]{1,0:T(8,128)S(1)}, bf16[1280,128]{1,0:T(8,128)(2,1)S(1)}, bf16[32,256]{1,0:T(8,128)(2,1)S(1)}) custom-call(s32[2]{0:T(128)S(1)} %pad_add_fusion.me_ref.refs_0_, f32[2,40,256]{2,1,0:T(8,128)S(1)} %pad_maximum_fusion.4.refs_1_, f32[2,40,256]{2,1,0:T(8,128)S(1)} %collective-permute-done.8.refs_2_, ...), custom_call_target="tpu_custom_call" | custom-call | tf_op jit(solution)/shard_map/pallas_call | solution.py:917
  78.6 1.5 %collective-permute-start.9 = (f32[1,40,256]{2,1,0:T(8,128)S(1)}, f32[1,40,256]{2,1,0:T(8,128)S(1)}, u32[]{:S(2)}, u32[]{:S(2)}) collective-permute-start(f32[1,40,256]{2,1,0:T(8,128)S(1)} %bitcast.18), channel_id=1, source_target_pairs={{0,16},{8,24},{16,0},{24,8},{1,17},{9,25},{17,1},{25,9},{2,18},{10... | collective-permute-start | bytes 122888 | tf_op jit(solution)/shard_map/ppermute | solution.py:59
  83.9 3.5 %shard_map.102 = (f32[40,256]{1,0:T(8,128)S(1)}, bf16[1280,128]{1,0:T(8,128)(2,1)S(1)}, bf16[32,256]{1,0:T(8,128)(2,1)S(1)}) custom-call(s32[2]{0:T(128)S(1)} %pad_add_fusion.me_ref.refs_0_, f32[2,40,256]{2,1,0:T(8,128)S(1)} %pad_maximum_fusion.5.refs_1_, f32[2,40,256]{2,1,0:T(8,128)S(1)} %collective-permute-done.10.refs_2_, ...), custom_call_target="tpu_custom_call" | custom-call | tf_op jit(solution)/shard_map/pallas_call | solution.py:917
  87.4 1.5 %collective-permute-start.11 = (f32[1,40,256]{2,1,0:T(8,128)S(1)}, f32[1,40,256]{2,1,0:T(8,128)S(1)}, u32[]{:S(2)}, u32[]{:S(2)}) collective-permute-start(f32[1,40,256]{2,1,0:T(8,128)S(1)} %bitcast.20), channel_id=1, source_target_pairs={{0,16},{8,24},{16,0},{24,8},{1,17},{9,25},{17,1},{25,9},{2,18},{10... | collective-permute-start | bytes 122888 | tf_op jit(solution)/shard_map/ppermute | solution.py:59
  88.9 2.6 %shard_map.103.refs_2_ = f32[32,32,128]{2,1,0:T(8,128)S(1)} custom-call(s32[2]{0:T(128)S(1)} %pad_add_fusion.me_ref.refs_0_, f32[8,144,128]{2,1,0:T(8,128)S(1)} %all-to-all-done.record_ref, bf16[1280,128]{1,0:T(8,128)(2,1)S(1)} %get-tuple-element.71.refs_0_.spread_ref, bf16[32,256]{1,0:T(8,128)(2,1)S(1)} %get-tuple-element.72.refs_1_.solved_ref, ...), custom_call_target="tpu_custom_call" | custom-call | tf_op jit(solution)/shard_map/pallas_call | solution.py:901
  92.9 3.5 %shard_map.105 = (f32[40,256]{1,0:T(8,128)S(1)}, bf16[1280,128]{1,0:T(8,128)(2,1)S(1)}, bf16[32,256]{1,0:T(8,128)(2,1)S(1)}) custom-call(s32[2]{0:T(128)S(1)} %pad_add_fusion.me_ref.refs_0_, f32[2,40,256]{2,1,0:T(8,128)S(1)} %pad_maximum_fusion.6.refs_1_, f32[2,40,256]{2,1,0:T(8,128)S(1)} %collective-permute-done.12.refs_2_, ...), custom_call_target="tpu_custom_call" | custom-call | tf_op jit(solution)/shard_map/pallas_call | solution.py:917
  96.4 1.5 %collective-permute-start.13 = (f32[1,40,256]{2,1,0:T(8,128)S(1)}, f32[1,40,256]{2,1,0:T(8,128)S(1)}, u32[]{:S(2)}, u32[]{:S(2)}) collective-permute-start(f32[1,40,256]{2,1,0:T(8,128)S(1)} %bitcast.16), channel_id=1, source_target_pairs={{0,16},{8,24},{16,0},{24,8},{1,17},{9,25},{17,1},{25,9},{2,18},{10... | collective-permute-start | bytes 122888 | tf_op jit(solution)/shard_map/ppermute | solution.py:59
  98.0 2.6 %shard_map.106.trans_ref = f32[32,32,128]{2,1,0:T(8,128)S(1)} custom-call(s32[2]{0:T(128)S(1)} %pad_add_fusion.me_ref.refs_0_, f32[8,144,128]{2,1,0:T(8,128)S(1)} %all-to-all-done.record_ref, bf16[1280,128]{1,0:T(8,128)(2,1)S(1)} %get-tuple-element.81.refs_0_, bf16[32,256]{1,0:T(8,128)(2,1)S(1)} %get-tuple-element.82.refs_1_, ...), custom_call_target="tpu_custom_call" | custom-call | tf_op jit(solution)/shard_map/pallas_call | solution.py:901
  102.0 9.3 %shard_map.107 = f32[32,128,128]{2,1,0:T(8,128)} custom-call(s32[2]{0:T(128)S(1)} %pad_add_fusion.me_ref.refs_0_, f32[2,40,256]{2,1,0:T(8,128)S(1)} %pad_maximum_fusion.7.lows_ref, f32[2,40,256]{2,1,0:T(8,128)S(1)} %collective-permute-done.14.highs_ref, f32[8,144,128]{2,1,0:T(8,128)S(1)} %all-to-all-done.record_ref, ...), custom_call_target="tpu_custom_call" | custom-call | tf_op jit(solution)/shard_map/pallas_call | solution.py:949
  (43 shorter events, 16.4 us)
Async XLA Ops:
  0.0 18.5 %copy-start = (f32[32,128,128]{2,1,0:T(8,128)S(1)}, f32[32,128,128]{2,1,0:T(8,128)}, u32[]{:S(2)}) copy-start(f32[32,128,128]{2,1,0:T(8,128)} %h_ref.1) | copy-start | bytes 6291460
  3.5 15.1 %copy-start.1 = (f32[2,128,128]{2,1,0:T(8,128)S(1)}, f32[2,128,128]{2,1,0:T(8,128)}, u32[]{:S(2)}) copy-start(f32[2,128,128]{2,1,0:T(8,128)} %get-tuple-element.47.coef_ref) | copy-start | bytes 393220
  3.5 15.1 %collective-permute-start = (f32[3,128,128]{2,1,0:T(8,128)}, f32[3,128,128]{2,1,0:T(8,128)S(1)}, u32[]{:S(2)}, u32[]{:S(2)}) collective-permute-start(f32[3,128,128]{2,1,0:T(8,128)} %get-tuple-element.48), channel_id=1, source_target_pairs={{0,1},{1,2},{2,3},{3,4},{4,5},{5,6},{6,7},{8,9},{9,10},{10,11},{11... | collective-permute-start | bytes 589832 | tf_op jit(solution)/shard_map/ppermute | solution.py:70
  8.5 10.1 %collective-permute-start.1 = (f32[3,128,128]{2,1,0:T(8,128)}, f32[3,128,128]{2,1,0:T(8,128)S(1)}, u32[]{:S(2)}, u32[]{:S(2)}) collective-permute-start(f32[3,128,128]{2,1,0:T(8,128)} %get-tuple-element.49), channel_id=1, source_target_pairs={{1,0},{2,1},{3,2},{4,3},{5,4},{6,5},{7,6},{9,8},{10,9},{11,10},{12... | collective-permute-start | bytes 589832 | tf_op jit(solution)/shard_map/ppermute | solution.py:70
  11.6 33.3 %all-to-all-start = ((f32[8,144,128]{2,1,0:T(8,128)}), f32[8,144,128]{2,1,0:T(8,128)S(1)}, u32[]{:S(2)}, u32[]{:S(2)}) async-start(f32[8,144,128]{2,1,0:T(8,128)} %broadcast_in_dim.18), calls=%async_computation | async-start | bytes 1179648 | tf_op jit(solution)/shard_map/all_to_all | solution.py:856
  19.3 4.7 %collective-permute-start.2 = (f32[40,8,128]{2,1,0:T(8,128)}, f32[40,8,128]{2,1,0:T(8,128)S(1)}, u32[]{:S(2)}, u32[]{:S(2)}) collective-permute-start(f32[40,8,128]{2,1,0:T(8,128)} %pad_maximum_fusion.1), channel_id=1, source_target_pairs={{0,8},{8,16},{16,24},{1,9},{9,17},{17,25},{2,10},{10,18},{18,26},{... | collective-permute-start | bytes 491528 | tf_op jit(solution)/shard_map/ppermute | solution.py:70
  21.3 5.2 %collective-permute-start.3 = (f32[40,8,128]{2,1,0:T(8,128)}, f32[40,8,128]{2,1,0:T(8,128)S(1)}, u32[]{:S(2)}, u32[]{:S(2)}) collective-permute-start(f32[40,8,128]{2,1,0:T(8,128)} %pad_maximum_fusion.2), channel_id=1, source_target_pairs={{8,0},{16,8},{24,16},{9,1},{17,9},{25,17},{10,2},{18,10},{26,18},{... | collective-permute-start | bytes 491528 | tf_op jit(solution)/shard_map/ppermute | solution.py:70
  49.3 5.3 %collective-permute-start.4 = (f32[1,144,128]{2,1,0:T(8,128)S(1)}, f32[1,144,128]{2,1,0:T(8,128)S(1)}, u32[]{:S(2)}, u32[]{:S(2)}) collective-permute-start(f32[1,144,128]{2,1,0:T(8,128)S(1)} %bitcast.11), channel_id=1, source_target_pairs={{0,4},{1,5},{2,6},{3,7},{4,0},{5,1},{6,2},{7,3},{8,12},{9,13},{10,... | collective-permute-start | bytes 221192 | tf_op jit(solution)/shard_map/ppermute | solution.py:59
  54.7 5.2 %collective-permute-start.5 = (f32[2,144,128]{2,1,0:T(8,128)S(1)}, f32[2,144,128]{2,1,0:T(8,128)S(1)}, u32[]{:S(2)}, u32[]{:S(2)}) collective-permute-start(f32[2,144,128]{2,1,0:T(8,128)S(1)} %pad_maximum_fusion.3), channel_id=1, source_target_pairs={{0,2},{1,3},{2,0},{3,1},{4,6},{5,7},{6,4},{7,5},{8,10},{9,11},{10,... | collective-permute-start | bytes 442376 | tf_op jit(solution)/shard_map/ppermute | solution.py:59
  59.9 8.9 %collective-permute-start.6 = (f32[4,144,128]{2,1,0:T(8,128)S(1)}, f32[4,144,128]{2,1,0:T(8,128)S(1)}, u32[]{:S(2)}, u32[]{:S(2)}) collective-permute-start(f32[4,144,128]{2,1,0:T(8,128)S(1)} %pad_maximum_fusion.low_ref.refs_4_.refs_0_), channel_id=1, source_target_pairs={{0,1},{1,0},{2,3},{3,2},{4,5},{5,4},{6,7},{7,6},{8,9},{9,8},{10,11... | collective-permute-start | bytes 884744 | tf_op jit(solution)/shard_map/ppermute | solution.py:59
  69.5 4.4 %collective-permute-start.7 = (f32[1,40,256]{2,1,0:T(8,128)S(1)}, f32[1,40,256]{2,1,0:T(8,128)S(1)}, u32[]{:S(2)}, u32[]{:S(2)}) collective-permute-start(f32[1,40,256]{2,1,0:T(8,128)S(1)} %bitcast.14), channel_id=1, source_target_pairs={{0,16},{8,24},{16,0},{24,8},{1,17},{9,25},{17,1},{25,9},{2,18},{10... | collective-permute-start | bytes 122888 | tf_op jit(solution)/shard_map/ppermute | solution.py:59
  73.8 1.3 %collective-permute-start.8 = (f32[2,40,256]{2,1,0:T(8,128)S(1)}, f32[2,40,256]{2,1,0:T(8,128)S(1)}, u32[]{:S(2)}, u32[]{:S(2)}) collective-permute-start(f32[2,40,256]{2,1,0:T(8,128)S(1)} %pad_maximum_fusion.4.refs_1_), channel_id=1, source_target_pairs={{0,8},{8,0},{16,24},{24,16},{1,9},{9,1},{17,25},{25,17},{2,10},{10... | collective-permute-start | bytes 245768 | tf_op jit(solution)/shard_map/ppermute | solution.py:59
  78.6 4.0 %collective-permute-start.9 = (f32[1,40,256]{2,1,0:T(8,128)S(1)}, f32[1,40,256]{2,1,0:T(8,128)S(1)}, u32[]{:S(2)}, u32[]{:S(2)}) collective-permute-start(f32[1,40,256]{2,1,0:T(8,128)S(1)} %bitcast.18), channel_id=1, source_target_pairs={{0,16},{8,24},{16,0},{24,8},{1,17},{9,25},{17,1},{25,9},{2,18},{10... | collective-permute-start | bytes 122888 | tf_op jit(solution)/shard_map/ppermute | solution.py:59
  82.6 1.3 %collective-permute-start.10 = (f32[2,40,256]{2,1,0:T(8,128)S(1)}, f32[2,40,256]{2,1,0:T(8,128)S(1)}, u32[]{:S(2)}, u32[]{:S(2)}) collective-permute-start(f32[2,40,256]{2,1,0:T(8,128)S(1)} %pad_maximum_fusion.5.refs_1_), channel_id=1, source_target_pairs={{0,8},{8,0},{16,24},{24,16},{1,9},{9,1},{17,25},{25,17},{2,10},{10... | collective-permute-start | bytes 245768 | tf_op jit(solution)/shard_map/ppermute | solution.py:59
  87.4 4.1 %collective-permute-start.11 = (f32[1,40,256]{2,1,0:T(8,128)S(1)}, f32[1,40,256]{2,1,0:T(8,128)S(1)}, u32[]{:S(2)}, u32[]{:S(2)}) collective-permute-start(f32[1,40,256]{2,1,0:T(8,128)S(1)} %bitcast.20), channel_id=1, source_target_pairs={{0,16},{8,24},{16,0},{24,8},{1,17},{9,25},{17,1},{25,9},{2,18},{10... | collective-permute-start | bytes 122888 | tf_op jit(solution)/shard_map/ppermute | solution.py:59
  91.6 1.3 %collective-permute-start.12 = (f32[2,40,256]{2,1,0:T(8,128)S(1)}, f32[2,40,256]{2,1,0:T(8,128)S(1)}, u32[]{:S(2)}, u32[]{:S(2)}) collective-permute-start(f32[2,40,256]{2,1,0:T(8,128)S(1)} %pad_maximum_fusion.6.refs_1_), channel_id=1, source_target_pairs={{0,8},{8,0},{16,24},{24,16},{1,9},{9,1},{17,25},{25,17},{2,10},{10... | collective-permute-start | bytes 245768 | tf_op jit(solution)/shard_map/ppermute | solution.py:59
  96.4 4.2 %collective-permute-start.13 = (f32[1,40,256]{2,1,0:T(8,128)S(1)}, f32[1,40,256]{2,1,0:T(8,128)S(1)}, u32[]{:S(2)}, u32[]{:S(2)}) collective-permute-start(f32[1,40,256]{2,1,0:T(8,128)S(1)} %bitcast.16), channel_id=1, source_target_pairs={{0,16},{8,24},{16,0},{24,8},{1,17},{9,25},{17,1},{25,9},{2,18},{10... | collective-permute-start | bytes 122888 | tf_op jit(solution)/shard_map/ppermute | solution.py:59
  100.7 1.3 %collective-permute-start.14 = (f32[2,40,256]{2,1,0:T(8,128)S(1)}, f32[2,40,256]{2,1,0:T(8,128)S(1)}, u32[]{:S(2)}, u32[]{:S(2)}) collective-permute-start(f32[2,40,256]{2,1,0:T(8,128)S(1)} %pad_maximum_fusion.7.lows_ref), channel_id=1, source_target_pairs={{0,8},{8,0},{16,24},{24,16},{1,9},{9,1},{17,25},{25,17},{2,10},{10... | collective-permute-start | bytes 245768 | tf_op jit(solution)/shard_map/ppermute | solution.py:59

commit v5 on v4

--- a/solution.py
+++ b/solution.py
@@ -657,7 +657,7 @@
             sums_steps(levels_ref, spread_ref, reader(seen, z_ref, members, target), found),
         ),
         solve_steps(bands, ncol, result),
-        3,
+        2,
     )
     solved = result[0]
     solved_ref[...] = solved
@@ -763,7 +763,7 @@
             compose_sums(spread_ref, levels, batch, trans_ref, height, members, found),
         ),
         solve_steps(bands, ncol, result),
-        6,
+        2,
     )
     compose_end(found, result[0], batch, trans_ref, whole_ref)
     for i in range(members):
@@ -774,7 +774,7 @@
     copies = []
     for c in range(sems.shape[0]):
 
-        @pl.loop(c * share // 8, (c + 1) * share // 8)
+        @pl.loop(c * share // 8, (c + 1) * share // 8, unroll=2)
         def _(b):
             start = pl.multiple_of(b * 8, 8)
             lefts = jnp.swapaxes(turned_ref[:, pl.ds(start, 8), :], 0, 1).astype(BF16)

time: 112 us -> 110 us (0.982)
  Pallas kernels: 59.2 us -> 57.8 us
    pallas_call x1, Pallas kernels: 9.31 us -> 7.94 us  [body(): call(functools.partial(final_kernel, row_strides), out(members, rows, col...]
where the time goes in v5:
time: 110 us
  Pallas kernels  57.8 us (53%)
  starting transfers between devices  29.4 us (27%)
  waiting for transfers between devices  19.2 us (17%)
  local copies, waits for them, and re-layouts  1.78 us (2%)
  other arithmetic  1.51 us (1%)
    pallas_call x1, Pallas kernels, body(): call(forecast_kernel, out(members, rows, cols), [VMEM] * 6, [pltpu.VMEM((...  18.4 us
    ppermute x11, waiting for transfers between devices, gather_over(): other = lax.ppermute(held, axis, [(i, i ^ stride) for i in range(n)])  16.8 us
    ppermute x11, starting transfers between devices, gather_over(): other = lax.ppermute(held, axis, [(i, i ^ stride) for i in range(n)])  13.6 us
    pallas_call x3, Pallas kernels, next_of(): call(functools.partial(next_kernel, row_strides, batch), (out(height, mem...  10.5 us
    pallas_call x1, Pallas kernels, body(): call(functools.partial(final_kernel, row_strides), out(members, rows, col...  7.94 us
    all_to_all x1, starting transfers between devices, body(): lax.all_to_all(jnp.broadcast_to(record, (ncol, *record.shape)), 'col', sp...  6.96 us
    ppermute x2, starting transfers between devices, shift_pair(): lax.ppermute(high_send, axis, forward)  6.3 us
    pallas_call x3, Pallas kernels, compose_of(): call(functools.partial(compose_kernel, batches), out(members, members, co...  6.27 us
  transfers between devices with their start and end apart: 16, of which 11 were waited for; matrix products, arithmetic and copies ran while one was open for 3% of the time, Pallas kernels for 28%

profile of v5, /device:TPU:0, one launch (start us, length us, event | category | flops | bytes accessed | tf_op | source)
XLA Modules:
  0.0 110.1 jit_solution(572551883464238841)
XLA Ops:
  0.0 3.5 %shard_map.91 = (f32[3,128,128]{2,1,0:T(8,128)}, f32[3,128,128]{2,1,0:T(8,128)}, f32[144,128]{1,0:T(8,128)}, f32[2,128,128]{2,1,0:T(8,128)}) custom-call(f32[32,128,128]{2,1,0:T(8,128)} %h_ref.1, s32[128,128]{1,0:T(8,128)} %depth_hbm.1, s32[128,128]{1,0:T(8,128)} %sea_hbm.1, s32[4,32,128]{2,1,0:T(8,128)} %bitcast.22, s32[4,64]{1,0:T(4,128)} %bitcast.23, ...), custom_call_target="tpu_custom_call" | custom-call | tf_op jit(solution)/shard_map/pallas_call | solution.py:828
  3.5 5.0 %collective-permute-start = (f32[3,128,128]{2,1,0:T(8,128)}, f32[3,128,128]{2,1,0:T(8,128)S(1)}, u32[]{:S(2)}, u32[]{:S(2)}) collective-permute-start(f32[3,128,128]{2,1,0:T(8,128)} %get-tuple-element.48), channel_id=1, source_target_pairs={{0,1},{1,2},{2,3},{3,4},{4,5},{5,6},{6,7},{8,9},{9,10},{10,11},{11... | collective-permute-start | bytes 589832 | tf_op jit(solution)/shard_map/ppermute | solution.py:70
  9.8 1.7 %broadcast_in_dim.18 = f32[8,144,128]{2,1,0:T(8,128)} broadcast(f32[144,128]{1,0:T(8,128)} %get-tuple-element.46), dimensions={1,2} | broadcast | bytes 663552 | tf_op jit(solution)/shard_map/broadcast_in_dim | solution.py:857
  11.6 7.0 %all-to-all-start = ((f32[8,144,128]{2,1,0:T(8,128)}), f32[8,144,128]{2,1,0:T(8,128)S(1)}, u32[]{:S(2)}, u32[]{:S(2)}) async-start(f32[8,144,128]{2,1,0:T(8,128)} %broadcast_in_dim.18), calls=%async_computation | async-start | bytes 1179648 | tf_op jit(solution)/shard_map/all_to_all | solution.py:856
  22.6 1.4 %shard_map.92 = (f32[8,128,128]{2,1,0:T(8,128)S(1)}, f32[4,128,128]{2,1,0:T(8,128)S(1)}, f32[32,128,128]{2,1,0:T(8,128)S(1)}) custom-call(f32[32,128,128]{2,1,0:T(8,128)S(1)} %copy-done, f32[2,128,128]{2,1,0:T(8,128)S(1)} %copy-done.1, f32[3,128,128]{2,1,0:T(8,128)S(1)} %collective-permute-done.left_ref, f32[3,128,128]{2,1,0:T(8,128)S(1)} %collective-permute-done.1.right_ref), custom_call_target="tpu_custom_call" | custom-call | tf_op jit(solution)/shard_map/pallas_call | solution.py:862
  24.0 2.4 %collective-permute-done.3.down_ref = f32[40,8,128]{2,1,0:T(8,128)S(1)} collective-permute-done((f32[40,8,128]{2,1,0:T(8,128)}, f32[40,8,128]{2,1,0:T(8,128)S(1)}, u32[]{:S(2)}, u32[]{:S(2)}) %collective-permute-start.3) | collective-permute-done | bytes 163872 | tf_op jit(solution)/shard_map/ppermute | solution.py:70
  26.5 18.4 %shard_map.93.state_ref = f32[32,128,128]{2,1,0:T(8,128)S(1)} custom-call(f32[32,128,128]{2,1,0:T(8,128)S(1)} %get-tuple-element.50.h_ref, f32[2,128,128]{2,1,0:T(8,128)S(1)} %copy-done.1, f32[8,128,128]{2,1,0:T(8,128)S(1)} %get-tuple-element.51.own_ref, f32[4,128,128]{2,1,0:T(8,128)S(1)} %get-tuple-element.52.own_k_ref, ...), custom_call_target="tpu_custom_call" | custom-call | tf_op jit(solution)/shard_map/pallas_call | solution.py:867
  44.9 4.4 %shard_map.94 = f32[144,128]{1,0:T(8,128)S(1)} custom-call(s32[2]{0:T(128)S(1)} %pad_add_fusion.me_ref.refs_0_, f32[8,144,128]{2,1,0:T(8,128)S(1)} %all-to-all-done.record_ref, f32[32,128,128]{2,1,0:T(8,128)S(1)} %shard_map.93.state_ref), custom_call_target="tpu_custom_call" | custom-call | tf_op jit(solution)/shard_map/pallas_call | solution.py:885
  49.3 3.0 %collective-permute-start.4 = (f32[1,144,128]{2,1,0:T(8,128)S(1)}, f32[1,144,128]{2,1,0:T(8,128)S(1)}, u32[]{:S(2)}, u32[]{:S(2)}) collective-permute-start(f32[1,144,128]{2,1,0:T(8,128)S(1)} %bitcast.11), channel_id=1, source_target_pairs={{0,4},{1,5},{2,6},{3,7},{4,0},{5,1},{6,2},{7,3},{8,12},{9,13},{10,... | collective-permute-start | bytes 221192 | tf_op jit(solution)/shard_map/ppermute | solution.py:59
  52.3 2.3 %collective-permute-done.4 = f32[1,144,128]{2,1,0:T(8,128)S(1)} collective-permute-done((f32[1,144,128]{2,1,0:T(8,128)S(1)}, f32[1,144,128]{2,1,0:T(8,128)S(1)}, u32[]{:S(2)}, u32[]{:S(2)}) %collective-permute-start.4) | collective-permute-done | bytes 73760 | tf_op jit(solution)/shard_map/ppermute | solution.py:59
  54.7 2.1 %collective-permute-start.5 = (f32[2,144,128]{2,1,0:T(8,128)S(1)}, f32[2,144,128]{2,1,0:T(8,128)S(1)}, u32[]{:S(2)}, u32[]{:S(2)}) collective-permute-start(f32[2,144,128]{2,1,0:T(8,128)S(1)} %pad_maximum_fusion.3), channel_id=1, source_target_pairs={{0,2},{1,3},{2,0},{3,1},{4,6},{5,7},{6,4},{7,5},{8,10},{9,11},{10,... | collective-permute-start | bytes 442376 | tf_op jit(solution)/shard_map/ppermute | solution.py:59
  56.7 3.1 %collective-permute-done.5 = f32[2,144,128]{2,1,0:T(8,128)S(1)} collective-permute-done((f32[2,144,128]{2,1,0:T(8,128)S(1)}, f32[2,144,128]{2,1,0:T(8,128)S(1)}, u32[]{:S(2)}, u32[]{:S(2)}) %collective-permute-start.5) | collective-permute-done | bytes 147488 | tf_op jit(solution)/shard_map/ppermute | solution.py:59
  59.9 2.1 %collective-permute-start.6 = (f32[4,144,128]{2,1,0:T(8,128)S(1)}, f32[4,144,128]{2,1,0:T(8,128)S(1)}, u32[]{:S(2)}, u32[]{:S(2)}) collective-permute-start(f32[4,144,128]{2,1,0:T(8,128)S(1)} %pad_maximum_fusion.low_ref.refs_4_.refs_0_), channel_id=1, source_target_pairs={{0,1},{1,0},{2,3},{3,2},{4,5},{5,4},{6,7},{7,6},{8,9},{9,8},{10,11... | collective-permute-start | bytes 884744 | tf_op jit(solution)/shard_map/ppermute | solution.py:59
  62.0 6.9 %collective-permute-done.6.high_ref.refs_5_.refs_1_ = f32[4,144,128]{2,1,0:T(8,128)S(1)} collective-permute-done((f32[4,144,128]{2,1,0:T(8,128)S(1)}, f32[4,144,128]{2,1,0:T(8,128)S(1)}, u32[]{:S(2)}, u32[]{:S(2)}) %collective-permute-start.6) | collective-permute-done | bytes 294944 | tf_op jit(solution)/shard_map/ppermute | solution.py:59
  69.5 1.8 %collective-permute-start.7 = (f32[1,40,256]{2,1,0:T(8,128)S(1)}, f32[1,40,256]{2,1,0:T(8,128)S(1)}, u32[]{:S(2)}, u32[]{:S(2)}) collective-permute-start(f32[1,40,256]{2,1,0:T(8,128)S(1)} %bitcast.14), channel_id=1, source_target_pairs={{0,16},{8,24},{16,0},{24,8},{1,17},{9,25},{17,1},{25,9},{2,18},{10... | collective-permute-start | bytes 122888 | tf_op jit(solution)/shard_map/ppermute | solution.py:59
  75.1 3.5 %shard_map.98 = (f32[40,256]{1,0:T(8,128)S(1)}, bf16[1280,128]{1,0:T(8,128)(2,1)S(1)}, bf16[32,256]{1,0:T(8,128)(2,1)S(1)}) custom-call(s32[2]{0:T(128)S(1)} %pad_add_fusion.me_ref.refs_0_, f32[2,40,256]{2,1,0:T(8,128)S(1)} %pad_maximum_fusion.4.refs_1_, f32[2,40,256]{2,1,0:T(8,128)S(1)} %collective-permute-done.8.refs_2_, ...), custom_call_target="tpu_custom_call" | custom-call | tf_op jit(solution)/shard_map/pallas_call | solution.py:917
  78.6 1.5 %collective-permute-start.9 = (f32[1,40,256]{2,1,0:T(8,128)S(1)}, f32[1,40,256]{2,1,0:T(8,128)S(1)}, u32[]{:S(2)}, u32[]{:S(2)}) collective-permute-start(f32[1,40,256]{2,1,0:T(8,128)S(1)} %bitcast.18), channel_id=1, source_target_pairs={{0,16},{8,24},{16,0},{24,8},{1,17},{9,25},{17,1},{25,9},{2,18},{10... | collective-permute-start | bytes 122888 | tf_op jit(solution)/shard_map/ppermute | solution.py:59
  83.9 3.5 %shard_map.102 = (f32[40,256]{1,0:T(8,128)S(1)}, bf16[1280,128]{1,0:T(8,128)(2,1)S(1)}, bf16[32,256]{1,0:T(8,128)(2,1)S(1)}) custom-call(s32[2]{0:T(128)S(1)} %pad_add_fusion.me_ref.refs_0_, f32[2,40,256]{2,1,0:T(8,128)S(1)} %pad_maximum_fusion.5.refs_1_, f32[2,40,256]{2,1,0:T(8,128)S(1)} %collective-permute-done.10.refs_2_, ...), custom_call_target="tpu_custom_call" | custom-call | tf_op jit(solution)/shard_map/pallas_call | solution.py:917
  87.4 1.5 %collective-permute-start.11 = (f32[1,40,256]{2,1,0:T(8,128)S(1)}, f32[1,40,256]{2,1,0:T(8,128)S(1)}, u32[]{:S(2)}, u32[]{:S(2)}) collective-permute-start(f32[1,40,256]{2,1,0:T(8,128)S(1)} %bitcast.20), channel_id=1, source_target_pairs={{0,16},{8,24},{16,0},{24,8},{1,17},{9,25},{17,1},{25,9},{2,18},{10... | collective-permute-start | bytes 122888 | tf_op jit(solution)/shard_map/ppermute | solution.py:59
  88.9 2.6 %shard_map.103.refs_2_ = f32[32,32,128]{2,1,0:T(8,128)S(1)} custom-call(s32[2]{0:T(128)S(1)} %pad_add_fusion.me_ref.refs_0_, f32[8,144,128]{2,1,0:T(8,128)S(1)} %all-to-all-done.record_ref, bf16[1280,128]{1,0:T(8,128)(2,1)S(1)} %get-tuple-element.71.refs_0_.spread_ref, bf16[32,256]{1,0:T(8,128)(2,1)S(1)} %get-tuple-element.72.refs_1_.solved_ref, ...), custom_call_target="tpu_custom_call" | custom-call | tf_op jit(solution)/shard_map/pallas_call | solution.py:901
  92.9 3.5 %shard_map.105 = (f32[40,256]{1,0:T(8,128)S(1)}, bf16[1280,128]{1,0:T(8,128)(2,1)S(1)}, bf16[32,256]{1,0:T(8,128)(2,1)S(1)}) custom-call(s32[2]{0:T(128)S(1)} %pad_add_fusion.me_ref.refs_0_, f32[2,40,256]{2,1,0:T(8,128)S(1)} %pad_maximum_fusion.6.refs_1_, f32[2,40,256]{2,1,0:T(8,128)S(1)} %collective-permute-done.12.refs_2_, ...), custom_call_target="tpu_custom_call" | custom-call | tf_op jit(solution)/shard_map/pallas_call | solution.py:917
  96.4 1.5 %collective-permute-start.13 = (f32[1,40,256]{2,1,0:T(8,128)S(1)}, f32[1,40,256]{2,1,0:T(8,128)S(1)}, u32[]{:S(2)}, u32[]{:S(2)}) collective-permute-start(f32[1,40,256]{2,1,0:T(8,128)S(1)} %bitcast.16), channel_id=1, source_target_pairs={{0,16},{8,24},{16,0},{24,8},{1,17},{9,25},{17,1},{25,9},{2,18},{10... | collective-permute-start | bytes 122888 | tf_op jit(solution)/shard_map/ppermute | solution.py:59
  98.0 2.6 %shard_map.106.trans_ref = f32[32,32,128]{2,1,0:T(8,128)S(1)} custom-call(s32[2]{0:T(128)S(1)} %pad_add_fusion.me_ref.refs_0_, f32[8,144,128]{2,1,0:T(8,128)S(1)} %all-to-all-done.record_ref, bf16[1280,128]{1,0:T(8,128)(2,1)S(1)} %get-tuple-element.81.refs_0_, bf16[32,256]{1,0:T(8,128)(2,1)S(1)} %get-tuple-element.82.refs_1_, ...), custom_call_target="tpu_custom_call" | custom-call | tf_op jit(solution)/shard_map/pallas_call | solution.py:901
  102.0 7.9 %shard_map.107 = f32[32,128,128]{2,1,0:T(8,128)} custom-call(s32[2]{0:T(128)S(1)} %pad_add_fusion.me_ref.refs_0_, f32[2,40,256]{2,1,0:T(8,128)S(1)} %pad_maximum_fusion.7.lows_ref, f32[2,40,256]{2,1,0:T(8,128)S(1)} %collective-permute-done.14.highs_ref, f32[8,144,128]{2,1,0:T(8,128)S(1)} %all-to-all-done.record_ref, ...), custom_call_target="tpu_custom_call" | custom-call | tf_op jit(solution)/shard_map/pallas_call | solution.py:949
  (43 shorter events, 16.4 us)
Async XLA Ops:
  0.0 18.5 %copy-start = (f32[32,128,128]{2,1,0:T(8,128)S(1)}, f32[32,128,128]{2,1,0:T(8,128)}, u32[]{:S(2)}) copy-start(f32[32,128,128]{2,1,0:T(8,128)} %h_ref.1) | copy-start | bytes 6291460
  3.5 15.1 %copy-start.1 = (f32[2,128,128]{2,1,0:T(8,128)S(1)}, f32[2,128,128]{2,1,0:T(8,128)}, u32[]{:S(2)}) copy-start(f32[2,128,128]{2,1,0:T(8,128)} %get-tuple-element.47.coef_ref) | copy-start | bytes 393220
  3.5 15.1 %collective-permute-start = (f32[3,128,128]{2,1,0:T(8,128)}, f32[3,128,128]{2,1,0:T(8,128)S(1)}, u32[]{:S(2)}, u32[]{:S(2)}) collective-permute-start(f32[3,128,128]{2,1,0:T(8,128)} %get-tuple-element.48), channel_id=1, source_target_pairs={{0,1},{1,2},{2,3},{3,4},{4,5},{5,6},{6,7},{8,9},{9,10},{10,11},{11... | collective-permute-start | bytes 589832 | tf_op jit(solution)/shard_map/ppermute | solution.py:70
  8.5 10.1 %collective-permute-start.1 = (f32[3,128,128]{2,1,0:T(8,128)}, f32[3,128,128]{2,1,0:T(8,128)S(1)}, u32[]{:S(2)}, u32[]{:S(2)}) collective-permute-start(f32[3,128,128]{2,1,0:T(8,128)} %get-tuple-element.49), channel_id=1, source_target_pairs={{1,0},{2,1},{3,2},{4,3},{5,4},{6,5},{7,6},{9,8},{10,9},{11,10},{12... | collective-permute-start | bytes 589832 | tf_op jit(solution)/shard_map/ppermute | solution.py:70
  11.6 33.3 %all-to-all-start = ((f32[8,144,128]{2,1,0:T(8,128)}), f32[8,144,128]{2,1,0:T(8,128)S(1)}, u32[]{:S(2)}, u32[]{:S(2)}) async-start(f32[8,144,128]{2,1,0:T(8,128)} %broadcast_in_dim.18), calls=%async_computation | async-start | bytes 1179648 | tf_op jit(solution)/shard_map/all_to_all | solution.py:856
  19.3 4.7 %collective-permute-start.2 = (f32[40,8,128]{2,1,0:T(8,128)}, f32[40,8,128]{2,1,0:T(8,128)S(1)}, u32[]{:S(2)}, u32[]{:S(2)}) collective-permute-start(f32[40,8,128]{2,1,0:T(8,128)} %pad_maximum_fusion.1), channel_id=1, source_target_pairs={{0,8},{8,16},{16,24},{1,9},{9,17},{17,25},{2,10},{10,18},{18,26},{... | collective-permute-start | bytes 491528 | tf_op jit(solution)/shard_map/ppermute | solution.py:70
  21.3 5.2 %collective-permute-start.3 = (f32[40,8,128]{2,1,0:T(8,128)}, f32[40,8,128]{2,1,0:T(8,128)S(1)}, u32[]{:S(2)}, u32[]{:S(2)}) collective-permute-start(f32[40,8,128]{2,1,0:T(8,128)} %pad_maximum_fusion.2), channel_id=1, source_target_pairs={{8,0},{16,8},{24,16},{9,1},{17,9},{25,17},{10,2},{18,10},{26,18},{... | collective-permute-start | bytes 491528 | tf_op jit(solution)/shard_map/ppermute | solution.py:70
  49.3 5.3 %collective-permute-start.4 = (f32[1,144,128]{2,1,0:T(8,128)S(1)}, f32[1,144,128]{2,1,0:T(8,128)S(1)}, u32[]{:S(2)}, u32[]{:S(2)}) collective-permute-start(f32[1,144,128]{2,1,0:T(8,128)S(1)} %bitcast.11), channel_id=1, source_target_pairs={{0,4},{1,5},{2,6},{3,7},{4,0},{5,1},{6,2},{7,3},{8,12},{9,13},{10,... | collective-permute-start | bytes 221192 | tf_op jit(solution)/shard_map/ppermute | solution.py:59
  54.7 5.2 %collective-permute-start.5 = (f32[2,144,128]{2,1,0:T(8,128)S(1)}, f32[2,144,128]{2,1,0:T(8,128)S(1)}, u32[]{:S(2)}, u32[]{:S(2)}) collective-permute-start(f32[2,144,128]{2,1,0:T(8,128)S(1)} %pad_maximum_fusion.3), channel_id=1, source_target_pairs={{0,2},{1,3},{2,0},{3,1},{4,6},{5,7},{6,4},{7,5},{8,10},{9,11},{10,... | collective-permute-start | bytes 442376 | tf_op jit(solution)/shard_map/ppermute | solution.py:59
  59.9 8.9 %collective-permute-start.6 = (f32[4,144,128]{2,1,0:T(8,128)S(1)}, f32[4,144,128]{2,1,0:T(8,128)S(1)}, u32[]{:S(2)}, u32[]{:S(2)}) collective-permute-start(f32[4,144,128]{2,1,0:T(8,128)S(1)} %pad_maximum_fusion.low_ref.refs_4_.refs_0_), channel_id=1, source_target_pairs={{0,1},{1,0},{2,3},{3,2},{4,5},{5,4},{6,7},{7,6},{8,9},{9,8},{10,11... | collective-permute-start | bytes 884744 | tf_op jit(solution)/shard_map/ppermute | solution.py:59
  69.5 4.4 %collective-permute-start.7 = (f32[1,40,256]{2,1,0:T(8,128)S(1)}, f32[1,40,256]{2,1,0:T(8,128)S(1)}, u32[]{:S(2)}, u32[]{:S(2)}) collective-permute-start(f32[1,40,256]{2,1,0:T(8,128)S(1)} %bitcast.14), channel_id=1, source_target_pairs={{0,16},{8,24},{16,0},{24,8},{1,17},{9,25},{17,1},{25,9},{2,18},{10... | collective-permute-start | bytes 122888 | tf_op jit(solution)/shard_map/ppermute | solution.py:59
  73.8 1.3 %collective-permute-start.8 = (f32[2,40,256]{2,1,0:T(8,128)S(1)}, f32[2,40,256]{2,1,0:T(8,128)S(1)}, u32[]{:S(2)}, u32[]{:S(2)}) collective-permute-start(f32[2,40,256]{2,1,0:T(8,128)S(1)} %pad_maximum_fusion.4.refs_1_), channel_id=1, source_target_pairs={{0,8},{8,0},{16,24},{24,16},{1,9},{9,1},{17,25},{25,17},{2,10},{10... | collective-permute-start | bytes 245768 | tf_op jit(solution)/shard_map/ppermute | solution.py:59
  78.6 4.0 %collective-permute-start.9 = (f32[1,40,256]{2,1,0:T(8,128)S(1)}, f32[1,40,256]{2,1,0:T(8,128)S(1)}, u32[]{:S(2)}, u32[]{:S(2)}) collective-permute-start(f32[1,40,256]{2,1,0:T(8,128)S(1)} %bitcast.18), channel_id=1, source_target_pairs={{0,16},{8,24},{16,0},{24,8},{1,17},{9,25},{17,1},{25,9},{2,18},{10... | collective-permute-start | bytes 122888 | tf_op jit(solution)/shard_map/ppermute | solution.py:59
  82.6 1.3 %collective-permute-start.10 = (f32[2,40,256]{2,1,0:T(8,128)S(1)}, f32[2,40,256]{2,1,0:T(8,128)S(1)}, u32[]{:S(2)}, u32[]{:S(2)}) collective-permute-start(f32[2,40,256]{2,1,0:T(8,128)S(1)} %pad_maximum_fusion.5.refs_1_), channel_id=1, source_target_pairs={{0,8},{8,0},{16,24},{24,16},{1,9},{9,1},{17,25},{25,17},{2,10},{10... | collective-permute-start | bytes 245768 | tf_op jit(solution)/shard_map/ppermute | solution.py:59
  87.4 4.1 %collective-permute-start.11 = (f32[1,40,256]{2,1,0:T(8,128)S(1)}, f32[1,40,256]{2,1,0:T(8,128)S(1)}, u32[]{:S(2)}, u32[]{:S(2)}) collective-permute-start(f32[1,40,256]{2,1,0:T(8,128)S(1)} %bitcast.20), channel_id=1, source_target_pairs={{0,16},{8,24},{16,0},{24,8},{1,17},{9,25},{17,1},{25,9},{2,18},{10... | collective-permute-start | bytes 122888 | tf_op jit(solution)/shard_map/ppermute | solution.py:59
  91.6 1.3 %collective-permute-start.12 = (f32[2,40,256]{2,1,0:T(8,128)S(1)}, f32[2,40,256]{2,1,0:T(8,128)S(1)}, u32[]{:S(2)}, u32[]{:S(2)}) collective-permute-start(f32[2,40,256]{2,1,0:T(8,128)S(1)} %pad_maximum_fusion.6.refs_1_), channel_id=1, source_target_pairs={{0,8},{8,0},{16,24},{24,16},{1,9},{9,1},{17,25},{25,17},{2,10},{10... | collective-permute-start | bytes 245768 | tf_op jit(solution)/shard_map/ppermute | solution.py:59
  96.4 4.2 %collective-permute-start.13 = (f32[1,40,256]{2,1,0:T(8,128)S(1)}, f32[1,40,256]{2,1,0:T(8,128)S(1)}, u32[]{:S(2)}, u32[]{:S(2)}) collective-permute-start(f32[1,40,256]{2,1,0:T(8,128)S(1)} %bitcast.16), channel_id=1, source_target_pairs={{0,16},{8,24},{16,0},{24,8},{1,17},{9,25},{17,1},{25,9},{2,18},{10... | collective-permute-start | bytes 122888 | tf_op jit(solution)/shard_map/ppermute | solution.py:59
  100.7 1.3 %collective-permute-start.14 = (f32[2,40,256]{2,1,0:T(8,128)S(1)}, f32[2,40,256]{2,1,0:T(8,128)S(1)}, u32[]{:S(2)}, u32[]{:S(2)}) collective-permute-start(f32[2,40,256]{2,1,0:T(8,128)S(1)} %pad_maximum_fusion.7.lows_ref), channel_id=1, source_target_pairs={{0,8},{8,0},{16,24},{24,16},{1,9},{9,1},{17,25},{25,17},{2,10},{10... | collective-permute-start | bytes 245768 | tf_op jit(solution)/shard_map/ppermute | solution.py:59
